TPU v7x, 256 devices: a whole 4x4x8 slice. The times are simulated.
256 devices in a mesh: label: 128 (over x, y_lo, z, core), dp: 2 (over y_hi).
Axes of the slice: x: 4, y: 4 (y_hi: 2, y_lo: 2; y = y_hi * 2 + y_lo), z: 8, core: 2. Of those that a mesh axis runs over, the one named last changes fastest.
Arguments:
- queries: bfloat16 [4096, 512], P(('label', 'dp')), may hold values from -9 to 9
- positives: int32 [4096, 8], P(('label', 'dp')), may hold values from -1 to 131071, as said below
- weights: float32 [131072, 512], P('label'), may hold values from -4 to 4
- first_moment: float32 [131072, 512], P('label'), may hold values from -1.8 to 1.8
- second_moment: float32 [131072, 512], P('label'), may hold values from 0.05 to 1
Outputs:
- new_weights: float32 [131072, 512], P('label')
- new_first: float32 [131072, 512], P('label')
- new_second: float32 [131072, 512], P('label')
- query_grads: float32 [2, 4096, 512], P(None, ('label', 'dp'))
Inputs may be any that keep to these rules, and one draw needn't show every extreme that they name: `positives`: each row lists its query's positive label ids (one to 8) first and -1 in the unused slots after them; ids may repeat within a row.
All inputs are finite; a program needn't handle non-finite values.
Results may differ from a plain program's by a relative error of at most 0.0023.
Values may be sent and summed in bfloat16 or wider, within the bound.
No kernel may reach another device: no remote copies, remote signals or barrier semaphores. Data moves between devices by JAX's collectives and lax.ppermute only.
A program may use at most 128 MiB of HBM per device.

v0:
```python
import jax
import jax.numpy as jnp
from jax import lax
from jax.experimental import pallas as pl
from jax.experimental.pallas import tpu as pltpu
from jax.sharding import Mesh, PartitionSpec as P

STEPS = 2

beta_one = 0.9
beta_two = 0.95
rate = 0.02
decay = 0.1
epsilon = 1e-08
past_steps = 1000

f32 = jnp.float32
bf16 = jnp.bfloat16
i32 = jnp.int32

NX, NLO, NZ, NCORE, NHI = 4, 2, 8, 2, 2
NY = NLO * NHI
AXES = ("x", "ylo", "z", "core", "yhi")
D = 512
ROWS = 16
SLOTS = 8
LINE = NZ * ROWS
NQ = NX * NY * LINE
BLOCK = 2 * LINE
LAB = 1024
TILE = 256
VMEM = 16 * 2**20
LOG2E = 1.4426950408889634


def spec(shape=None, index=None, space=pltpu.VMEM):
    if shape is None:
        return pl.BlockSpec(memory_space=space)
    return pl.BlockSpec(shape, index, memory_space=space)


def params():
    return pltpu.CompilerParams(vmem_limit_bytes=VMEM)


def cost(flops=0, size=0, exps=0):
    return pl.CostEstimate(flops=flops, bytes_accessed=size, transcendentals=exps)


def descending(rows):
    rows = list(rows)
    for a, b in (
        (0, 1), (2, 3), (4, 5), (6, 7), (0, 2), (1, 3), (4, 6), (5, 7), (1, 2), (5, 6),
        (0, 4), (1, 5), (2, 6), (3, 7), (2, 4), (3, 5), (1, 2), (3, 4), (5, 6),
    ):
        rows[a], rows[b] = jnp.maximum(rows[a], rows[b]), jnp.minimum(rows[a], rows[b])
    return rows


def here_is():
    high, core = lax.axis_index("yhi"), lax.axis_index("core")
    chip = (lax.axis_index("x") * NLO + lax.axis_index("ylo")) * NZ + lax.axis_index("z")
    base = chip * NCORE * LAB
    return high, core, base + core * LAB, base + (1 - core) * LAB


def gray(slot):
    return slot ^ (slot >> 1)


def place_of(late, early):
    high, core = here_is()[:2]
    y = late + core * (early - late)
    x = early + core * (late - early)
    return (y ^ (2 * high)) * NX + ((x + core * (4 - 2 * x)) & 3)


def span(late, early):
    return pl.ds(pl.multiple_of(place_of(late, early) * LINE, LINE), LINE)


FAST = 2


def contract_last(left, right):
    return lax.dot_general(left, right, (((1,), (1,)), ((), ())), preferred_element_type=f32)


def contract_first(left, right):
    return lax.dot_general(left, right, (((0,), (0,)), ((), ())), preferred_element_type=f32)


def fill_tile(logits, hits, first):
    share = pl.reciprocal(1.0 + jnp.exp2(logits * -LOG2E), approx=True)
    label = lax.broadcasted_iota(i32, logits.shape, 0) + first
    hit = hits[0] == label
    for row in hits[1:]:
        hit = hit | (row == label)
    return jnp.where(hit, share - 1.0, share).astype(bf16)


def more_hits(count, pos_ref, half, out_ref, at):
    @pl.loop(FAST, count)
    def _(j):
        slots = pos_ref[half, :, at]
        slots = jnp.where(lax.broadcasted_iota(i32, slots.shape, 0) == j, slots, -1)
        hit = jnp.max(slots, axis=0, keepdims=True)

        @pl.loop(0, LAB // TILE)
        def _(t):
            rows = pl.ds(pl.multiple_of(t * TILE, TILE), TILE)
            old = out_ref[rows, at].astype(f32)
            label = lax.broadcasted_iota(i32, old.shape, 0) + t * TILE
            out_ref[rows, at] = jnp.where(hit == label, old - 1.0, old).astype(bf16)


def fill_grad(resid_ref, q_ref, out_ref):
    @pl.loop(0, LAB // (2 * TILE))
    def _(t):
        rows = pl.ds(pl.multiple_of(2 * TILE * t, 2 * TILE), 2 * TILE)
        out_ref[rows, :] = jnp.dot(resid_ref[rows, :], q_ref[...], preferred_element_type=f32)


def part_kernel(part_ref, wb_own, wb_other, *refs, late):
    first_labels = here_is()[2:]
    grads = refs[-1:] if late == LAST else ()
    before = refs[4] if late else None
    q_ref, pos_ref, own_ref, other_ref, most_ref = refs[-5 - len(grads) : len(refs) - len(grads)]
    spans = [span(late, gray(early)) for early in range(4)]
    coded = part_ref[NX * LINE :, : 3 * LINE].astype(f32)
    ids = coded[:, :LINE] + 256.0 * coded[:, LINE : 2 * LINE] + 65536.0 * coded[:, 2 * LINE :]
    ids = ids.astype(i32)
    rows = []
    for j in range(SLOTS):
        row = jnp.concatenate([ids[SLOTS * early + j : SLOTS * early + j + 1] for early in range(4)], axis=0)
        local = jnp.concatenate([row - first for first in first_labels], axis=0)
        rows.append(jnp.where((local >= 0) & (local < LAB), local, -1))
    rows = descending(rows)
    count = sum((row >= 0).astype(f32) for row in rows)
    most = jnp.max(count).astype(i32)
    most_ref[...] = count if before is None else jnp.maximum(count, before[...])
    rows = rows[:1] + [jnp.where(row == last, -1, row) for last, row in zip(rows, rows[1:])]
    for half in range(2):
        for early, at in enumerate(spans):
            k = 4 * half + early
            for j in range(SLOTS):
                pos_ref[half, j : j + 1, at] = rows[j][k : k + 1]

    @pl.loop(0, 2)
    def _(pair):
        q = part_ref[pl.ds(pl.multiple_of(pair * BLOCK, BLOCK), BLOCK), :]
        ends = [span(late, 3 * pair), span(late, 1 + pair)]
        for half, wb_ref, out_ref in ((1, wb_other, other_ref), (0, wb_own, own_ref)):
            hits = [[pos_ref[half, j : j + 1, at] for j in range(FAST)] for at in ends]
            for t in range(LAB // TILE):
                tile = slice(t * TILE, (t + 1) * TILE)
                logits = contract_last(wb_ref[tile, :], q)
                for k, at in enumerate(ends):
                    out_ref[tile, at] = fill_tile(logits[:, k * LINE : (k + 1) * LINE], hits[k], t * TILE)

    for early, at in enumerate(spans):
        q_ref[at, :] = part_ref[early * LINE : (early + 1) * LINE, :]

    @pl.when(most > FAST)
    def _():
        @pl.loop(0, 4)
        def _(early):
            for half, out_ref in enumerate((own_ref, other_ref)):
                more_hits(most, pos_ref, half, out_ref, span(late, early))

    for out_ref in grads:
        fill_grad(other_ref, q_ref, out_ref)


LAST = 2


def first_residuals(part, wb, wb_other, late, into):
    shapes = (
        jax.ShapeDtypeStruct((NQ, D), bf16),
        jax.ShapeDtypeStruct((2, SLOTS, NQ), i32),
        jax.ShapeDtypeStruct((LAB, NQ), bf16),
        jax.ShapeDtypeStruct((LAB, NQ), bf16),
        jax.ShapeDtypeStruct((2 * NX, LINE), f32),
    )
    if late == LAST:
        shapes += (jax.ShapeDtypeStruct((LAB, D), f32),)
    size = LAB * NX * LINE
    return pl.pallas_call(
        lambda *refs: part_kernel(*refs, late=late),
        out_shape=shapes,
        in_specs=[spec()] * (3 + len(into)),
        out_specs=(spec(),) * len(shapes),
        input_output_aliases={3 + i: i for i in range(len(into))},
        compiler_params=params(),
        cost_estimate=cost((8 if late == LAST else 4) * size * D, 4 * size, 4 * size),
        name="part",
    )(part, wb, wb_other, *into)


def code_kernel(q_ref, pos_ref, out_ref):
    ids = pos_ref[...]
    out_ref[:, :D] = q_ref[...]
    digits = [ids & 255, (ids >> 8) & 255, ids >> 16]
    lane = lax.broadcasted_iota(i32, (SLOTS, LINE), 1) - lax.broadcasted_iota(i32, (SLOTS, LINE), 0)
    coded = jnp.zeros((ROWS, LINE), f32)
    for i, digit in enumerate(digits):
        put = (lane == i * SLOTS).astype(f32).astype(bf16)
        coded = coded + contract_first(digit.astype(f32).astype(bf16), put)
    out_ref[:, D:] = coded.astype(bf16)


def code(queries, positives):
    return pl.pallas_call(
        code_kernel,
        out_shape=jax.ShapeDtypeStruct((ROWS, D + LINE), bf16),
        in_specs=[spec()] * 2,
        out_specs=spec(),
        compiler_params=params(),
        cost_estimate=cost(size=4 * ROWS * D),
        name="code",
    )(queries, positives.T)


def pack_kernel(*refs):
    out_ref = refs[-1]
    for i, ref in enumerate(refs[:-1]):
        out_ref[i * LINE : (i + 1) * LINE, :] = ref[:LINE, :]
    tails = [ref[LINE:, :] for ref in refs[:-1]]
    out_ref[NX * LINE :, :] = jnp.concatenate(tails, axis=0)


def pack(parts):
    return pl.pallas_call(
        pack_kernel,
        out_shape=jax.ShapeDtypeStruct((NX * (LINE + SLOTS), D), bf16),
        in_specs=[spec()] * 4,
        out_specs=spec(),
        compiler_params=params(),
        cost_estimate=cost(size=4 * NX * LINE * D),
        name="pack",
    )(*parts)


def beside():
    high, core = here_is()[:2]
    plane = (1 + 2 * core) ^ (2 * high)
    return [2 * plane, 2 * plane + 1]


def here():
    first = 4 * lax.axis_index("yhi")
    return [first, first + 1]


def remaining():
    return [block ^ 4 for block in beside() + here()]


def chosen(blocks, i):
    block = blocks[0]
    for k in range(1, len(blocks)):
        block = jnp.where(i == k, blocks[k], block)
    return pl.ds(pl.multiple_of(block * BLOCK, BLOCK), BLOCK)


def fill_block(q_ref, pos_ref, wb_ref, out_ref, half, at):
    q = q_ref[at, :]
    hits = [pos_ref[half, j : j + 1, at] for j in range(FAST)]
    for t in range(LAB // TILE):
        rows = slice(t * TILE, (t + 1) * TILE)
        out_ref[rows, at] = fill_tile(contract_last(wb_ref[rows, :], q), hits, t * TILE)


def finish(most, pos_ref, parts, blocks):
    count = jnp.max(most[...]).astype(i32)

    @pl.when(count > FAST)
    def _():
        @pl.loop(0, len(blocks))
        def _(i):
            for half, out_ref in parts:
                more_hits(count, pos_ref, half, out_ref, chosen(blocks, i))


def fill_terms(own_ref, other_ref, wb_own, wb_other, out_ref, blocks):
    @pl.loop(0, len(blocks))
    def _(i):
        at = chosen(blocks, i)
        first = contract_first(own_ref[:, at], wb_own[...])
        second = contract_first(other_ref[:, at], wb_other[...])
        rows = pl.ds(pl.multiple_of(i * BLOCK, BLOCK), BLOCK)
        out_ref[rows, :] = (first + second).astype(out_ref.dtype)


def plane_kernel(most, q_ref, pos_ref, wb_own, wb_other, *refs, blocks):
    own_ref, other_ref, out_ref = refs[-3:]
    blocks = blocks()

    @pl.loop(0, len(blocks))
    def _(i):
        at = chosen(blocks, i)
        fill_block(q_ref, pos_ref, wb_own, own_ref, 0, at)
        fill_block(q_ref, pos_ref, wb_other, other_ref, 1, at)

    finish(most, pos_ref, ((0, own_ref), (1, other_ref)), blocks)
    fill_terms(own_ref, other_ref, wb_own, wb_other, out_ref, blocks)


def plane_terms(most, q, pos, wb, wb_other, blocks, kind, into=()):
    size = 2 * LAB * 2 * BLOCK
    resid = jax.ShapeDtypeStruct((LAB, NQ), bf16)
    return pl.pallas_call(
        lambda *refs: plane_kernel(*refs, blocks=blocks),
        out_shape=(resid, resid, jax.ShapeDtypeStruct((2 * BLOCK, D), kind)),
        in_specs=[spec()] * (5 + len(into)),
        out_specs=(spec(),) * 3,
        input_output_aliases={5 + i: i for i in range(len(into))},
        compiler_params=params(),
        cost_estimate=cost(4 * size * D, 4 * size, 2 * size),
        name="plane",
    )(most, q, pos, wb, wb_other, *into)


def terms_kernel(own_ref, other_ref, wb_own, wb_other, out_ref, *, blocks):
    fill_terms(own_ref, other_ref, wb_own, wb_other, out_ref, blocks())


def terms(own, other, wb_own, wb_other, blocks, kind):
    return pl.pallas_call(
        lambda *refs: terms_kernel(*refs, blocks=blocks),
        out_shape=jax.ShapeDtypeStruct((2 * BLOCK, D), kind),
        in_specs=[spec()] * 4,
        out_specs=spec(),
        compiler_params=params(),
        cost_estimate=cost(8 * LAB * BLOCK * D, 4 * 2**20),
        name="terms",
    )(own, other, wb_own, wb_other)


def rest_kernel(most, q_ref, pos_ref, wb_ref, resid_ref, out_ref, *, half):
    blocks = remaining()

    @pl.loop(0, len(blocks) // 2)
    def _(i):
        for k in range(2):
            fill_block(q_ref, pos_ref, wb_ref, resid_ref, half, chosen(blocks, 2 * i + k))

    finish(most, pos_ref, ((half, resid_ref),), blocks)
    fill_grad(resid_ref, q_ref, out_ref)


def rest_gradient(most, q, pos, wb, resid, half):
    size = LAB * 4 * BLOCK
    return pl.pallas_call(
        lambda most, q, pos, wb, old, resid, out: rest_kernel(most, q, pos, wb, resid, out, half=half),
        out_shape=(jax.ShapeDtypeStruct((LAB, NQ), bf16), jax.ShapeDtypeStruct((LAB, D), f32)),
        in_specs=[spec()] * 5,
        out_specs=(spec(),) * 2,
        input_output_aliases={4: 0},
        compiler_params=params(),
        cost_estimate=cost(6 * size * D, 8 * size, 2 * size),
        name="rest",
    )(most, q, pos, wb, resid)[1]


def grad_kernel(resid_ref, q_ref, out_ref):
    fill_grad(resid_ref, q_ref, out_ref)


def gradient(resid, q):
    return pl.pallas_call(
        grad_kernel,
        out_shape=jax.ShapeDtypeStruct((LAB, D), f32),
        in_specs=[spec()] * 2,
        out_specs=spec(),
        compiler_params=params(),
        cost_estimate=cost(2 * LAB * NQ * D, 8 * 2**20),
        name="grad",
    )(resid, q)


def adamw(count, grad, weight, first, second):
    first = beta_one * first + (1.0 - beta_one) * grad
    second = beta_two * second + (1.0 - beta_two) * grad * grad
    first_hat = first * (1.0 / (1.0 - beta_one**count))
    second_hat = second * (1.0 / (1.0 - beta_two**count))
    weight = weight - rate * (first_hat / (jnp.sqrt(second_hat) + epsilon) + decay * weight)
    return weight, first, second


def adamw_kernel(count, one, two, w_ref, m_ref, v_ref, w_out, m_out, v_out, *wb_out):
    @pl.loop(0, one.shape[0] // 64)
    def _(t):
        rows = pl.ds(pl.multiple_of(t * 64, 64), 64)
        grad = one[rows, :] + two[rows, :]
        weight, first, second = adamw(count, grad, w_ref[rows, :], m_ref[rows, :], v_ref[rows, :])
        w_out[rows, :] = weight
        m_out[rows, :] = first
        v_out[rows, :] = second
        if wb_out:
            wb_out[0][rows, :] = weight.astype(bf16)


def update(count, last, one, two, weight, first, second):
    full = jax.ShapeDtypeStruct((LAB, D), f32)
    tile = spec((TILE, D), lambda i: (i, 0)) if last else spec()
    return pl.pallas_call(
        lambda *refs: adamw_kernel(count, *refs),
        grid=(LAB // TILE,) if last else (),
        out_shape=(full, full, full) + (() if last else (jax.ShapeDtypeStruct((LAB, D), bf16),)),
        in_specs=[tile] * 5,
        out_specs=(tile,) * (3 if last else 4),
        compiler_params=params(),
        cost_estimate=cost(20 * LAB * D, 12 * LAB * D, 2 * LAB * D),
        name="adamw",
    )(one, two, weight, first, second)


def moved(move):
    pairs = []
    for x in range(NX):
        for y in range(NY):
            for z in range(NZ):
                for core in range(NCORE):
                    tx, ty, tz, tcore = move(x, y, z, core)
                    name = lambda x, y, z, core: (
                        (((x % NX) * NLO + y % NLO) * NZ + z % NZ) * NCORE + core
                    ) * NHI + (y % NY) // NLO
                    pairs.append((name(x, y, z, core), name(tx, ty, tz, tcore)))
    return pairs


def send(array, move):
    return lax.ppermute(array, AXES, moved(move))


def along_x(by):
    return lambda x, y, z, core: (x ^ by, y, z, core)


def along_y(by):
    return lambda x, y, z, core: (x, y ^ by, z, core)


def by_core(zero, one):
    return lambda x, y, z, core: one(x, y, z, core) if core else zero(x, y, z, core)


def onward(by):
    def move(x, y, z, core):
        place = 2 * z + core + (by if core else -by)
        return x, y, place // 2, place % 2

    return move


def back(by):
    moves = {onward(by)(0, 0, z, core)[2] % NZ * 2 + onward(by)(0, 0, z, core)[3]: (z, core) for z in range(NZ) for core in range(2)}
    return lambda x, y, z, core: (x, y, *moves[2 * z + core])


def swap(array):
    return send(array, lambda x, y, z, core: (x, y, z, 1 - core))


def gather(queries, positives):
    line = code(queries, positives)
    line = jnp.concatenate([line] + [send(line, back(by)) for by in (1, 2, 3)], axis=0)
    line = jnp.concatenate([line, send(line, back(4))], axis=0)
    coded = line[:, D : D + 3 * SLOTS].T
    coded = jnp.concatenate([coded[i * SLOTS : (i + 1) * SLOTS] for i in range(3)], axis=1)
    coded = jnp.pad(coded, ((0, 0), (0, D - 3 * LINE)))
    chip = jnp.concatenate([line[:, :D], coded], axis=0)
    four = [chip] + [send(chip, by_core(along_x(by), along_y(by))) for by in (1, 3, 2)]
    four = pack(four)
    return [four] + [send(four, by_core(along_y(by), along_x(by))) for by in (1, 3, 2)]


def after(array, *others):
    return lax.optimization_barrier((array, *others))


def shards(queries, positives, weights, first_moment, second_moment):
    weight, first, second = weights, first_moment, second_moment
    to_plane = lambda part: send(part, by_core(along_y(1), along_y(3)))
    to_half = lambda plane: send(plane[1:3].astype(bf16), by_core(along_x(1), along_x(3)))
    to_line = lambda plane, got: send(plane[3] + got[1].astype(f32), by_core(along_x(3), along_x(1)))
    as_plane = lambda part, got: (part + got.astype(f32)).reshape(NX, LINE, D)

    wb = weight.astype(bf16)
    wb_other = swap(wb)
    state = ()
    for late, part in zip((0, 1, 3, LAST), gather(queries, positives)):
        *state, theirs = (*first_residuals(part, wb, wb_other, late, state[:5]), None)[:6]
    q, pos, own, other, most = state
    step0 = (own, other, wb, wb_other)

    part = swap(theirs)
    mine = gradient(own, q)
    out0 = terms(*step0, beside, bf16)
    part, mine, out0 = after(part, mine, out0)
    weight, first, second, wb = update(past_steps + 1, False, mine, part, weight, first, second)

    wb_other = swap(wb)
    wb, out0, *step0 = after(wb, out0, *step0)
    out0 = to_plane(out0)
    part0 = terms(*step0, here, f32)
    wb_other, part0 = after(wb_other, part0)
    own, other, out1 = plane_terms(most, q, pos, wb, wb_other, beside, bf16)

    out1, own, other = after(out1, own, other)
    out1 = to_plane(out1)
    own, other, part1 = plane_terms(most, q, pos, wb, wb_other, here, f32, (own, other))
    out0, part1 = after(out0, part1)
    plane0 = as_plane(part0, out0)
    half0 = to_half(plane0)
    plane1 = as_plane(part1, out1)

    half1 = to_half(plane1)
    plane1, plane0, other = after(plane1, plane0, other)
    theirs = rest_gradient(most, q, pos, wb_other, other, 1)
    half1, half0, theirs, own = after(half1, half0, theirs, own)

    part = swap(theirs)
    quarter1 = to_line(plane1, half1)
    quarter0 = to_line(plane0, half0)
    mine = rest_gradient(most, q, pos, wb, own, 0)
    quarter1, quarter0, mine = after(quarter1, quarter0, mine)
    line = [
        plane[0] + half[0].astype(f32) + quarter
        for plane, half, quarter in ((plane0, half0, quarter0), (plane1, half1, quarter1))
    ]
    line = jnp.stack([part.reshape(NZ, ROWS, D) for part in line], axis=1)
    got = send(line[4:].astype(bf16), onward(4))
    weight, first, second = update(past_steps + 2, True, mine, part, weight, first, second)
    got, weight, first, second = after(got, weight, first, second)
    line = line[:4] + got.astype(f32)
    got = [send(line[by], onward(by)) for by in (1, 2, 3)]
    return weight, first, second, line[0] + got[0] + got[1] + got[2]


def solution(mesh):
    devices = mesh.devices.reshape(NX, NLO, NZ, NCORE, NHI)
    label = AXES[:4]
    in_specs = (P(AXES, None), P(AXES, None), P(label, None), P(label, None), P(label, None))
    out_specs = (P(label, None), P(label, None), P(label, None), P(None, AXES, None))
    return jax.shard_map(
        shards, mesh=Mesh(devices, AXES), in_specs=in_specs, out_specs=out_specs, check_vma=False
    )
```

profile of v0, /device:TPU:1, one launch (start us, length us, event | category | flops | bytes accessed | tf_op | source)
XLA Modules:
  0.0 118.5 jit_solution(2076437383994163965)
XLA Ops:
  2.4 4.5 %collective-permute-start.2 = (bf16[16,640]{0,1:T(8,128)(2,1)S(1)}, bf16[16,640]{0,1:T(8,128)(2,1)S(1)}, u32[]{:S(2)}, u32[]{:S(2)}) collective-permute-start(bf16[16,640]{0,1:T(8,128)(2,1)S(1)} %copy.32), channel_id=1, source_target_pairs={{0,26},{2,8},{4,30},{6,12},{8,2},{10,16},{12,6},{14,20},{16,10},{1... | collective-permute-start | bytes 61448 | tf_op jit(solution)/shard_map/ppermute | solution.py:435
  6.9 2.1 %collective-permute-start.1 = (bf16[16,640]{0,1:T(8,128)(2,1)S(1)}, bf16[16,640]{0,1:T(8,128)(2,1)S(1)}, u32[]{:S(2)}, u32[]{:S(2)}) collective-permute-start(bf16[16,640]{0,1:T(8,128)(2,1)S(1)} %copy.32), channel_id=1, source_target_pairs={{0,4},{2,30},{4,8},{6,2},{8,12},{10,6},{12,16},{14,10},{16,20},{18... | collective-permute-start | bytes 61448 | tf_op jit(solution)/shard_map/ppermute | solution.py:435
  11.9 1.8 %collective-permute-done.1 = bf16[16,640]{0,1:T(8,128)(2,1)S(1)} collective-permute-done((bf16[16,640]{0,1:T(8,128)(2,1)S(1)}, bf16[16,640]{0,1:T(8,128)(2,1)S(1)}, u32[]{:S(2)}, u32[]{:S(2)}) %collective-permute-start.1) | collective-permute-done | bytes 20512 | tf_op jit(solution)/shard_map/ppermute | solution.py:435
  13.7 1.8 %collective-permute-done = bf16[16,640]{0,1:T(8,128)(2,1)S(1)} collective-permute-done((bf16[16,640]{0,1:T(8,128)(2,1)S(1)}, bf16[16,640]{0,1:T(8,128)(2,1)S(1)}, u32[]{:S(2)}, u32[]{:S(2)}) %collective-permute-start) | collective-permute-done | bytes 20512 | tf_op jit(solution)/shard_map/ppermute | solution.py:435
  15.7 3.5 %collective-permute-start.3 = (bf16[64,640]{0,1:T(8,128)(2,1)S(1)}, bf16[64,640]{0,1:T(8,128)(2,1)S(1)}, u32[]{:S(2)}, u32[]{:S(2)}) collective-permute-start(bf16[64,640]{0,1:T(8,128)(2,1)S(1)} %pad_maximum_fusion.1), channel_id=1, source_target_pairs={{0,8},{2,26},{4,12},{6,30},{8,16},{10,2},{12,20},{14,6},{16,24},{1... | collective-permute-start | bytes 245768 | tf_op jit(solution)/shard_map/ppermute | solution.py:435
  21.0 2.1 %collective-permute-done.3 = bf16[64,640]{0,1:T(8,128)(2,1)S(1)} collective-permute-done((bf16[64,640]{0,1:T(8,128)(2,1)S(1)}, bf16[64,640]{0,1:T(8,128)(2,1)S(1)}, u32[]{:S(2)}, u32[]{:S(2)}) %collective-permute-start.3) | collective-permute-done | bytes 81952 | tf_op jit(solution)/shard_map/ppermute | solution.py:435
  23.6 3.0 %collective-permute-start.6 = (bf16[136,512]{1,0:T(8,128)(2,1)S(1)}, bf16[136,512]{1,0:T(8,128)(2,1)S(1)}, u32[]{:S(2)}, u32[]{:S(2)}) collective-permute-start(bf16[136,512]{1,0:T(8,128)(2,1)S(1)} %pad_maximum_fusion.2.refs_0_), channel_id=1, source_target_pairs={{0,128},{2,3},{4,132},{6,7},{8,136},{10,11},{12,140},{14,15},{16,1... | collective-permute-start | bytes 417800 | tf_op jit(solution)/shard_map/ppermute | solution.py:435
  29.1 2.6 %collective-permute-done.5.refs_2_ = bf16[136,512]{1,0:T(8,128)(2,1)S(1)} collective-permute-done((bf16[136,512]{1,0:T(8,128)(2,1)S(1)}, bf16[136,512]{1,0:T(8,128)(2,1)S(1)}, u32[]{:S(2)}, u32[]{:S(2)}) %collective-permute-start.5) | collective-permute-done | bytes 139296 | tf_op jit(solution)/shard_map/ppermute | solution.py:435
  33.0 1.8 %collective-permute-start.9 = (bf16[544,512]{1,0:T(8,128)(2,1)S(1)}, bf16[544,512]{1,0:T(8,128)(2,1)S(1)}, u32[]{:S(2)}, u32[]{:S(2)}) collective-permute-start(bf16[544,512]{1,0:T(8,128)(2,1)S(1)} %pack.1.refs_0_), channel_id=1, source_target_pairs={{0,33},{2,194},{4,37},{6,198},{8,41},{10,202},{12,45},{14,206},{16... | collective-permute-start | bytes 1671176 | tf_op jit(solution)/shard_map/ppermute | solution.py:435
  35.5 2.6 %part.4 = (bf16[2048,512]{1,0:T(8,128)(2,1)S(1)}, s32[2,8,2048]{2,1,0:T(8,128)S(1)}, bf16[1024,2048]{1,0:T(8,128)(2,1)S(1)}, bf16[1024,2048]{1,0:T(8,128)(2,1)S(1)}, f32[8,128]{1,0:T(8,128)S(1)}) custom-call(bf16[544,512]{1,0:T(8,128)(2,1)S(1)} %pack.1.refs_0_, bf16[1024,512]{1,0:T(8,128)(2,1)S(1)} %convert_element_type.39.refs_1_.refs_2_, ...), custom_call_target="tpu_custom_call" | custom-call | flops 1073741824 | bytes 2097152 | tf_op jit(solution)/shard_map/part/pallas_call | solution.py:189
  38.1 3.9 %collective-permute-done.10.refs_0_ = bf16[544,512]{1,0:T(8,128)(2,1)S(1)} collective-permute-done((bf16[544,512]{1,0:T(8,128)(2,1)S(1)}, bf16[544,512]{1,0:T(8,128)(2,1)S(1)}, u32[]{:S(2)}, u32[]{:S(2)}) %collective-permute-start.10) | collective-permute-done | bytes 557088 | tf_op jit(solution)/shard_map/ppermute | solution.py:435
  42.0 2.6 %part.5 = (bf16[2048,512]{1,0:T(8,128)(2,1)S(1)}, s32[2,8,2048]{2,1,0:T(8,128)S(1)}, bf16[1024,2048]{1,0:T(8,128)(2,1)S(1)}, bf16[1024,2048]{1,0:T(8,128)(2,1)S(1)}, f32[8,128]{1,0:T(8,128)S(1)}) custom-call(bf16[544,512]{1,0:T(8,128)(2,1)S(1)} %collective-permute-done.10.refs_0_, ...), custom_call_target="tpu_custom_call", output_to_operand_aliasing={{0}: (3, {}), {1}: (4, {}), {2}: (5, {}), {3}: (6, {}), {4}... | custom-call | flops 1073741824 | bytes 2097152 | tf_op jit(solution)/shard_map/part/pallas_call | solution.py:189
  44.6 2.7 %collective-permute-done.9.refs_0_ = bf16[544,512]{1,0:T(8,128)(2,1)S(1)} collective-permute-done((bf16[544,512]{1,0:T(8,128)(2,1)S(1)}, bf16[544,512]{1,0:T(8,128)(2,1)S(1)}, u32[]{:S(2)}, u32[]{:S(2)}) %collective-permute-start.9) | collective-permute-done | bytes 557088 | tf_op jit(solution)/shard_map/ppermute | solution.py:435
  47.3 2.6 %part.6 = (bf16[2048,512]{1,0:T(8,128)(2,1)S(1)}, s32[2,8,2048]{2,1,0:T(8,128)S(1)}, bf16[1024,2048]{1,0:T(8,128)(2,1)S(1)}, bf16[1024,2048]{1,0:T(8,128)(2,1)S(1)}, f32[8,128]{1,0:T(8,128)S(1)}) custom-call(bf16[544,512]{1,0:T(8,128)(2,1)S(1)} %collective-permute-done.9.refs_0_, ...), custom_call_target="tpu_custom_call", output_to_operand_aliasing={{0}: (3, {}), {1}: (4, {}), {2}: (5, {}), {3}: (6, {}), {4}... | custom-call | flops 1073741824 | bytes 2097152 | tf_op jit(solution)/shard_map/part/pallas_call | solution.py:189
  49.9 5.3 %part.7 = (bf16[2048,512]{1,0:T(8,128)(2,1)S(1)}, s32[2,8,2048]{2,1,0:T(8,128)S(1)}, bf16[1024,2048]{1,0:T(8,128)(2,1)S(1)}, bf16[1024,2048]{1,0:T(8,128)(2,1)S(...) custom-call(bf16[544,512]{1,0:T(8,128)(2,1)S(1)} %collective-permute, ...), custom_call_target="tpu_custom_call", output_to_operand_aliasing={{0}: (3, {}), {1}: (4, {}), {2}: (5, {}), {3}: (6, {}), {4}... | custom-call | flops 2147483648 | bytes 2097152 | tf_op jit(solution)/shard_map/part/pallas_call | solution.py:189
  55.2 9.2 %collective-permute-start.11 = (f32[1024,512]{1,0:T(8,128)S(1)}, f32[1024,512]{1,0:T(8,128)S(1)}, u32[]{:S(2)}, u32[]{:S(2)}) collective-permute-start(f32[1024,512]{1,0:T(8,128)S(1)} %get-tuple-element.85), channel_id=1, source_target_pairs={{0,2},{2,0},{4,6},{6,4},{8,10},{10,8},{12,14},{14,12},{16,18},{18,... | collective-permute-start | bytes 6291464 | tf_op jit(solution)/shard_map/ppermute | solution.py:435
  66.0 2.5 %grad.1.refs_0_ = f32[1024,512]{1,0:T(8,128)S(1)} custom-call(bf16[1024,2048]{1,0:T(8,128)(2,1)S(1)} %get-tuple-element.97.resid_ref.refs_0_, bf16[2048,512]{1,0:T(8,128)(2,1)S(1)} %get-tuple-element.87.q_ref.refs_1_.q), custom_call_target="tpu_custom_call" | custom-call | flops 2147483648 | bytes 8388608 | tf_op jit(solution)/shard_map/grad/pallas_call | solution.py:372
  68.8 1.8 %adamw.2 = (f32[1024,512]{1,0:T(8,128)S(1)}, f32[1024,512]{1,0:T(8,128)S(1)}, f32[1024,512]{1,0:T(8,128)S(1)}, bf16[1024,512]{1,0:T(8,128)(2,1)S(1)}) custom-call(f32[1024,512]{1,0:T(8,128)S(1)} %grad.1.refs_0_, f32[1024,512]{1,0:T(8,128)S(1)} %collective-permute-done.11.refs_1_, f32[1024,512]{1,0:T(8,128)S(1)} %copy-done, f32[1024,512]{1,0:T(8,128)S(1)} %copy-done.1, ...), custom_call_target="tpu_custom_call" | custom-call | flops 10485760 | bytes 6291456 | tf_op jit(solution)/shard_map/adamw/pallas_call | solution.py:408
  70.7 2.0 %collective-permute-start.12 = (bf16[512,512]{1,0:T(8,128)(2,1)S(1)}, bf16[512,512]{1,0:T(8,128)(2,1)S(1)}, u32[]{:S(2)}, u32[]{:S(2)}) collective-permute-start(bf16[512,512]{1,0:T(8,128)(2,1)S(1)} %terms.2), channel_id=1, source_target_pairs={{0,32},{2,35},{4,36},{6,39},{8,40},{10,43},{12,44},{14,47},{16,48}... | collective-permute-start | bytes 1572872 | tf_op jit(solution)/shard_map/ppermute | solution.py:435
  74.3 3.5 %plane.2 = (bf16[1024,2048]{1,0:T(8,128)(2,1)S(1)}, bf16[1024,2048]{1,0:T(8,128)(2,1)S(1)}, bf16[512,512]{1,0:T(8,128)(2,1)S(1)}) custom-call(f32[8,128]{1,0:T(8,128)S(1)} %get-tuple-element.94.refs_0_.most, bf16[2048,512]{1,0:T(8,128)(2,1)S(1)} %get-tuple-element.87.q_ref.refs_1_.q, s32[2,8,2048]{2,1,0:T(8,128)S(1)} %get-tuple-element.95.refs_2_.pos, ...), custom_call_target="tpu_custom_call" | custom-call | flops 2147483648 | bytes 4194304 | tf_op jit(solution)/shard_map/plane/pallas_call | solution.py:313
  78.9 3.5 %plane.3 = (bf16[1024,2048]{1,0:T(8,128)(2,1)S(1)}, bf16[1024,2048]{1,0:T(8,128)(2,1)S(1)}, f32[512,512]{1,0:T(8,128)S(1)}) custom-call(f32[8,128]{1,0:T(8,128)S(1)} %get-tuple-element.94.refs_0_.most, bf16[2048,512]{1,0:T(8,128)(2,1)S(1)} %get-tuple-element.87.q_ref.refs_1_.q, ...), custom_call_target="tpu_custom_call", output_to_operand_aliasing={{0}: (5, {}), {1}: (6, {})} | custom-call | flops 2147483648 | bytes 4194304 | tf_op jit(solution)/shard_map/plane/pallas_call | solution.py:313
  82.6 1.9 %collective-permute-start.16 = (bf16[2,128,512]{2,1,0:T(8,128)(2,1)S(1)}, bf16[2,128,512]{2,1,0:T(8,128)(2,1)S(1)}, u32[]{:S(2)}, u32[]{:S(2)}) collective-permute-start(bf16[2,128,512]{2,1,0:T(8,128)(2,1)S(1)} %bitcast.40), channel_id=1, source_target_pairs={{0,64},{2,194},{4,68},{6,198},{8,72},{10,202},{12,76},{14,206},{16... | collective-permute-start | bytes 786440 | tf_op jit(solution)/shard_map/ppermute | solution.py:435
  84.5 2.6 %collective-permute-done.14 = bf16[512,512]{1,0:T(8,128)(2,1)S(1)} collective-permute-done((bf16[512,512]{1,0:T(8,128)(2,1)S(1)}, bf16[512,512]{1,0:T(8,128)(2,1)S(1)}, u32[]{:S(2)}, u32[]{:S(2)}) %collective-permute-start.14) | collective-permute-done | bytes 524320 | tf_op jit(solution)/shard_map/ppermute | solution.py:435
  87.4 1.9 %collective-permute-start.15 = (bf16[2,128,512]{2,1,0:T(8,128)(2,1)S(1)}, bf16[2,128,512]{2,1,0:T(8,128)(2,1)S(1)}, u32[]{:S(2)}, u32[]{:S(2)}) collective-permute-start(bf16[2,128,512]{2,1,0:T(8,128)(2,1)S(1)} %bitcast.41), channel_id=1, source_target_pairs={{0,64},{2,194},{4,68},{6,198},{8,72},{10,202},{12,76},{14,206},{16... | collective-permute-start | bytes 786440 | tf_op jit(solution)/shard_map/ppermute | solution.py:435
  89.2 4.5 %rest.2 = (bf16[1024,2048]{1,0:T(8,128)(2,1)S(1)}, f32[1024,512]{1,0:T(8,128)S(1)}) custom-call(f32[8,128]{1,0:T(8,128)S(1)} %get-tuple-element.94.refs_0_.most, bf16[2048,512]{1,0:T(8,128)(2,1)S(1)} %get-tuple-element.87.q_ref.refs_1_.q, s32[2,8,2048]{2,1,0:T(8,128)S(1)} %get-tuple-element.95.refs_2_.pos, ...), custom_call_target="tpu_custom_call", output_to_operand_aliasing={{0}: (4, {})} | custom-call | flops 3221225472 | bytes 8388608 | tf_op jit(solution)/shard_map/rest/pallas_call | solution.py:355
  95.8 4.5 %rest.3 = (bf16[1024,2048]{1,0:T(8,128)(2,1)S(1)}, f32[1024,512]{1,0:T(8,128)S(1)}) custom-call(f32[8,128]{1,0:T(8,128)S(1)} %get-tuple-element.94.refs_0_.most, bf16[2048,512]{1,0:T(8,128)(2,1)S(1)} %get-tuple-element.87.q_ref.refs_1_.q, s32[2,8,2048]{2,1,0:T(8,128)S(1)} %get-tuple-element.95.refs_2_.pos, ...), custom_call_target="tpu_custom_call", output_to_operand_aliasing={{0}: (4, {})} | custom-call | flops 3221225472 | bytes 8388608 | tf_op jit(solution)/shard_map/rest/pallas_call | solution.py:355
  100.3 2.0 %collective-permute-done.18 = f32[128,512]{1,0:T(8,128)S(1)} collective-permute-done((f32[128,512]{1,0:T(8,128)S(1)}, f32[128,512]{1,0:T(8,128)S(1)}, u32[]{:S(2)}, u32[]{:S(2)}) %collective-permute-start.18) | collective-permute-done | bytes 262176 | tf_op jit(solution)/shard_map/ppermute | solution.py:435
  102.6 3.7 %adamw.3 = (f32[1024,512]{1,0:T(8,128)}, f32[1024,512]{1,0:T(8,128)}, f32[1024,512]{1,0:T(8,128)}) custom-call(f32[1024,512]{1,0:T(8,128)S(1)} %get-tuple-element.124.refs_0_, f32[1024,512]{1,0:T(8,128)S(1)} %collective-permute-done.20.refs_1_, f32[1024,512]{1,0:T(8,128)S(1)} %get-tuple-element.126.refs_2_, f32[1024,512]{1,0:T(8,128)S(1)} %get-tuple-element.127.refs_3_, ...), custom_call_target="tpu_custom_call" | custom-call | flops 10485760 | bytes 6291456 | tf_op jit(solution)/shard_map/adamw/pallas_call | solution.py:408
  106.3 2.2 %collective-permute-done.19 = bf16[4,2,16,512]{3,2,1,0:T(8,128)(2,1)S(1)} collective-permute-done((bf16[4,2,16,512]{3,2,1,0:T(8,128)(2,1)S(1)}, bf16[4,2,16,512]{3,2,1,0:T(8,128)(2,1)S(1)}, u32[]{:S(2)}, u32[]{:S(2)}) %collective-permute-start.19) | collective-permute-done | bytes 131104 | tf_op jit(solution)/shard_map/ppermute | solution.py:435
  110.3 3.1 %collective-permute-start.23 = (f32[2,16,512]{2,1,0:T(8,128)S(1)}, f32[2,16,512]{2,1,0:T(8,128)S(1)}, u32[]{:S(2)}, u32[]{:S(2)}) collective-permute-start(f32[2,16,512]{2,1,0:T(8,128)S(1)} %get-tuple-element.137), channel_id=1, source_target_pairs={{0,26},{2,8},{4,30},{6,12},{8,2},{10,16},{12,6},{14,20},{16,10},{1... | collective-permute-start | bytes 196616 | tf_op jit(solution)/shard_map/ppermute | solution.py:435
  113.6 2.4 %collective-permute-done.23 = f32[2,16,512]{2,1,0:T(8,128)S(1)} collective-permute-done((f32[2,16,512]{2,1,0:T(8,128)S(1)}, f32[2,16,512]{2,1,0:T(8,128)S(1)}, u32[]{:S(2)}, u32[]{:S(2)}) %collective-permute-start.23) | collective-permute-done | bytes 65568 | tf_op jit(solution)/shard_map/ppermute | solution.py:435
  116.0 1.8 %collective-permute-done.22 = f32[2,16,512]{2,1,0:T(8,128)S(1)} collective-permute-done((f32[2,16,512]{2,1,0:T(8,128)S(1)}, f32[2,16,512]{2,1,0:T(8,128)S(1)}, u32[]{:S(2)}, u32[]{:S(2)}) %collective-permute-start.22) | collective-permute-done | bytes 65568 | tf_op jit(solution)/shard_map/ppermute | solution.py:435
  (62 shorter events, 21.6 us)
Async XLA Ops:
  0.6 0.7 copy-start.3
  1.3 0.7 copy-start.4
  2.4 9.5 %collective-permute-start.2 = (bf16[16,640]{0,1:T(8,128)(2,1)S(1)}, bf16[16,640]{0,1:T(8,128)(2,1)S(1)}, u32[]{:S(2)}, u32[]{:S(2)}) collective-permute-start(bf16[16,640]{0,1:T(8,128)(2,1)S(1)} %copy.32), channel_id=1, source_target_pairs={{0,26},{2,8},{4,30},{6,12},{8,2},{10,16},{12,6},{14,20},{16,10},{1... | collective-permute-start | bytes 61448 | tf_op jit(solution)/shard_map/ppermute | solution.py:435
  6.9 6.8 %collective-permute-start.1 = (bf16[16,640]{0,1:T(8,128)(2,1)S(1)}, bf16[16,640]{0,1:T(8,128)(2,1)S(1)}, u32[]{:S(2)}, u32[]{:S(2)}) collective-permute-start(bf16[16,640]{0,1:T(8,128)(2,1)S(1)} %copy.32), channel_id=1, source_target_pairs={{0,4},{2,30},{4,8},{6,2},{8,12},{10,6},{12,16},{14,10},{16,20},{18... | collective-permute-start | bytes 61448 | tf_op jit(solution)/shard_map/ppermute | solution.py:435
  9.0 6.5 %collective-permute-start = (bf16[16,640]{0,1:T(8,128)(2,1)S(1)}, bf16[16,640]{0,1:T(8,128)(2,1)S(1)}, u32[]{:S(2)}, u32[]{:S(2)}) collective-permute-start(bf16[16,640]{0,1:T(8,128)(2,1)S(1)} %copy.32), channel_id=1, source_target_pairs={{0,30},{2,4},{4,2},{6,8},{8,6},{10,12},{12,10},{14,16},{16,14},{18... | collective-permute-start | bytes 61448 | tf_op jit(solution)/shard_map/ppermute | solution.py:435
  15.7 7.4 %collective-permute-start.3 = (bf16[64,640]{0,1:T(8,128)(2,1)S(1)}, bf16[64,640]{0,1:T(8,128)(2,1)S(1)}, u32[]{:S(2)}, u32[]{:S(2)}) collective-permute-start(bf16[64,640]{0,1:T(8,128)(2,1)S(1)} %pad_maximum_fusion.1), channel_id=1, source_target_pairs={{0,8},{2,26},{4,12},{6,30},{8,16},{10,2},{12,20},{14,6},{16,24},{1... | collective-permute-start | bytes 245768 | tf_op jit(solution)/shard_map/ppermute | solution.py:435
  20.9 14.6 %collective-permute-start.8 = (bf16[1024,512]{1,0:T(8,128)(2,1)S(1)}, bf16[1024,512]{1,0:T(8,128)(2,1)S(1)}, u32[]{:S(2)}, u32[]{:S(2)}) collective-permute-start(bf16[1024,512]{1,0:T(8,128)(2,1)S(1)} %convert_element_type.39.refs_1_.refs_2_), channel_id=1, source_target_pairs={{0,2},{2,0},{4,6},{6,4},{8,10},{10,8},{12,14},{14,12},{16,18},{18,... | collective-permute-start | bytes 3145736 | tf_op jit(solution)/shard_map/ppermute | solution.py:435
  23.6 5.5 %collective-permute-start.6 = (bf16[136,512]{1,0:T(8,128)(2,1)S(1)}, bf16[136,512]{1,0:T(8,128)(2,1)S(1)}, u32[]{:S(2)}, u32[]{:S(2)}) collective-permute-start(bf16[136,512]{1,0:T(8,128)(2,1)S(1)} %pad_maximum_fusion.2.refs_0_), channel_id=1, source_target_pairs={{0,128},{2,3},{4,132},{6,7},{8,136},{10,11},{12,140},{14,15},{16,1... | collective-permute-start | bytes 417800 | tf_op jit(solution)/shard_map/ppermute | solution.py:435
  26.6 5.1 %collective-permute-start.5 = (bf16[136,512]{1,0:T(8,128)(2,1)S(1)}, bf16[136,512]{1,0:T(8,128)(2,1)S(1)}, u32[]{:S(2)}, u32[]{:S(2)}) collective-permute-start(bf16[136,512]{1,0:T(8,128)(2,1)S(1)} %pad_maximum_fusion.2.refs_0_), channel_id=1, source_target_pairs={{0,192},{2,35},{4,196},{6,39},{8,200},{10,43},{12,204},{14,47},{16... | collective-permute-start | bytes 417800 | tf_op jit(solution)/shard_map/ppermute | solution.py:435
  27.4 4.3 %collective-permute-start.4 = (bf16[136,512]{1,0:T(8,128)(2,1)S(1)}, bf16[136,512]{1,0:T(8,128)(2,1)S(1)}, u32[]{:S(2)}, u32[]{:S(2)}) collective-permute-start(bf16[136,512]{1,0:T(8,128)(2,1)S(1)} %pad_maximum_fusion.2.refs_0_), channel_id=1, source_target_pairs={{0,64},{2,34},{4,68},{6,38},{8,72},{10,42},{12,76},{14,46},{16,80}... | collective-permute-start | bytes 417800 | tf_op jit(solution)/shard_map/ppermute | solution.py:435
  31.8 10.3 %collective-permute-start.10 = (bf16[544,512]{1,0:T(8,128)(2,1)S(1)}, bf16[544,512]{1,0:T(8,128)(2,1)S(1)}, u32[]{:S(2)}, u32[]{:S(2)}) collective-permute-start(bf16[544,512]{1,0:T(8,128)(2,1)S(1)} %pack.1.refs_0_), channel_id=1, source_target_pairs={{0,32},{2,66},{4,36},{6,70},{8,40},{10,74},{12,44},{14,78},{16,48}... | collective-permute-start | bytes 1671176 | tf_op jit(solution)/shard_map/ppermute | solution.py:435
  33.0 14.3 %collective-permute-start.9 = (bf16[544,512]{1,0:T(8,128)(2,1)S(1)}, bf16[544,512]{1,0:T(8,128)(2,1)S(1)}, u32[]{:S(2)}, u32[]{:S(2)}) collective-permute-start(bf16[544,512]{1,0:T(8,128)(2,1)S(1)} %pack.1.refs_0_), channel_id=1, source_target_pairs={{0,33},{2,194},{4,37},{6,198},{8,41},{10,202},{12,45},{14,206},{16... | collective-permute-start | bytes 1671176 | tf_op jit(solution)/shard_map/ppermute | solution.py:435
  34.9 15.0 %collective-permute-start.7 = (bf16[544,512]{1,0:T(8,128)(2,1)S(1)}, bf16[544,512]{1,0:T(8,128)(2,1)S(1)}, u32[]{:S(2)}, u32[]{:S(2)}) collective-permute-start(bf16[544,512]{1,0:T(8,128)(2,1)S(1)} %pack.1.refs_0_), channel_id=1, source_target_pairs={{0,1},{2,130},{4,5},{6,134},{8,9},{10,138},{12,13},{14,142},{16,17... | collective-permute-start | bytes 1671176 | tf_op jit(solution)/shard_map/ppermute | solution.py:435
  55.2 13.3 %collective-permute-start.11 = (f32[1024,512]{1,0:T(8,128)S(1)}, f32[1024,512]{1,0:T(8,128)S(1)}, u32[]{:S(2)}, u32[]{:S(2)}) collective-permute-start(f32[1024,512]{1,0:T(8,128)S(1)} %get-tuple-element.85), channel_id=1, source_target_pairs={{0,2},{2,0},{4,6},{6,4},{8,10},{10,8},{12,14},{14,12},{16,18},{18,... | collective-permute-start | bytes 6291464 | tf_op jit(solution)/shard_map/ppermute | solution.py:435
  66.0 2.5 %copy-start = (f32[1024,512]{1,0:T(8,128)S(1)}, f32[1024,512]{1,0:T(8,128)}, u32[]{:S(2)}) copy-start(f32[1024,512]{1,0:T(8,128)} %refs_2_.1) | copy-start | bytes 6291460
  66.0 2.5 %copy-start.1 = (f32[1024,512]{1,0:T(8,128)S(1)}, f32[1024,512]{1,0:T(8,128)}, u32[]{:S(2)}) copy-start(f32[1024,512]{1,0:T(8,128)} %refs_3_.1) | copy-start | bytes 6291460
  66.0 2.8 %copy-start.2 = (f32[1024,512]{1,0:T(8,128)S(1)}, f32[1024,512]{1,0:T(8,128)}, u32[]{:S(2)}) copy-start(f32[1024,512]{1,0:T(8,128)} %refs_4_.1) | copy-start | bytes 6291460
  70.6 3.7 %collective-permute-start.13 = (bf16[1024,512]{1,0:T(8,128)(2,1)S(1)}, bf16[1024,512]{1,0:T(8,128)(2,1)S(1)}, u32[]{:S(2)}, u32[]{:S(2)}) collective-permute-start(bf16[1024,512]{1,0:T(8,128)(2,1)S(1)} %get-tuple-element.96.refs_3_.wb), channel_id=1, source_target_pairs={{0,2},{2,0},{4,6},{6,4},{8,10},{10,8},{12,14},{14,12},{16,18},{18,... | collective-permute-start | bytes 3145736 | tf_op jit(solution)/shard_map/ppermute | solution.py:435
  70.7 11.7 %collective-permute-start.12 = (bf16[512,512]{1,0:T(8,128)(2,1)S(1)}, bf16[512,512]{1,0:T(8,128)(2,1)S(1)}, u32[]{:S(2)}, u32[]{:S(2)}) collective-permute-start(bf16[512,512]{1,0:T(8,128)(2,1)S(1)} %terms.2), channel_id=1, source_target_pairs={{0,32},{2,35},{4,36},{6,39},{8,40},{10,43},{12,44},{14,47},{16,48}... | collective-permute-start | bytes 1572872 | tf_op jit(solution)/shard_map/ppermute | solution.py:435
  77.8 9.3 %collective-permute-start.14 = (bf16[512,512]{1,0:T(8,128)(2,1)S(1)}, bf16[512,512]{1,0:T(8,128)(2,1)S(1)}, u32[]{:S(2)}, u32[]{:S(2)}) collective-permute-start(bf16[512,512]{1,0:T(8,128)(2,1)S(1)} %get-tuple-element.109), channel_id=1, source_target_pairs={{0,32},{2,35},{4,36},{6,39},{8,40},{10,43},{12,44},{14,47},{16,48}... | collective-permute-start | bytes 1572872 | tf_op jit(solution)/shard_map/ppermute | solution.py:435
  82.6 11.1 %collective-permute-start.16 = (bf16[2,128,512]{2,1,0:T(8,128)(2,1)S(1)}, bf16[2,128,512]{2,1,0:T(8,128)(2,1)S(1)}, u32[]{:S(2)}, u32[]{:S(2)}) collective-permute-start(bf16[2,128,512]{2,1,0:T(8,128)(2,1)S(1)} %bitcast.40), channel_id=1, source_target_pairs={{0,64},{2,194},{4,68},{6,198},{8,72},{10,202},{12,76},{14,206},{16... | collective-permute-start | bytes 786440 | tf_op jit(solution)/shard_map/ppermute | solution.py:435
  87.4 6.5 %collective-permute-start.15 = (bf16[2,128,512]{2,1,0:T(8,128)(2,1)S(1)}, bf16[2,128,512]{2,1,0:T(8,128)(2,1)S(1)}, u32[]{:S(2)}, u32[]{:S(2)}) collective-permute-start(bf16[2,128,512]{2,1,0:T(8,128)(2,1)S(1)} %bitcast.41), channel_id=1, source_target_pairs={{0,64},{2,194},{4,68},{6,198},{8,72},{10,202},{12,76},{14,206},{16... | collective-permute-start | bytes 786440 | tf_op jit(solution)/shard_map/ppermute | solution.py:435
  93.9 8.7 %collective-permute-start.20 = (f32[1024,512]{1,0:T(8,128)S(1)}, f32[1024,512]{1,0:T(8,128)S(1)}, u32[]{:S(2)}, u32[]{:S(2)}) collective-permute-start(f32[1024,512]{1,0:T(8,128)S(1)} %get-tuple-element.125), channel_id=1, source_target_pairs={{0,2},{2,0},{4,6},{6,4},{8,10},{10,8},{12,14},{14,12},{16,18},{18,... | collective-permute-start | bytes 6291464 | tf_op jit(solution)/shard_map/ppermute | solution.py:435
  93.9 6.4 %collective-permute-start.17 = (f32[128,512]{1,0:T(8,128)S(1)}, f32[128,512]{1,0:T(8,128)S(1)}, u32[]{:S(2)}, u32[]{:S(2)}) collective-permute-start(f32[128,512]{1,0:T(8,128)S(1)} %add_bitcast_fusion.1), channel_id=1, source_target_pairs={{0,192},{2,66},{4,196},{6,70},{8,200},{10,74},{12,204},{14,78},{16... | collective-permute-start | bytes 786440 | tf_op jit(solution)/shard_map/ppermute | solution.py:435
  94.1 8.3 %collective-permute-start.18 = (f32[128,512]{1,0:T(8,128)S(1)}, f32[128,512]{1,0:T(8,128)S(1)}, u32[]{:S(2)}, u32[]{:S(2)}) collective-permute-start(f32[128,512]{1,0:T(8,128)S(1)} %add_bitcast_fusion), channel_id=1, source_target_pairs={{0,192},{2,66},{4,196},{6,70},{8,200},{10,74},{12,204},{14,78},{16... | collective-permute-start | bytes 786440 | tf_op jit(solution)/shard_map/ppermute | solution.py:435
  102.5 6.0 %collective-permute-start.19 = (bf16[4,2,16,512]{3,2,1,0:T(8,128)(2,1)S(1)}, bf16[4,2,16,512]{3,2,1,0:T(8,128)(2,1)S(1)}, u32[]{:S(2)}, u32[]{:S(2)}) collective-permute-start(bf16[4,2,16,512]{3,2,1,0:T(8,128)(2,1)S(1)} %fusion.1), channel_id=1, source_target_pairs={{0,24},{2,10},{4,28},{6,14},{8,0},{10,18},{12,4},{14,22},{16,8},{1... | collective-permute-start | bytes 393224 | tf_op jit(solution)/shard_map/ppermute | solution.py:435
  108.6 5.1 %collective-permute-start.21 = (f32[2,16,512]{2,1,0:T(8,128)S(1)}, f32[2,16,512]{2,1,0:T(8,128)S(1)}, u32[]{:S(2)}, u32[]{:S(2)}) collective-permute-start(f32[2,16,512]{2,1,0:T(8,128)S(1)} %get-tuple-element.136), channel_id=1, source_target_pairs={{0,30},{2,4},{4,2},{6,8},{8,6},{10,12},{12,10},{14,16},{16,14},{18... | collective-permute-start | bytes 196616 | tf_op jit(solution)/shard_map/ppermute | solution.py:435
  110.3 5.7 %collective-permute-start.23 = (f32[2,16,512]{2,1,0:T(8,128)S(1)}, f32[2,16,512]{2,1,0:T(8,128)S(1)}, u32[]{:S(2)}, u32[]{:S(2)}) collective-permute-start(f32[2,16,512]{2,1,0:T(8,128)S(1)} %get-tuple-element.137), channel_id=1, source_target_pairs={{0,26},{2,8},{4,30},{6,12},{8,2},{10,16},{12,6},{14,20},{16,10},{1... | collective-permute-start | bytes 196616 | tf_op jit(solution)/shard_map/ppermute | solution.py:435
  113.4 4.4 %collective-permute-start.22 = (f32[2,16,512]{2,1,0:T(8,128)S(1)}, f32[2,16,512]{2,1,0:T(8,128)S(1)}, u32[]{:S(2)}, u32[]{:S(2)}) collective-permute-start(f32[2,16,512]{2,1,0:T(8,128)S(1)} %get-tuple-element.138), channel_id=1, source_target_pairs={{0,28},{2,6},{4,0},{6,10},{8,4},{10,14},{12,8},{14,18},{16,12},{18... | collective-permute-start | bytes 196616 | tf_op jit(solution)/shard_map/ppermute | solution.py:435
where the time goes:
time: 119 us; the launch traced here: 118 us
  starting transfers between devices  42.3 us (36%)
  Pallas kernels  40.2 us (34%)
  waiting for transfers between devices  29.3 us (25%)
  other arithmetic  3.21 us (3%)
  local copies, waits for them, and re-layouts  2.44 us (2%)
    ppermute x24, starting transfers between devices, send(): return lax.ppermute(array, AXES, moved(move))  42.3 us
    ppermute x24, waiting for transfers between devices, send(): return lax.ppermute(array, AXES, moved(move))  29.3 us
    pallas_call x4, Pallas kernels, first_residuals(): pl.pallas_call(lambda *refs: part_kernel(*refs, late=late), out_shape=sha...  13 us
    pallas_call x2, Pallas kernels, rest_gradient(): pl.pallas_call(lambda most, q, pos, wb, old, resid, out: rest_kernel(most...  9.01 us
    pallas_call x2, Pallas kernels, plane_terms(): pl.pallas_call(lambda *refs: plane_kernel(*refs, blocks=blocks), out_shap...  7 us
    pallas_call x2, Pallas kernels, update(): pl.pallas_call(lambda *refs: adamw_kernel(count, *refs), grid=(LAB // TIL...  5.43 us
    pallas_call x2, Pallas kernels, terms(): pl.pallas_call(lambda *refs: terms_kernel(*refs, blocks=blocks), out_shap...  3.03 us
    pallas_call x1, Pallas kernels, gradient(): pl.pallas_call(grad_kernel, out_shape=jax.ShapeDtypeStruct((LAB, D), f32)...  2.49 us
  transfers between devices with their start and end apart: 24, of which 14 were waited for; matrix products, arithmetic and copies ran while one was open for 2% of the time, Pallas kernels for 28%

commit v1 on v0

--- a/solution.py
+++ b/solution.py
@@ -72,7 +72,7 @@
     high, core = here_is()[:2]
     y = late + core * (early - late)
     x = early + core * (late - early)
-    return (y ^ (2 * high)) * NX + ((x + core * (4 - 2 * x)) & 3)
+    return (y ^ (2 * high)) * NX + gray((x + (1 - core) * (4 - 2 * x)) & 3)
 
 
 def span(late, early):
@@ -460,6 +460,10 @@
     return lambda x, y, z, core: (x, y, *moves[2 * z + core])
 
 
+def then(one, two):
+    return lambda *at: two(*(i % n for i, n in zip(one(*at), (NX, NY, NZ, NCORE))))
+
+
 def swap(array):
     return send(array, lambda x, y, z, core: (x, y, z, 1 - core))
 
@@ -483,10 +487,9 @@
 
 def shards(queries, positives, weights, first_moment, second_moment):
     weight, first, second = weights, first_moment, second_moment
-    to_plane = lambda part: send(part, by_core(along_y(1), along_y(3)))
-    to_half = lambda plane: send(plane[1:3].astype(bf16), by_core(along_x(1), along_x(3)))
-    to_line = lambda plane, got: send(plane[3] + got[1].astype(f32), by_core(along_x(3), along_x(1)))
-    as_plane = lambda part, got: (part + got.astype(f32)).reshape(NX, LINE, D)
+    over_y = by_core(along_y(1), along_y(3))
+    first_x = by_core(along_x(1), along_x(3))
+    second_x = by_core(along_x(3), along_x(1))
 
     wb = weight.astype(bf16)
     wb_other = swap(wb)
@@ -504,39 +507,38 @@
 
     wb_other = swap(wb)
     wb, out0, *step0 = after(wb, out0, *step0)
-    out0 = to_plane(out0)
+    out0 = send(out0, over_y)
     part0 = terms(*step0, here, f32)
     wb_other, part0 = after(wb_other, part0)
     own, other, out1 = plane_terms(most, q, pos, wb, wb_other, beside, bf16)
 
     out1, own, other = after(out1, own, other)
-    out1 = to_plane(out1)
+    got = [send(out1[:BLOCK], over_y), send(out1[BLOCK:], then(over_y, first_x))]
     own, other, part1 = plane_terms(most, q, pos, wb, wb_other, here, f32, (own, other))
     out0, part1 = after(out0, part1)
-    plane0 = as_plane(part0, out0)
-    half0 = to_half(plane0)
-    plane1 = as_plane(part1, out1)
-
-    half1 = to_half(plane1)
-    plane1, plane0, other = after(plane1, plane0, other)
+    got.append(send(part1[BLOCK:].astype(bf16), first_x))
+    part0 = part0 + out0.astype(f32)
+    half0 = send(part0[BLOCK:].astype(bf16), first_x)
+
+    part1, part0, other = after(part1, part0, other)
     theirs = rest_gradient(most, q, pos, wb_other, other, 1)
-    half1, half0, theirs, own = after(half1, half0, theirs, own)
-
+    *got, half0, theirs, own = after(*got, half0, theirs, own)
     part = swap(theirs)
-    quarter1 = to_line(plane1, half1)
-    quarter0 = to_line(plane0, half0)
+    pair0 = part0[:BLOCK] + half0.astype(f32)
+    pair1 = part1[:BLOCK] + got[0].astype(f32) + got[1].astype(f32) + got[2].astype(f32)
+
+    lines = jnp.stack([pair.reshape(2, NZ, ROWS, D) for pair in (pair0, pair1)], axis=2)
+    far = lines.astype(bf16)
+    got = [send(far[1, :4], second_x), send(far[0, 4:], onward(4)), send(far[1, 4:], then(second_x, onward(4)))]
+    lines, own = after(lines, own)
     mine = rest_gradient(most, q, pos, wb, own, 0)
-    quarter1, quarter0, mine = after(quarter1, quarter0, mine)
-    line = [
-        plane[0] + half[0].astype(f32) + quarter
-        for plane, half, quarter in ((plane0, half0, quarter0), (plane1, half1, quarter1))
-    ]
-    line = jnp.stack([part.reshape(NZ, ROWS, D) for part in line], axis=1)
-    got = send(line[4:].astype(bf16), onward(4))
+    *got, mine = after(*got, mine)
+    line = lines[0, :4] + got[0].astype(f32) + got[1].astype(f32) + got[2].astype(f32)
+
+    got = [send(line[by], onward(by)) for by in (1, 2, 3)]
+    line, mine = after(line, mine)
     weight, first, second = update(past_steps + 2, True, mine, part, weight, first, second)
-    got, weight, first, second = after(got, weight, first, second)
-    line = line[:4] + got.astype(f32)
-    got = [send(line[by], onward(by)) for by in (1, 2, 3)]
+    *got, weight, first, second = after(*got, weight, first, second)
     return weight, first, second, line[0] + got[0] + got[1] + got[2]
 
 

time: 119 us -> 116 us (0.975)
  waiting for transfers between devices: 29.3 us -> 20.2 us
  starting transfers between devices: 42.3 us -> 48.7 us
    ppermute x24 -> x25, waiting for transfers between devices: 29.3 us -> 20.2 us  [send(): return lax.ppermute(array, AXES, moved(move))]
    ppermute x24 -> x25, starting transfers between devices: 42.3 us -> 48.7 us  [send(): return lax.ppermute(array, AXES, moved(move))]
  transfers between devices with their start and end apart: 24 -> 25, of which waited for: 14 -> 9; matrix products, arithmetic and copies ran while one was open for 2% -> 3% of each run, Pallas kernels for 28% -> 28%
where the time goes in v1:
time: 116 us
  starting transfers between devices  48.7 us (42%)
  Pallas kernels  40.2 us (35%)
  waiting for transfers between devices  20.2 us (17%)
  other arithmetic  3.26 us (3%)
  local copies, waits for them, and re-layouts  2.5 us (2%)
    ppermute x25, starting transfers between devices, send(): return lax.ppermute(array, AXES, moved(move))  48.7 us
    ppermute x25, waiting for transfers between devices, send(): return lax.ppermute(array, AXES, moved(move))  20.2 us
    pallas_call x4, Pallas kernels, first_residuals(): pl.pallas_call(lambda *refs: part_kernel(*refs, late=late), out_shape=sha...  13 us
    pallas_call x2, Pallas kernels, rest_gradient(): pl.pallas_call(lambda most, q, pos, wb, old, resid, out: rest_kernel(most...  9.02 us
    pallas_call x2, Pallas kernels, plane_terms(): pl.pallas_call(lambda *refs: plane_kernel(*refs, blocks=blocks), out_shap...  7.01 us
    pallas_call x2, Pallas kernels, update(): pl.pallas_call(lambda *refs: adamw_kernel(count, *refs), grid=(LAB // TIL...  5.39 us
    pallas_call x2, Pallas kernels, terms(): pl.pallas_call(lambda *refs: terms_kernel(*refs, blocks=blocks), out_shap...  3.03 us
    pallas_call x1, Pallas kernels, gradient(): pl.pallas_call(grad_kernel, out_shape=jax.ShapeDtypeStruct((LAB, D), f32)...  2.49 us
  transfers between devices with their start and end apart: 25, of which 9 were waited for; matrix products, arithmetic and copies ran while one was open for 3% of the time, Pallas kernels for 28%

profile of v1, /device:TPU:1, one launch (start us, length us, event | category | flops | bytes accessed | tf_op | source)
XLA Modules:
  0.0 115.8 jit_solution(14312783719848472393)
XLA Ops:
  2.4 4.5 %collective-permute-start.2 = (bf16[16,640]{0,1:T(8,128)(2,1)S(1)}, bf16[16,640]{0,1:T(8,128)(2,1)S(1)}, u32[]{:S(2)}, u32[]{:S(2)}) collective-permute-start(bf16[16,640]{0,1:T(8,128)(2,1)S(1)} %copy.32), channel_id=1, source_target_pairs={{0,26},{2,8},{4,30},{6,12},{8,2},{10,16},{12,6},{14,20},{16,10},{1... | collective-permute-start | bytes 61448 | tf_op jit(solution)/shard_map/ppermute | solution.py:435
  6.9 2.1 %collective-permute-start.1 = (bf16[16,640]{0,1:T(8,128)(2,1)S(1)}, bf16[16,640]{0,1:T(8,128)(2,1)S(1)}, u32[]{:S(2)}, u32[]{:S(2)}) collective-permute-start(bf16[16,640]{0,1:T(8,128)(2,1)S(1)} %copy.32), channel_id=1, source_target_pairs={{0,4},{2,30},{4,8},{6,2},{8,12},{10,6},{12,16},{14,10},{16,20},{18... | collective-permute-start | bytes 61448 | tf_op jit(solution)/shard_map/ppermute | solution.py:435
  11.9 1.8 %collective-permute-done.1 = bf16[16,640]{0,1:T(8,128)(2,1)S(1)} collective-permute-done((bf16[16,640]{0,1:T(8,128)(2,1)S(1)}, bf16[16,640]{0,1:T(8,128)(2,1)S(1)}, u32[]{:S(2)}, u32[]{:S(2)}) %collective-permute-start.1) | collective-permute-done | bytes 20512 | tf_op jit(solution)/shard_map/ppermute | solution.py:435
  13.7 1.8 %collective-permute-done = bf16[16,640]{0,1:T(8,128)(2,1)S(1)} collective-permute-done((bf16[16,640]{0,1:T(8,128)(2,1)S(1)}, bf16[16,640]{0,1:T(8,128)(2,1)S(1)}, u32[]{:S(2)}, u32[]{:S(2)}) %collective-permute-start) | collective-permute-done | bytes 20512 | tf_op jit(solution)/shard_map/ppermute | solution.py:435
  15.7 3.5 %collective-permute-start.3 = (bf16[64,640]{0,1:T(8,128)(2,1)S(1)}, bf16[64,640]{0,1:T(8,128)(2,1)S(1)}, u32[]{:S(2)}, u32[]{:S(2)}) collective-permute-start(bf16[64,640]{0,1:T(8,128)(2,1)S(1)} %pad_maximum_fusion.1), channel_id=1, source_target_pairs={{0,8},{2,26},{4,12},{6,30},{8,16},{10,2},{12,20},{14,6},{16,24},{1... | collective-permute-start | bytes 245768 | tf_op jit(solution)/shard_map/ppermute | solution.py:435
  19.2 1.7 %convert_element_type.34.refs_1_.refs_2_ = bf16[1024,512]{1,0:T(8,128)(2,1)S(1)} convert(f32[1024,512]{1,0:T(8,128)} %refs_2_.1) | non-fusion elementwise | flops 524288 | bytes 3145728 | tf_op jit(solution)/shard_map/convert_element_type | solution.py:494
  21.0 2.1 %collective-permute-done.3 = bf16[64,640]{0,1:T(8,128)(2,1)S(1)} collective-permute-done((bf16[64,640]{0,1:T(8,128)(2,1)S(1)}, bf16[64,640]{0,1:T(8,128)(2,1)S(1)}, u32[]{:S(2)}, u32[]{:S(2)}) %collective-permute-start.3) | collective-permute-done | bytes 81952 | tf_op jit(solution)/shard_map/ppermute | solution.py:435
  23.6 3.0 %collective-permute-start.6 = (bf16[136,512]{1,0:T(8,128)(2,1)S(1)}, bf16[136,512]{1,0:T(8,128)(2,1)S(1)}, u32[]{:S(2)}, u32[]{:S(2)}) collective-permute-start(bf16[136,512]{1,0:T(8,128)(2,1)S(1)} %pad_maximum_fusion.2.refs_0_), channel_id=1, source_target_pairs={{0,128},{2,3},{4,132},{6,7},{8,136},{10,11},{12,140},{14,15},{16,1... | collective-permute-start | bytes 417800 | tf_op jit(solution)/shard_map/ppermute | solution.py:435
  27.4 1.7 %collective-permute-done.6.refs_3_ = bf16[136,512]{1,0:T(8,128)(2,1)S(1)} collective-permute-done((bf16[136,512]{1,0:T(8,128)(2,1)S(1)}, bf16[136,512]{1,0:T(8,128)(2,1)S(1)}, u32[]{:S(2)}, u32[]{:S(2)}) %collective-permute-start.6) | collective-permute-done | bytes 139296 | tf_op jit(solution)/shard_map/ppermute | solution.py:435
  29.1 2.6 %collective-permute-done.5.refs_2_ = bf16[136,512]{1,0:T(8,128)(2,1)S(1)} collective-permute-done((bf16[136,512]{1,0:T(8,128)(2,1)S(1)}, bf16[136,512]{1,0:T(8,128)(2,1)S(1)}, u32[]{:S(2)}, u32[]{:S(2)}) %collective-permute-start.5) | collective-permute-done | bytes 139296 | tf_op jit(solution)/shard_map/ppermute | solution.py:435
  33.0 1.8 %collective-permute-start.9 = (bf16[544,512]{1,0:T(8,128)(2,1)S(1)}, bf16[544,512]{1,0:T(8,128)(2,1)S(1)}, u32[]{:S(2)}, u32[]{:S(2)}) collective-permute-start(bf16[544,512]{1,0:T(8,128)(2,1)S(1)} %pack.1.refs_0_), channel_id=1, source_target_pairs={{0,33},{2,194},{4,37},{6,198},{8,41},{10,202},{12,45},{14,206},{16... | collective-permute-start | bytes 1671176 | tf_op jit(solution)/shard_map/ppermute | solution.py:435
  35.5 2.6 %part.4 = (bf16[2048,512]{1,0:T(8,128)(2,1)S(1)}, s32[2,8,2048]{2,1,0:T(8,128)S(1)}, bf16[1024,2048]{1,0:T(8,128)(2,1)S(1)}, bf16[1024,2048]{1,0:T(8,128)(2,1)S(1)}, f32[8,128]{1,0:T(8,128)S(1)}) custom-call(bf16[544,512]{1,0:T(8,128)(2,1)S(1)} %pack.1.refs_0_, bf16[1024,512]{1,0:T(8,128)(2,1)S(1)} %convert_element_type.34.refs_1_.refs_2_, ...), custom_call_target="tpu_custom_call" | custom-call | flops 1073741824 | bytes 2097152 | tf_op jit(solution)/shard_map/part/pallas_call | solution.py:189
  38.1 3.9 %collective-permute-done.10.refs_0_ = bf16[544,512]{1,0:T(8,128)(2,1)S(1)} collective-permute-done((bf16[544,512]{1,0:T(8,128)(2,1)S(1)}, bf16[544,512]{1,0:T(8,128)(2,1)S(1)}, u32[]{:S(2)}, u32[]{:S(2)}) %collective-permute-start.10) | collective-permute-done | bytes 557088 | tf_op jit(solution)/shard_map/ppermute | solution.py:435
  42.0 2.6 %part.5 = (bf16[2048,512]{1,0:T(8,128)(2,1)S(1)}, s32[2,8,2048]{2,1,0:T(8,128)S(1)}, bf16[1024,2048]{1,0:T(8,128)(2,1)S(1)}, bf16[1024,2048]{1,0:T(8,128)(2,1)S(1)}, f32[8,128]{1,0:T(8,128)S(1)}) custom-call(bf16[544,512]{1,0:T(8,128)(2,1)S(1)} %collective-permute-done.10.refs_0_, ...), custom_call_target="tpu_custom_call", output_to_operand_aliasing={{0}: (3, {}), {1}: (4, {}), {2}: (5, {}), {3}: (6, {}), {4}... | custom-call | flops 1073741824 | bytes 2097152 | tf_op jit(solution)/shard_map/part/pallas_call | solution.py:189
  44.6 2.7 %collective-permute-done.9.refs_0_ = bf16[544,512]{1,0:T(8,128)(2,1)S(1)} collective-permute-done((bf16[544,512]{1,0:T(8,128)(2,1)S(1)}, bf16[544,512]{1,0:T(8,128)(2,1)S(1)}, u32[]{:S(2)}, u32[]{:S(2)}) %collective-permute-start.9) | collective-permute-done | bytes 557088 | tf_op jit(solution)/shard_map/ppermute | solution.py:435
  47.3 2.6 %part.6 = (bf16[2048,512]{1,0:T(8,128)(2,1)S(1)}, s32[2,8,2048]{2,1,0:T(8,128)S(1)}, bf16[1024,2048]{1,0:T(8,128)(2,1)S(1)}, bf16[1024,2048]{1,0:T(8,128)(2,1)S(1)}, f32[8,128]{1,0:T(8,128)S(1)}) custom-call(bf16[544,512]{1,0:T(8,128)(2,1)S(1)} %collective-permute-done.9.refs_0_, ...), custom_call_target="tpu_custom_call", output_to_operand_aliasing={{0}: (3, {}), {1}: (4, {}), {2}: (5, {}), {3}: (6, {}), {4}... | custom-call | flops 1073741824 | bytes 2097152 | tf_op jit(solution)/shard_map/part/pallas_call | solution.py:189
  49.9 5.3 %part.7 = (bf16[2048,512]{1,0:T(8,128)(2,1)S(1)}, s32[2,8,2048]{2,1,0:T(8,128)S(1)}, bf16[1024,2048]{1,0:T(8,128)(2,1)S(1)}, bf16[1024,2048]{1,0:T(8,128)(2,1)S(...) custom-call(bf16[544,512]{1,0:T(8,128)(2,1)S(1)} %collective-permute, ...), custom_call_target="tpu_custom_call", output_to_operand_aliasing={{0}: (3, {}), {1}: (4, {}), {2}: (5, {}), {3}: (6, {}), {4}... | custom-call | flops 2147483648 | bytes 2097152 | tf_op jit(solution)/shard_map/part/pallas_call | solution.py:189
  55.2 9.2 %collective-permute-start.11 = (f32[1024,512]{1,0:T(8,128)S(1)}, f32[1024,512]{1,0:T(8,128)S(1)}, u32[]{:S(2)}, u32[]{:S(2)}) collective-permute-start(f32[1024,512]{1,0:T(8,128)S(1)} %get-tuple-element.94), channel_id=1, source_target_pairs={{0,2},{2,0},{4,6},{6,4},{8,10},{10,8},{12,14},{14,12},{16,18},{18,... | collective-permute-start | bytes 6291464 | tf_op jit(solution)/shard_map/ppermute | solution.py:435
  66.0 2.5 %grad.1.refs_0_ = f32[1024,512]{1,0:T(8,128)S(1)} custom-call(bf16[1024,2048]{1,0:T(8,128)(2,1)S(1)} %get-tuple-element.106.resid_ref.refs_0_, bf16[2048,512]{1,0:T(8,128)(2,1)S(1)} %get-tuple-element.96.q_ref.refs_1_.q), custom_call_target="tpu_custom_call" | custom-call | flops 2147483648 | bytes 8388608 | tf_op jit(solution)/shard_map/grad/pallas_call | solution.py:372
  68.8 1.8 %adamw.2 = (f32[1024,512]{1,0:T(8,128)S(1)}, f32[1024,512]{1,0:T(8,128)S(1)}, f32[1024,512]{1,0:T(8,128)S(1)}, bf16[1024,512]{1,0:T(8,128)(2,1)S(1)}) custom-call(f32[1024,512]{1,0:T(8,128)S(1)} %grad.1.refs_0_, f32[1024,512]{1,0:T(8,128)S(1)} %collective-permute-done.11.refs_1_, f32[1024,512]{1,0:T(8,128)S(1)} %copy-done, f32[1024,512]{1,0:T(8,128)S(1)} %copy-done.1, ...), custom_call_target="tpu_custom_call" | custom-call | flops 10485760 | bytes 6291456 | tf_op jit(solution)/shard_map/adamw/pallas_call | solution.py:408
  70.7 2.0 %collective-permute-start.12 = (bf16[512,512]{1,0:T(8,128)(2,1)S(1)}, bf16[512,512]{1,0:T(8,128)(2,1)S(1)}, u32[]{:S(2)}, u32[]{:S(2)}) collective-permute-start(bf16[512,512]{1,0:T(8,128)(2,1)S(1)} %terms.2), channel_id=1, source_target_pairs={{0,32},{2,35},{4,36},{6,39},{8,40},{10,43},{12,44},{14,47},{16,48}... | collective-permute-start | bytes 1572872 | tf_op jit(solution)/shard_map/ppermute | solution.py:435
  74.3 3.5 %plane.2 = (bf16[1024,2048]{1,0:T(8,128)(2,1)S(1)}, bf16[1024,2048]{1,0:T(8,128)(2,1)S(1)}, bf16[512,512]{1,0:T(8,128)(2,1)S(1)}) custom-call(f32[8,128]{1,0:T(8,128)S(1)} %get-tuple-element.103.refs_0_.most, bf16[2048,512]{1,0:T(8,128)(2,1)S(1)} %get-tuple-element.96.q_ref.refs_1_.q, s32[2,8,2048]{2,1,0:T(8,128)S(1)} %get-tuple-element.104.refs_2_.pos, ...), custom_call_target="tpu_custom_call" | custom-call | flops 2147483648 | bytes 4194304 | tf_op jit(solution)/shard_map/plane/pallas_call | solution.py:313
  77.9 2.6 %collective-permute-start.15 = (bf16[256,512]{1,0:T(8,128)(2,1)S(1)}, bf16[256,512]{1,0:T(8,128)(2,1)S(1)}, u32[]{:S(2)}, u32[]{:S(2)}) collective-permute-start(bf16[256,512]{1,0:T(8,128)(2,1)S(1)} %get-tuple-element.157), channel_id=1, source_target_pairs={{0,96},{2,227},{4,100},{6,231},{8,104},{10,235},{12,108},{14,239},... | collective-permute-start | bytes 786440 | tf_op jit(solution)/shard_map/ppermute | solution.py:435
  82.1 3.5 %plane.3 = (bf16[1024,2048]{1,0:T(8,128)(2,1)S(1)}, bf16[1024,2048]{1,0:T(8,128)(2,1)S(1)}, f32[512,512]{1,0:T(8,128)S(1)}) custom-call(f32[8,128]{1,0:T(8,128)S(1)} %get-tuple-element.103.refs_0_.most, bf16[2048,512]{1,0:T(8,128)(2,1)S(1)} %get-tuple-element.96.q_ref.refs_1_.q, ...), custom_call_target="tpu_custom_call", output_to_operand_aliasing={{0}: (5, {}), {1}: (6, {})} | custom-call | flops 2147483648 | bytes 4194304 | tf_op jit(solution)/shard_map/plane/pallas_call | solution.py:313
  86.9 1.8 %collective-permute-start.17 = (bf16[256,512]{1,0:T(8,128)(2,1)S(1)}, bf16[256,512]{1,0:T(8,128)(2,1)S(1)}, u32[]{:S(2)}, u32[]{:S(2)}) collective-permute-start(bf16[256,512]{1,0:T(8,128)(2,1)S(1)} %slice.104), channel_id=1, source_target_pairs={{0,64},{2,194},{4,68},{6,198},{8,72},{10,202},{12,76},{14,206},{16... | collective-permute-start | bytes 786440 | tf_op jit(solution)/shard_map/ppermute | solution.py:435
  88.6 4.5 %rest.2 = (bf16[1024,2048]{1,0:T(8,128)(2,1)S(1)}, f32[1024,512]{1,0:T(8,128)S(1)}) custom-call(f32[8,128]{1,0:T(8,128)S(1)} %get-tuple-element.103.refs_0_.most, bf16[2048,512]{1,0:T(8,128)(2,1)S(1)} %get-tuple-element.96.q_ref.refs_1_.q, s32[2,8,2048]{2,1,0:T(8,128)S(1)} %get-tuple-element.104.refs_2_.pos, ...), custom_call_target="tpu_custom_call", output_to_operand_aliasing={{0}: (4, {})} | custom-call | flops 3221225472 | bytes 8388608 | tf_op jit(solution)/shard_map/rest/pallas_call | solution.py:355
  93.2 2.0 %collective-permute-done.17 = bf16[256,512]{1,0:T(8,128)(2,1)S(1)} collective-permute-done((bf16[256,512]{1,0:T(8,128)(2,1)S(1)}, bf16[256,512]{1,0:T(8,128)(2,1)S(1)}, u32[]{:S(2)}, u32[]{:S(2)}) %collective-permute-start.17) | collective-permute-done | bytes 262176 | tf_op jit(solution)/shard_map/ppermute | solution.py:435
  95.9 2.7 %collective-permute-start.19 = (bf16[4,2,16,512]{3,2,1,0:T(8,128)(2,1)S(1)}, bf16[4,2,16,512]{3,2,1,0:T(8,128)(2,1)S(1)}, u32[]{:S(2)}, u32[]{:S(2)}) collective-permute-start(bf16[4,2,16,512]{3,2,1,0:T(8,128)(2,1)S(1)} %get-tuple-element.155), channel_id=1, source_target_pairs={{0,24},{2,10},{4,28},{6,14},{8,0},{10,18},{12,4},{14,22},{16,8},{1... | collective-permute-start | bytes 393224 | tf_op jit(solution)/shard_map/ppermute | solution.py:435
  98.7 3.8 %collective-permute-start.18 = (bf16[4,2,16,512]{3,2,1,0:T(8,128)(2,1)S(1)}, bf16[4,2,16,512]{3,2,1,0:T(8,128)(2,1)S(1)}, u32[]{:S(2)}, u32[]{:S(2)}) collective-permute-start(bf16[4,2,16,512]{3,2,1,0:T(8,128)(2,1)S(1)} %get-tuple-element.156), channel_id=1, source_target_pairs={{0,192},{2,66},{4,196},{6,70},{8,200},{10,74},{12,204},{14,78},{16... | collective-permute-start | bytes 393224 | tf_op jit(solution)/shard_map/ppermute | solution.py:435
  102.5 4.5 %rest.3 = (bf16[1024,2048]{1,0:T(8,128)(2,1)S(1)}, f32[1024,512]{1,0:T(8,128)S(1)}) custom-call(f32[8,128]{1,0:T(8,128)S(1)} %get-tuple-element.103.refs_0_.most, bf16[2048,512]{1,0:T(8,128)(2,1)S(1)} %get-tuple-element.96.q_ref.refs_1_.q, s32[2,8,2048]{2,1,0:T(8,128)S(1)} %get-tuple-element.104.refs_2_.pos, ...), custom_call_target="tpu_custom_call", output_to_operand_aliasing={{0}: (4, {})} | custom-call | flops 3221225472 | bytes 8388608 | tf_op jit(solution)/shard_map/rest/pallas_call | solution.py:355
  107.9 3.6 %collective-permute-start.21 = (f32[2,16,512]{2,1,0:T(8,128)S(1)}, f32[2,16,512]{2,1,0:T(8,128)S(1)}, u32[]{:S(2)}, u32[]{:S(2)}) collective-permute-start(f32[2,16,512]{2,1,0:T(8,128)S(1)} %get-tuple-element.161), channel_id=1, source_target_pairs={{0,30},{2,4},{4,2},{6,8},{8,6},{10,12},{12,10},{14,16},{16,14},{18... | collective-permute-start | bytes 196616 | tf_op jit(solution)/shard_map/ppermute | solution.py:435
  111.5 3.6 %adamw.3 = (f32[1024,512]{1,0:T(8,128)}, f32[1024,512]{1,0:T(8,128)}, f32[1024,512]{1,0:T(8,128)}) custom-call(f32[1024,512]{1,0:T(8,128)S(1)} %get-tuple-element.139.refs_0_, f32[1024,512]{1,0:T(8,128)S(1)} %collective-permute-done.24.refs_1_, f32[1024,512]{1,0:T(8,128)S(1)} %get-tuple-element.141.refs_2_, f32[1024,512]{1,0:T(8,128)S(1)} %get-tuple-element.142.refs_3_, ...), custom_call_target="tpu_custom_call" | custom-call | flops 10485760 | bytes 6291456 | tf_op jit(solution)/shard_map/adamw/pallas_call | solution.py:408
  (64 shorter events, 16.9 us)
Async XLA Ops:
  0.6 0.7 copy-start.3
  1.3 0.7 copy-start.4
  2.4 9.5 %collective-permute-start.2 = (bf16[16,640]{0,1:T(8,128)(2,1)S(1)}, bf16[16,640]{0,1:T(8,128)(2,1)S(1)}, u32[]{:S(2)}, u32[]{:S(2)}) collective-permute-start(bf16[16,640]{0,1:T(8,128)(2,1)S(1)} %copy.32), channel_id=1, source_target_pairs={{0,26},{2,8},{4,30},{6,12},{8,2},{10,16},{12,6},{14,20},{16,10},{1... | collective-permute-start | bytes 61448 | tf_op jit(solution)/shard_map/ppermute | solution.py:435
  6.9 6.8 %collective-permute-start.1 = (bf16[16,640]{0,1:T(8,128)(2,1)S(1)}, bf16[16,640]{0,1:T(8,128)(2,1)S(1)}, u32[]{:S(2)}, u32[]{:S(2)}) collective-permute-start(bf16[16,640]{0,1:T(8,128)(2,1)S(1)} %copy.32), channel_id=1, source_target_pairs={{0,4},{2,30},{4,8},{6,2},{8,12},{10,6},{12,16},{14,10},{16,20},{18... | collective-permute-start | bytes 61448 | tf_op jit(solution)/shard_map/ppermute | solution.py:435
  9.0 6.5 %collective-permute-start = (bf16[16,640]{0,1:T(8,128)(2,1)S(1)}, bf16[16,640]{0,1:T(8,128)(2,1)S(1)}, u32[]{:S(2)}, u32[]{:S(2)}) collective-permute-start(bf16[16,640]{0,1:T(8,128)(2,1)S(1)} %copy.32), channel_id=1, source_target_pairs={{0,30},{2,4},{4,2},{6,8},{8,6},{10,12},{12,10},{14,16},{16,14},{18... | collective-permute-start | bytes 61448 | tf_op jit(solution)/shard_map/ppermute | solution.py:435
  15.7 7.4 %collective-permute-start.3 = (bf16[64,640]{0,1:T(8,128)(2,1)S(1)}, bf16[64,640]{0,1:T(8,128)(2,1)S(1)}, u32[]{:S(2)}, u32[]{:S(2)}) collective-permute-start(bf16[64,640]{0,1:T(8,128)(2,1)S(1)} %pad_maximum_fusion.1), channel_id=1, source_target_pairs={{0,8},{2,26},{4,12},{6,30},{8,16},{10,2},{12,20},{14,6},{16,24},{1... | collective-permute-start | bytes 245768 | tf_op jit(solution)/shard_map/ppermute | solution.py:435
  20.9 14.6 %collective-permute-start.8 = (bf16[1024,512]{1,0:T(8,128)(2,1)S(1)}, bf16[1024,512]{1,0:T(8,128)(2,1)S(1)}, u32[]{:S(2)}, u32[]{:S(2)}) collective-permute-start(bf16[1024,512]{1,0:T(8,128)(2,1)S(1)} %convert_element_type.34.refs_1_.refs_2_), channel_id=1, source_target_pairs={{0,2},{2,0},{4,6},{6,4},{8,10},{10,8},{12,14},{14,12},{16,18},{18,... | collective-permute-start | bytes 3145736 | tf_op jit(solution)/shard_map/ppermute | solution.py:435
  23.6 5.5 %collective-permute-start.6 = (bf16[136,512]{1,0:T(8,128)(2,1)S(1)}, bf16[136,512]{1,0:T(8,128)(2,1)S(1)}, u32[]{:S(2)}, u32[]{:S(2)}) collective-permute-start(bf16[136,512]{1,0:T(8,128)(2,1)S(1)} %pad_maximum_fusion.2.refs_0_), channel_id=1, source_target_pairs={{0,128},{2,3},{4,132},{6,7},{8,136},{10,11},{12,140},{14,15},{16,1... | collective-permute-start | bytes 417800 | tf_op jit(solution)/shard_map/ppermute | solution.py:435
  26.6 5.1 %collective-permute-start.5 = (bf16[136,512]{1,0:T(8,128)(2,1)S(1)}, bf16[136,512]{1,0:T(8,128)(2,1)S(1)}, u32[]{:S(2)}, u32[]{:S(2)}) collective-permute-start(bf16[136,512]{1,0:T(8,128)(2,1)S(1)} %pad_maximum_fusion.2.refs_0_), channel_id=1, source_target_pairs={{0,192},{2,35},{4,196},{6,39},{8,200},{10,43},{12,204},{14,47},{16... | collective-permute-start | bytes 417800 | tf_op jit(solution)/shard_map/ppermute | solution.py:435
  27.4 4.3 %collective-permute-start.4 = (bf16[136,512]{1,0:T(8,128)(2,1)S(1)}, bf16[136,512]{1,0:T(8,128)(2,1)S(1)}, u32[]{:S(2)}, u32[]{:S(2)}) collective-permute-start(bf16[136,512]{1,0:T(8,128)(2,1)S(1)} %pad_maximum_fusion.2.refs_0_), channel_id=1, source_target_pairs={{0,64},{2,34},{4,68},{6,38},{8,72},{10,42},{12,76},{14,46},{16,80}... | collective-permute-start | bytes 417800 | tf_op jit(solution)/shard_map/ppermute | solution.py:435
  31.8 10.3 %collective-permute-start.10 = (bf16[544,512]{1,0:T(8,128)(2,1)S(1)}, bf16[544,512]{1,0:T(8,128)(2,1)S(1)}, u32[]{:S(2)}, u32[]{:S(2)}) collective-permute-start(bf16[544,512]{1,0:T(8,128)(2,1)S(1)} %pack.1.refs_0_), channel_id=1, source_target_pairs={{0,32},{2,66},{4,36},{6,70},{8,40},{10,74},{12,44},{14,78},{16,48}... | collective-permute-start | bytes 1671176 | tf_op jit(solution)/shard_map/ppermute | solution.py:435
  33.0 14.3 %collective-permute-start.9 = (bf16[544,512]{1,0:T(8,128)(2,1)S(1)}, bf16[544,512]{1,0:T(8,128)(2,1)S(1)}, u32[]{:S(2)}, u32[]{:S(2)}) collective-permute-start(bf16[544,512]{1,0:T(8,128)(2,1)S(1)} %pack.1.refs_0_), channel_id=1, source_target_pairs={{0,33},{2,194},{4,37},{6,198},{8,41},{10,202},{12,45},{14,206},{16... | collective-permute-start | bytes 1671176 | tf_op jit(solution)/shard_map/ppermute | solution.py:435
  34.9 15.1 %collective-permute-start.7 = (bf16[544,512]{1,0:T(8,128)(2,1)S(1)}, bf16[544,512]{1,0:T(8,128)(2,1)S(1)}, u32[]{:S(2)}, u32[]{:S(2)}) collective-permute-start(bf16[544,512]{1,0:T(8,128)(2,1)S(1)} %pack.1.refs_0_), channel_id=1, source_target_pairs={{0,1},{2,130},{4,5},{6,134},{8,9},{10,138},{12,13},{14,142},{16,17... | collective-permute-start | bytes 1671176 | tf_op jit(solution)/shard_map/ppermute | solution.py:435
  55.2 13.3 %collective-permute-start.11 = (f32[1024,512]{1,0:T(8,128)S(1)}, f32[1024,512]{1,0:T(8,128)S(1)}, u32[]{:S(2)}, u32[]{:S(2)}) collective-permute-start(f32[1024,512]{1,0:T(8,128)S(1)} %get-tuple-element.94), channel_id=1, source_target_pairs={{0,2},{2,0},{4,6},{6,4},{8,10},{10,8},{12,14},{14,12},{16,18},{18,... | collective-permute-start | bytes 6291464 | tf_op jit(solution)/shard_map/ppermute | solution.py:435
  66.0 2.5 %copy-start = (f32[1024,512]{1,0:T(8,128)S(1)}, f32[1024,512]{1,0:T(8,128)}, u32[]{:S(2)}) copy-start(f32[1024,512]{1,0:T(8,128)} %refs_2_.1) | copy-start | bytes 6291460
  66.0 2.5 %copy-start.1 = (f32[1024,512]{1,0:T(8,128)S(1)}, f32[1024,512]{1,0:T(8,128)}, u32[]{:S(2)}) copy-start(f32[1024,512]{1,0:T(8,128)} %refs_3_.1) | copy-start | bytes 6291460
  66.0 2.8 %copy-start.2 = (f32[1024,512]{1,0:T(8,128)S(1)}, f32[1024,512]{1,0:T(8,128)}, u32[]{:S(2)}) copy-start(f32[1024,512]{1,0:T(8,128)} %refs_4_.1) | copy-start | bytes 6291460
  70.6 3.7 %collective-permute-start.13 = (bf16[1024,512]{1,0:T(8,128)(2,1)S(1)}, bf16[1024,512]{1,0:T(8,128)(2,1)S(1)}, u32[]{:S(2)}, u32[]{:S(2)}) collective-permute-start(bf16[1024,512]{1,0:T(8,128)(2,1)S(1)} %get-tuple-element.105.refs_3_.wb), channel_id=1, source_target_pairs={{0,2},{2,0},{4,6},{6,4},{8,10},{10,8},{12,14},{14,12},{16,18},{18,... | collective-permute-start | bytes 3145736 | tf_op jit(solution)/shard_map/ppermute | solution.py:435
  70.7 14.9 %collective-permute-start.12 = (bf16[512,512]{1,0:T(8,128)(2,1)S(1)}, bf16[512,512]{1,0:T(8,128)(2,1)S(1)}, u32[]{:S(2)}, u32[]{:S(2)}) collective-permute-start(bf16[512,512]{1,0:T(8,128)(2,1)S(1)} %terms.2), channel_id=1, source_target_pairs={{0,32},{2,35},{4,36},{6,39},{8,40},{10,43},{12,44},{14,47},{16,48}... | collective-permute-start | bytes 1572872 | tf_op jit(solution)/shard_map/ppermute | solution.py:435
  77.9 15.3 %collective-permute-start.15 = (bf16[256,512]{1,0:T(8,128)(2,1)S(1)}, bf16[256,512]{1,0:T(8,128)(2,1)S(1)}, u32[]{:S(2)}, u32[]{:S(2)}) collective-permute-start(bf16[256,512]{1,0:T(8,128)(2,1)S(1)} %get-tuple-element.157), channel_id=1, source_target_pairs={{0,96},{2,227},{4,100},{6,231},{8,104},{10,235},{12,108},{14,239},... | collective-permute-start | bytes 786440 | tf_op jit(solution)/shard_map/ppermute | solution.py:435
  80.4 12.7 %collective-permute-start.14 = (bf16[256,512]{1,0:T(8,128)(2,1)S(1)}, bf16[256,512]{1,0:T(8,128)(2,1)S(1)}, u32[]{:S(2)}, u32[]{:S(2)}) collective-permute-start(bf16[256,512]{1,0:T(8,128)(2,1)S(1)} %get-tuple-element.158), channel_id=1, source_target_pairs={{0,32},{2,35},{4,36},{6,39},{8,40},{10,43},{12,44},{14,47},{16,48}... | collective-permute-start | bytes 786440 | tf_op jit(solution)/shard_map/ppermute | solution.py:435
  85.9 7.3 %collective-permute-start.16 = (bf16[256,512]{1,0:T(8,128)(2,1)S(1)}, bf16[256,512]{1,0:T(8,128)(2,1)S(1)}, u32[]{:S(2)}, u32[]{:S(2)}) collective-permute-start(bf16[256,512]{1,0:T(8,128)(2,1)S(1)} %slice.105), channel_id=1, source_target_pairs={{0,64},{2,194},{4,68},{6,198},{8,72},{10,202},{12,76},{14,206},{16... | collective-permute-start | bytes 786440 | tf_op jit(solution)/shard_map/ppermute | solution.py:435
  86.9 8.3 %collective-permute-start.17 = (bf16[256,512]{1,0:T(8,128)(2,1)S(1)}, bf16[256,512]{1,0:T(8,128)(2,1)S(1)}, u32[]{:S(2)}, u32[]{:S(2)}) collective-permute-start(bf16[256,512]{1,0:T(8,128)(2,1)S(1)} %slice.104), channel_id=1, source_target_pairs={{0,64},{2,194},{4,68},{6,198},{8,72},{10,202},{12,76},{14,206},{16... | collective-permute-start | bytes 786440 | tf_op jit(solution)/shard_map/ppermute | solution.py:435
  95.2 16.3 %collective-permute-start.24 = (f32[1024,512]{1,0:T(8,128)S(1)}, f32[1024,512]{1,0:T(8,128)S(1)}, u32[]{:S(2)}, u32[]{:S(2)}) collective-permute-start(f32[1024,512]{1,0:T(8,128)S(1)} %get-tuple-element.140), channel_id=1, source_target_pairs={{0,2},{2,0},{4,6},{6,4},{8,10},{10,8},{12,14},{14,12},{16,18},{18,... | collective-permute-start | bytes 6291464 | tf_op jit(solution)/shard_map/ppermute | solution.py:435
  95.6 11.4 %collective-permute-start.20 = (bf16[4,2,16,512]{3,2,1,0:T(8,128)(2,1)S(1)}, bf16[4,2,16,512]{3,2,1,0:T(8,128)(2,1)S(1)}, u32[]{:S(2)}, u32[]{:S(2)}) collective-permute-start(bf16[4,2,16,512]{3,2,1,0:T(8,128)(2,1)S(1)} %get-tuple-element.154), channel_id=1, source_target_pairs={{0,216},{2,74},{4,220},{6,78},{8,192},{10,82},{12,196},{14,86},{16... | collective-permute-start | bytes 393224 | tf_op jit(solution)/shard_map/ppermute | solution.py:435
  95.9 11.1 %collective-permute-start.19 = (bf16[4,2,16,512]{3,2,1,0:T(8,128)(2,1)S(1)}, bf16[4,2,16,512]{3,2,1,0:T(8,128)(2,1)S(1)}, u32[]{:S(2)}, u32[]{:S(2)}) collective-permute-start(bf16[4,2,16,512]{3,2,1,0:T(8,128)(2,1)S(1)} %get-tuple-element.155), channel_id=1, source_target_pairs={{0,24},{2,10},{4,28},{6,14},{8,0},{10,18},{12,4},{14,22},{16,8},{1... | collective-permute-start | bytes 393224 | tf_op jit(solution)/shard_map/ppermute | solution.py:435
  98.7 8.4 %collective-permute-start.18 = (bf16[4,2,16,512]{3,2,1,0:T(8,128)(2,1)S(1)}, bf16[4,2,16,512]{3,2,1,0:T(8,128)(2,1)S(1)}, u32[]{:S(2)}, u32[]{:S(2)}) collective-permute-start(bf16[4,2,16,512]{3,2,1,0:T(8,128)(2,1)S(1)} %get-tuple-element.156), channel_id=1, source_target_pairs={{0,192},{2,66},{4,196},{6,70},{8,200},{10,74},{12,204},{14,78},{16... | collective-permute-start | bytes 393224 | tf_op jit(solution)/shard_map/ppermute | solution.py:435
  107.2 8.0 %collective-permute-start.23 = (f32[2,16,512]{2,1,0:T(8,128)S(1)}, f32[2,16,512]{2,1,0:T(8,128)S(1)}, u32[]{:S(2)}, u32[]{:S(2)}) collective-permute-start(f32[2,16,512]{2,1,0:T(8,128)S(1)} %get-tuple-element.159), channel_id=1, source_target_pairs={{0,26},{2,8},{4,30},{6,12},{8,2},{10,16},{12,6},{14,20},{16,10},{1... | collective-permute-start | bytes 196616 | tf_op jit(solution)/shard_map/ppermute | solution.py:435
  107.9 7.2 %collective-permute-start.22 = (f32[2,16,512]{2,1,0:T(8,128)S(1)}, f32[2,16,512]{2,1,0:T(8,128)S(1)}, u32[]{:S(2)}, u32[]{:S(2)}) collective-permute-start(f32[2,16,512]{2,1,0:T(8,128)S(1)} %get-tuple-element.160), channel_id=1, source_target_pairs={{0,28},{2,6},{4,0},{6,10},{8,4},{10,14},{12,8},{14,18},{16,12},{18... | collective-permute-start | bytes 196616 | tf_op jit(solution)/shard_map/ppermute | solution.py:435
  107.9 7.2 %collective-permute-start.21 = (f32[2,16,512]{2,1,0:T(8,128)S(1)}, f32[2,16,512]{2,1,0:T(8,128)S(1)}, u32[]{:S(2)}, u32[]{:S(2)}) collective-permute-start(f32[2,16,512]{2,1,0:T(8,128)S(1)} %get-tuple-element.161), channel_id=1, source_target_pairs={{0,30},{2,4},{4,2},{6,8},{8,6},{10,12},{12,10},{14,16},{16,14},{18... | collective-permute-start | bytes 196616 | tf_op jit(solution)/shard_map/ppermute | solution.py:435

commit v2 on v1

--- a/solution.py
+++ b/solution.py
@@ -115,9 +115,8 @@
 
 
 def fill_grad(resid_ref, q_ref, out_ref):
-    @pl.loop(0, LAB // (2 * TILE))
-    def _(t):
-        rows = pl.ds(pl.multiple_of(2 * TILE * t, 2 * TILE), 2 * TILE)
+    for t in range(LAB // (2 * TILE)):
+        rows = slice(2 * TILE * t, 2 * TILE * (t + 1))
         out_ref[rows, :] = jnp.dot(resid_ref[rows, :], q_ref[...], preferred_element_type=f32)
 
 
@@ -389,32 +388,47 @@
     return weight, first, second
 
 
-def adamw_kernel(count, one, two, w_ref, m_ref, v_ref, w_out, m_out, v_out, *wb_out):
-    @pl.loop(0, one.shape[0] // 64)
+def fill_update(count, ins, outs, start, size):
+    @pl.loop(0, size // 64)
     def _(t):
-        rows = pl.ds(pl.multiple_of(t * 64, 64), 64)
-        grad = one[rows, :] + two[rows, :]
-        weight, first, second = adamw(count, grad, w_ref[rows, :], m_ref[rows, :], v_ref[rows, :])
-        w_out[rows, :] = weight
-        m_out[rows, :] = first
-        v_out[rows, :] = second
-        if wb_out:
-            wb_out[0][rows, :] = weight.astype(bf16)
-
-
-def update(count, last, one, two, weight, first, second):
+        rows = pl.ds(pl.multiple_of(start + t * 64, 64), 64)
+        one, two, weight, first, second = (ref[rows, :] for ref in ins)
+        new = adamw(count, one + two, weight, first, second)
+        for ref, value in zip(outs, new + new[:1]):
+            ref[rows, :] = value.astype(ref.dtype)
+
+
+def adamw_kernel(count, *refs):
+    fill_update(count, refs[:5], refs[5:], 0, LAB)
+
+
+def last_adamw_kernel(count, *refs):
+    ins, outs, held, sems = refs[:5], refs[5:8], refs[8:11], refs[11]
+    copies = []
+    for i in range(LAB // TILE):
+        fill_update(count, ins, held, i * TILE, TILE)
+        rows = slice(i * TILE, (i + 1) * TILE)
+        for k in range(3):
+            copies.append(pltpu.make_async_copy(held[k].at[rows], outs[k].at[rows], sems.at[i, k]))
+            copies[-1].start()
+    for copy in copies:
+        copy.wait()
+
+
+def update(count, last, *arrays):
     full = jax.ShapeDtypeStruct((LAB, D), f32)
-    tile = spec((TILE, D), lambda i: (i, 0)) if last else spec()
-    return pl.pallas_call(
-        lambda *refs: adamw_kernel(count, *refs),
-        grid=(LAB // TILE,) if last else (),
+    kernel = last_adamw_kernel if last else adamw_kernel
+    held = [pltpu.VMEM((LAB, D), f32)] * 3 + [pltpu.SemaphoreType.DMA((LAB // TILE, 3))]
+    return pl.pallas_call(
+        lambda *refs: kernel(count, *refs),
         out_shape=(full, full, full) + (() if last else (jax.ShapeDtypeStruct((LAB, D), bf16),)),
-        in_specs=[tile] * 5,
-        out_specs=(tile,) * (3 if last else 4),
+        in_specs=[spec()] * 5,
+        out_specs=(spec(space=pl.ANY),) * 3 if last else (spec(),) * 4,
+        scratch_shapes=held if last else [],
         compiler_params=params(),
         cost_estimate=cost(20 * LAB * D, 12 * LAB * D, 2 * LAB * D),
         name="adamw",
-    )(one, two, weight, first, second)
+    )(*arrays)
 
 
 def moved(move):
@@ -478,7 +492,7 @@
     chip = jnp.concatenate([line[:, :D], coded], axis=0)
     four = [chip] + [send(chip, by_core(along_x(by), along_y(by))) for by in (1, 3, 2)]
     four = pack(four)
-    return [four] + [send(four, by_core(along_y(by), along_x(by))) for by in (1, 3, 2)]
+    return four
 
 
 def after(array, *others):
@@ -493,10 +507,14 @@
 
     wb = weight.astype(bf16)
     wb_other = swap(wb)
-    state = ()
-    for late, part in zip((0, 1, 3, LAST), gather(queries, positives)):
-        *state, theirs = (*first_residuals(part, wb, wb_other, late, state[:5]), None)[:6]
-    q, pos, own, other, most = state
+    four = gather(queries, positives)
+    near = [send(four, by_core(along_y(by), along_x(by))) for by in (1, 3)]
+    state = first_residuals(four, wb, wb_other, 0, ())
+    far, *state = after(four, *state)
+    far = send(far, by_core(along_y(LAST), along_x(LAST)))
+    for late, part in zip((1, 3), near):
+        state = first_residuals(part, wb, wb_other, late, state)
+    q, pos, own, other, most, theirs = first_residuals(far, wb, wb_other, LAST, state)
     step0 = (own, other, wb, wb_other)
 
     part = swap(theirs)

time: 116 us -> 114 us (0.983)
  transfers between devices with their start and end apart: 25 -> 25, of which waited for: 9 -> 8; matrix products, arithmetic and copies ran while one was open for 3% -> 3% of each run, Pallas kernels for 28% -> 28%
where the time goes in v2:
time: 114 us
  starting transfers between devices  48.1 us (42%)
  Pallas kernels  39.3 us (34%)
  waiting for transfers between devices  19.7 us (17%)
  other arithmetic  3.26 us (3%)
  local copies, waits for them, and re-layouts  2.67 us (2%)
    ppermute x25, starting transfers between devices, send(): return lax.ppermute(array, AXES, moved(move))  48.1 us
    ppermute x25, waiting for transfers between devices, send(): return lax.ppermute(array, AXES, moved(move))  19.7 us
    pallas_call x4, Pallas kernels, first_residuals(): pl.pallas_call(lambda *refs: part_kernel(*refs, late=late), out_shape=sha...  12.9 us
    pallas_call x2, Pallas kernels, rest_gradient(): pl.pallas_call(lambda most, q, pos, wb, old, resid, out: rest_kernel(most...  8.91 us
    pallas_call x2, Pallas kernels, plane_terms(): pl.pallas_call(lambda *refs: plane_kernel(*refs, blocks=blocks), out_shap...  7.01 us
    pallas_call x2, Pallas kernels, update(): pl.pallas_call(lambda *refs: kernel(count, *refs), out_shape=(full, full,...  4.94 us
    pallas_call x2, Pallas kernels, terms(): pl.pallas_call(lambda *refs: terms_kernel(*refs, blocks=blocks), out_shap...  3.03 us
    pallas_call x1, Pallas kernels, gradient(): pl.pallas_call(grad_kernel, out_shape=jax.ShapeDtypeStruct((LAB, D), f32)...  2.32 us
  transfers between devices with their start and end apart: 25, of which 8 were waited for; matrix products, arithmetic and copies ran while one was open for 3% of the time, Pallas kernels for 28%

profile of v2, /device:TPU:1, one launch (start us, length us, event | category | flops | bytes accessed | tf_op | source)
XLA Modules:
  0.0 114.0 jit_solution(6516680532258671806)
XLA Ops:
  2.4 4.5 %collective-permute-start.2 = (bf16[16,640]{0,1:T(8,128)(2,1)S(1)}, bf16[16,640]{0,1:T(8,128)(2,1)S(1)}, u32[]{:S(2)}, u32[]{:S(2)}) collective-permute-start(bf16[16,640]{0,1:T(8,128)(2,1)S(1)} %copy.32), channel_id=1, source_target_pairs={{0,26},{2,8},{4,30},{6,12},{8,2},{10,16},{12,6},{14,20},{16,10},{1... | collective-permute-start | bytes 61448 | tf_op jit(solution)/shard_map/ppermute | solution.py:449
  6.9 2.1 %collective-permute-start.1 = (bf16[16,640]{0,1:T(8,128)(2,1)S(1)}, bf16[16,640]{0,1:T(8,128)(2,1)S(1)}, u32[]{:S(2)}, u32[]{:S(2)}) collective-permute-start(bf16[16,640]{0,1:T(8,128)(2,1)S(1)} %copy.32), channel_id=1, source_target_pairs={{0,4},{2,30},{4,8},{6,2},{8,12},{10,6},{12,16},{14,10},{16,20},{18... | collective-permute-start | bytes 61448 | tf_op jit(solution)/shard_map/ppermute | solution.py:449
  10.4 1.7 %convert_element_type.34.refs_1_.refs_2_ = bf16[1024,512]{1,0:T(8,128)(2,1)S(1)} convert(f32[1024,512]{1,0:T(8,128)} %refs_2_.1) | non-fusion elementwise | flops 524288 | bytes 3145728 | tf_op jit(solution)/shard_map/convert_element_type | solution.py:508
  13.7 1.8 %collective-permute-done = bf16[16,640]{0,1:T(8,128)(2,1)S(1)} collective-permute-done((bf16[16,640]{0,1:T(8,128)(2,1)S(1)}, bf16[16,640]{0,1:T(8,128)(2,1)S(1)}, u32[]{:S(2)}, u32[]{:S(2)}) %collective-permute-start) | collective-permute-done | bytes 20512 | tf_op jit(solution)/shard_map/ppermute | solution.py:449
  15.7 3.5 %collective-permute-start.3 = (bf16[64,640]{0,1:T(8,128)(2,1)S(1)}, bf16[64,640]{0,1:T(8,128)(2,1)S(1)}, u32[]{:S(2)}, u32[]{:S(2)}) collective-permute-start(bf16[64,640]{0,1:T(8,128)(2,1)S(1)} %pad_maximum_fusion.1), channel_id=1, source_target_pairs={{0,8},{2,26},{4,12},{6,30},{8,16},{10,2},{12,20},{14,6},{16,24},{1... | collective-permute-start | bytes 245768 | tf_op jit(solution)/shard_map/ppermute | solution.py:449
  19.2 3.9 %collective-permute-done.3 = bf16[64,640]{0,1:T(8,128)(2,1)S(1)} collective-permute-done((bf16[64,640]{0,1:T(8,128)(2,1)S(1)}, bf16[64,640]{0,1:T(8,128)(2,1)S(1)}, u32[]{:S(2)}, u32[]{:S(2)}) %collective-permute-start.3) | collective-permute-done | bytes 81952 | tf_op jit(solution)/shard_map/ppermute | solution.py:449
  23.6 3.0 %collective-permute-start.6 = (bf16[136,512]{1,0:T(8,128)(2,1)S(1)}, bf16[136,512]{1,0:T(8,128)(2,1)S(1)}, u32[]{:S(2)}, u32[]{:S(2)}) collective-permute-start(bf16[136,512]{1,0:T(8,128)(2,1)S(1)} %pad_maximum_fusion.2.refs_0_), channel_id=1, source_target_pairs={{0,128},{2,3},{4,132},{6,7},{8,136},{10,11},{12,140},{14,15},{16,1... | collective-permute-start | bytes 417800 | tf_op jit(solution)/shard_map/ppermute | solution.py:449
  27.4 1.7 %collective-permute-done.6.refs_3_ = bf16[136,512]{1,0:T(8,128)(2,1)S(1)} collective-permute-done((bf16[136,512]{1,0:T(8,128)(2,1)S(1)}, bf16[136,512]{1,0:T(8,128)(2,1)S(1)}, u32[]{:S(2)}, u32[]{:S(2)}) %collective-permute-start.6) | collective-permute-done | bytes 139296 | tf_op jit(solution)/shard_map/ppermute | solution.py:449
  29.1 2.6 %collective-permute-done.5.refs_2_ = bf16[136,512]{1,0:T(8,128)(2,1)S(1)} collective-permute-done((bf16[136,512]{1,0:T(8,128)(2,1)S(1)}, bf16[136,512]{1,0:T(8,128)(2,1)S(1)}, u32[]{:S(2)}, u32[]{:S(2)}) %collective-permute-start.5) | collective-permute-done | bytes 139296 | tf_op jit(solution)/shard_map/ppermute | solution.py:449
  33.0 1.8 %collective-permute-start.9 = (bf16[544,512]{1,0:T(8,128)(2,1)S(1)}, bf16[544,512]{1,0:T(8,128)(2,1)S(1)}, u32[]{:S(2)}, u32[]{:S(2)}) collective-permute-start(bf16[544,512]{1,0:T(8,128)(2,1)S(1)} %pack.1.refs_0_), channel_id=1, source_target_pairs={{0,33},{2,194},{4,37},{6,198},{8,41},{10,202},{12,45},{14,206},{16... | collective-permute-start | bytes 1671176 | tf_op jit(solution)/shard_map/ppermute | solution.py:449
  34.9 2.6 %part.4 = (bf16[2048,512]{1,0:T(8,128)(2,1)S(1)}, s32[2,8,2048]{2,1,0:T(8,128)S(1)}, bf16[1024,2048]{1,0:T(8,128)(2,1)S(1)}, bf16[1024,2048]{1,0:T(8,128)(2,1)S(1)}, f32[8,128]{1,0:T(8,128)S(1)}) custom-call(bf16[544,512]{1,0:T(8,128)(2,1)S(1)} %pack.1.refs_0_, bf16[1024,512]{1,0:T(8,128)(2,1)S(1)} %convert_element_type.34.refs_1_.refs_2_, ...), custom_call_target="tpu_custom_call" | custom-call | flops 1073741824 | bytes 2097152 | tf_op jit(solution)/shard_map/part/pallas_call | solution.py:188
  38.2 3.8 %collective-permute-done.10.refs_0_ = bf16[544,512]{1,0:T(8,128)(2,1)S(1)} collective-permute-done((bf16[544,512]{1,0:T(8,128)(2,1)S(1)}, bf16[544,512]{1,0:T(8,128)(2,1)S(1)}, u32[]{:S(2)}, u32[]{:S(2)}) %collective-permute-start.10) | collective-permute-done | bytes 557088 | tf_op jit(solution)/shard_map/ppermute | solution.py:449
  42.0 2.6 %part.5 = (bf16[2048,512]{1,0:T(8,128)(2,1)S(1)}, s32[2,8,2048]{2,1,0:T(8,128)S(1)}, bf16[1024,2048]{1,0:T(8,128)(2,1)S(1)}, bf16[1024,2048]{1,0:T(8,128)(2,1)S(1)}, f32[8,128]{1,0:T(8,128)S(1)}) custom-call(bf16[544,512]{1,0:T(8,128)(2,1)S(1)} %collective-permute-done.10.refs_0_, ...), custom_call_target="tpu_custom_call", output_to_operand_aliasing={{0}: (3, {}), {1}: (4, {}), {2}: (5, {}), {3}: (6, {}), {4}... | custom-call | flops 1073741824 | bytes 2097152 | tf_op jit(solution)/shard_map/part/pallas_call | solution.py:188
  44.6 2.7 %collective-permute-done.9.refs_0_ = bf16[544,512]{1,0:T(8,128)(2,1)S(1)} collective-permute-done((bf16[544,512]{1,0:T(8,128)(2,1)S(1)}, bf16[544,512]{1,0:T(8,128)(2,1)S(1)}, u32[]{:S(2)}, u32[]{:S(2)}) %collective-permute-start.9) | collective-permute-done | bytes 557088 | tf_op jit(solution)/shard_map/ppermute | solution.py:449
  47.3 2.6 %part.6 = (bf16[2048,512]{1,0:T(8,128)(2,1)S(1)}, s32[2,8,2048]{2,1,0:T(8,128)S(1)}, bf16[1024,2048]{1,0:T(8,128)(2,1)S(1)}, bf16[1024,2048]{1,0:T(8,128)(2,1)S(1)}, f32[8,128]{1,0:T(8,128)S(1)}) custom-call(bf16[544,512]{1,0:T(8,128)(2,1)S(1)} %collective-permute-done.9.refs_0_, ...), custom_call_target="tpu_custom_call", output_to_operand_aliasing={{0}: (3, {}), {1}: (4, {}), {2}: (5, {}), {3}: (6, {}), {4}... | custom-call | flops 1073741824 | bytes 2097152 | tf_op jit(solution)/shard_map/part/pallas_call | solution.py:188
  49.9 5.1 %part.7 = (bf16[2048,512]{1,0:T(8,128)(2,1)S(1)}, s32[2,8,2048]{2,1,0:T(8,128)S(1)}, bf16[1024,2048]{1,0:T(8,128)(2,1)S(1)}, bf16[1024,2048]{1,0:T(8,128)(2,1)S(...) custom-call(bf16[544,512]{1,0:T(8,128)(2,1)S(1)} %collective-permute, ...), custom_call_target="tpu_custom_call", output_to_operand_aliasing={{0}: (3, {}), {1}: (4, {}), {2}: (5, {}), {3}: (6, {}), {4}... | custom-call | flops 2147483648 | bytes 2097152 | tf_op jit(solution)/shard_map/part/pallas_call | solution.py:188
  55.0 9.2 %collective-permute-start.11 = (f32[1024,512]{1,0:T(8,128)S(1)}, f32[1024,512]{1,0:T(8,128)S(1)}, u32[]{:S(2)}, u32[]{:S(2)}) collective-permute-start(f32[1024,512]{1,0:T(8,128)S(1)} %get-tuple-element.106), channel_id=1, source_target_pairs={{0,2},{2,0},{4,6},{6,4},{8,10},{10,8},{12,14},{14,12},{16,18},{18,... | collective-permute-start | bytes 6291464 | tf_op jit(solution)/shard_map/ppermute | solution.py:449
  65.8 2.3 %grad.1.refs_0_ = f32[1024,512]{1,0:T(8,128)S(1)} custom-call(bf16[1024,2048]{1,0:T(8,128)(2,1)S(1)} %get-tuple-element.118.resid_ref.refs_0_, bf16[2048,512]{1,0:T(8,128)(2,1)S(1)} %get-tuple-element.108.q_ref.refs_1_.q), custom_call_target="tpu_custom_call" | custom-call | flops 2147483648 | bytes 8388608 | tf_op jit(solution)/shard_map/grad/pallas_call | solution.py:371
  68.7 1.8 %adamw.2 = (f32[1024,512]{1,0:T(8,128)S(1)}, f32[1024,512]{1,0:T(8,128)S(1)}, f32[1024,512]{1,0:T(8,128)S(1)}, bf16[1024,512]{1,0:T(8,128)(2,1)S(1)}) custom-call(f32[1024,512]{1,0:T(8,128)S(1)} %grad.1.refs_0_, f32[1024,512]{1,0:T(8,128)S(1)} %collective-permute-done.11.refs_1_, f32[1024,512]{1,0:T(8,128)S(1)} %copy-done, f32[1024,512]{1,0:T(8,128)S(1)} %copy-done.1, ...), custom_call_target="tpu_custom_call" | custom-call | flops 10485760 | bytes 6291456 | tf_op jit(solution)/shard_map/adamw/pallas_call | solution.py:422
  70.5 2.0 %collective-permute-start.12 = (bf16[512,512]{1,0:T(8,128)(2,1)S(1)}, bf16[512,512]{1,0:T(8,128)(2,1)S(1)}, u32[]{:S(2)}, u32[]{:S(2)}) collective-permute-start(bf16[512,512]{1,0:T(8,128)(2,1)S(1)} %terms.2), channel_id=1, source_target_pairs={{0,32},{2,35},{4,36},{6,39},{8,40},{10,43},{12,44},{14,47},{16,48}... | collective-permute-start | bytes 1572872 | tf_op jit(solution)/shard_map/ppermute | solution.py:449
  74.1 3.5 %plane.2 = (bf16[1024,2048]{1,0:T(8,128)(2,1)S(1)}, bf16[1024,2048]{1,0:T(8,128)(2,1)S(1)}, bf16[512,512]{1,0:T(8,128)(2,1)S(1)}) custom-call(f32[8,128]{1,0:T(8,128)S(1)} %get-tuple-element.115.refs_0_.most, bf16[2048,512]{1,0:T(8,128)(2,1)S(1)} %get-tuple-element.108.q_ref.refs_1_.q, s32[2,8,2048]{2,1,0:T(8,128)S(1)} %get-tuple-element.116.refs_2_.pos, ...), custom_call_target="tpu_custom_call" | custom-call | flops 2147483648 | bytes 4194304 | tf_op jit(solution)/shard_map/plane/pallas_call | solution.py:312
  77.7 2.6 %collective-permute-start.15 = (bf16[256,512]{1,0:T(8,128)(2,1)S(1)}, bf16[256,512]{1,0:T(8,128)(2,1)S(1)}, u32[]{:S(2)}, u32[]{:S(2)}) collective-permute-start(bf16[256,512]{1,0:T(8,128)(2,1)S(1)} %get-tuple-element.169), channel_id=1, source_target_pairs={{0,96},{2,227},{4,100},{6,231},{8,104},{10,235},{12,108},{14,239},... | collective-permute-start | bytes 786440 | tf_op jit(solution)/shard_map/ppermute | solution.py:449
  80.3 1.7 %collective-permute-start.14 = (bf16[256,512]{1,0:T(8,128)(2,1)S(1)}, bf16[256,512]{1,0:T(8,128)(2,1)S(1)}, u32[]{:S(2)}, u32[]{:S(2)}) collective-permute-start(bf16[256,512]{1,0:T(8,128)(2,1)S(1)} %get-tuple-element.170), channel_id=1, source_target_pairs={{0,32},{2,35},{4,36},{6,39},{8,40},{10,43},{12,44},{14,47},{16,48}... | collective-permute-start | bytes 786440 | tf_op jit(solution)/shard_map/ppermute | solution.py:449
  81.9 3.5 %plane.3 = (bf16[1024,2048]{1,0:T(8,128)(2,1)S(1)}, bf16[1024,2048]{1,0:T(8,128)(2,1)S(1)}, f32[512,512]{1,0:T(8,128)S(1)}) custom-call(f32[8,128]{1,0:T(8,128)S(1)} %get-tuple-element.115.refs_0_.most, bf16[2048,512]{1,0:T(8,128)(2,1)S(1)} %get-tuple-element.108.q_ref.refs_1_.q, ...), custom_call_target="tpu_custom_call", output_to_operand_aliasing={{0}: (5, {}), {1}: (6, {})} | custom-call | flops 2147483648 | bytes 4194304 | tf_op jit(solution)/shard_map/plane/pallas_call | solution.py:312
  86.7 1.8 %collective-permute-start.17 = (bf16[256,512]{1,0:T(8,128)(2,1)S(1)}, bf16[256,512]{1,0:T(8,128)(2,1)S(1)}, u32[]{:S(2)}, u32[]{:S(2)}) collective-permute-start(bf16[256,512]{1,0:T(8,128)(2,1)S(1)} %slice.104), channel_id=1, source_target_pairs={{0,64},{2,194},{4,68},{6,198},{8,72},{10,202},{12,76},{14,206},{16... | collective-permute-start | bytes 786440 | tf_op jit(solution)/shard_map/ppermute | solution.py:449
  88.5 4.6 %rest.2 = (bf16[1024,2048]{1,0:T(8,128)(2,1)S(1)}, f32[1024,512]{1,0:T(8,128)S(1)}) custom-call(f32[8,128]{1,0:T(8,128)S(1)} %get-tuple-element.115.refs_0_.most, bf16[2048,512]{1,0:T(8,128)(2,1)S(1)} %get-tuple-element.108.q_ref.refs_1_.q, s32[2,8,2048]{2,1,0:T(8,128)S(1)} %get-tuple-element.116.refs_2_.pos, ...), custom_call_target="tpu_custom_call", output_to_operand_aliasing={{0}: (4, {})} | custom-call | flops 3221225472 | bytes 8388608 | tf_op jit(solution)/shard_map/rest/pallas_call | solution.py:354
  93.1 2.0 %collective-permute-done.17 = bf16[256,512]{1,0:T(8,128)(2,1)S(1)} collective-permute-done((bf16[256,512]{1,0:T(8,128)(2,1)S(1)}, bf16[256,512]{1,0:T(8,128)(2,1)S(1)}, u32[]{:S(2)}, u32[]{:S(2)}) %collective-permute-start.17) | collective-permute-done | bytes 262176 | tf_op jit(solution)/shard_map/ppermute | solution.py:449
  95.6 2.7 %collective-permute-start.19 = (bf16[4,2,16,512]{3,2,1,0:T(8,128)(2,1)S(1)}, bf16[4,2,16,512]{3,2,1,0:T(8,128)(2,1)S(1)}, u32[]{:S(2)}, u32[]{:S(2)}) collective-permute-start(bf16[4,2,16,512]{3,2,1,0:T(8,128)(2,1)S(1)} %get-tuple-element.167), channel_id=1, source_target_pairs={{0,24},{2,10},{4,28},{6,14},{8,0},{10,18},{12,4},{14,22},{16,8},{1... | collective-permute-start | bytes 393224 | tf_op jit(solution)/shard_map/ppermute | solution.py:449
  98.3 3.0 %collective-permute-start.18 = (bf16[4,2,16,512]{3,2,1,0:T(8,128)(2,1)S(1)}, bf16[4,2,16,512]{3,2,1,0:T(8,128)(2,1)S(1)}, u32[]{:S(2)}, u32[]{:S(2)}) collective-permute-start(bf16[4,2,16,512]{3,2,1,0:T(8,128)(2,1)S(1)} %get-tuple-element.168), channel_id=1, source_target_pairs={{0,192},{2,66},{4,196},{6,70},{8,200},{10,74},{12,204},{14,78},{16... | collective-permute-start | bytes 393224 | tf_op jit(solution)/shard_map/ppermute | solution.py:449
  101.3 4.3 %rest.3 = (bf16[1024,2048]{1,0:T(8,128)(2,1)S(1)}, f32[1024,512]{1,0:T(8,128)S(1)}) custom-call(f32[8,128]{1,0:T(8,128)S(1)} %get-tuple-element.115.refs_0_.most, bf16[2048,512]{1,0:T(8,128)(2,1)S(1)} %get-tuple-element.108.q_ref.refs_1_.q, s32[2,8,2048]{2,1,0:T(8,128)S(1)} %get-tuple-element.116.refs_2_.pos, ...), custom_call_target="tpu_custom_call", output_to_operand_aliasing={{0}: (4, {})} | custom-call | flops 3221225472 | bytes 8388608 | tf_op jit(solution)/shard_map/rest/pallas_call | solution.py:354
  107.0 3.1 %collective-permute-start.21 = (f32[2,16,512]{2,1,0:T(8,128)S(1)}, f32[2,16,512]{2,1,0:T(8,128)S(1)}, u32[]{:S(2)}, u32[]{:S(2)}) collective-permute-start(f32[2,16,512]{2,1,0:T(8,128)S(1)} %get-tuple-element.173), channel_id=1, source_target_pairs={{0,30},{2,4},{4,2},{6,8},{8,6},{10,12},{12,10},{14,16},{16,14},{18... | collective-permute-start | bytes 196616 | tf_op jit(solution)/shard_map/ppermute | solution.py:449
  110.1 3.2 %adamw.3 = (f32[1024,512]{1,0:T(8,128)}, f32[1024,512]{1,0:T(8,128)}, f32[1024,512]{1,0:T(8,128)}) custom-call(f32[1024,512]{1,0:T(8,128)S(1)} %get-tuple-element.151.refs_0_, f32[1024,512]{1,0:T(8,128)S(1)} %collective-permute-done.24.refs_1_, f32[1024,512]{1,0:T(8,128)S(1)} %get-tuple-element.153.refs_2_, f32[1024,512]{1,0:T(8,128)S(1)} %get-tuple-element.154.refs_3_, ...), custom_call_target="tpu_custom_call" | custom-call | flops 10485760 | bytes 6291456 | tf_op jit(solution)/shard_map/adamw/pallas_call | solution.py:422
  (64 shorter events, 15.7 us)
Async XLA Ops:
  0.6 0.7 copy-start.3
  1.3 0.7 copy-start.4
  2.4 10.2 %collective-permute-start.2 = (bf16[16,640]{0,1:T(8,128)(2,1)S(1)}, bf16[16,640]{0,1:T(8,128)(2,1)S(1)}, u32[]{:S(2)}, u32[]{:S(2)}) collective-permute-start(bf16[16,640]{0,1:T(8,128)(2,1)S(1)} %copy.32), channel_id=1, source_target_pairs={{0,26},{2,8},{4,30},{6,12},{8,2},{10,16},{12,6},{14,20},{16,10},{1... | collective-permute-start | bytes 61448 | tf_op jit(solution)/shard_map/ppermute | solution.py:449
  6.9 6.8 %collective-permute-start.1 = (bf16[16,640]{0,1:T(8,128)(2,1)S(1)}, bf16[16,640]{0,1:T(8,128)(2,1)S(1)}, u32[]{:S(2)}, u32[]{:S(2)}) collective-permute-start(bf16[16,640]{0,1:T(8,128)(2,1)S(1)} %copy.32), channel_id=1, source_target_pairs={{0,4},{2,30},{4,8},{6,2},{8,12},{10,6},{12,16},{14,10},{16,20},{18... | collective-permute-start | bytes 61448 | tf_op jit(solution)/shard_map/ppermute | solution.py:449
  9.0 6.5 %collective-permute-start = (bf16[16,640]{0,1:T(8,128)(2,1)S(1)}, bf16[16,640]{0,1:T(8,128)(2,1)S(1)}, u32[]{:S(2)}, u32[]{:S(2)}) collective-permute-start(bf16[16,640]{0,1:T(8,128)(2,1)S(1)} %copy.32), channel_id=1, source_target_pairs={{0,30},{2,4},{4,2},{6,8},{8,6},{10,12},{12,10},{14,16},{16,14},{18... | collective-permute-start | bytes 61448 | tf_op jit(solution)/shard_map/ppermute | solution.py:449
  12.1 22.8 %collective-permute-start.7 = (bf16[1024,512]{1,0:T(8,128)(2,1)S(1)}, bf16[1024,512]{1,0:T(8,128)(2,1)S(1)}, u32[]{:S(2)}, u32[]{:S(2)}) collective-permute-start(bf16[1024,512]{1,0:T(8,128)(2,1)S(1)} %convert_element_type.34.refs_1_.refs_2_), channel_id=1, source_target_pairs={{0,2},{2,0},{4,6},{6,4},{8,10},{10,8},{12,14},{14,12},{16,18},{18,... | collective-permute-start | bytes 3145736 | tf_op jit(solution)/shard_map/ppermute | solution.py:449
  15.7 7.4 %collective-permute-start.3 = (bf16[64,640]{0,1:T(8,128)(2,1)S(1)}, bf16[64,640]{0,1:T(8,128)(2,1)S(1)}, u32[]{:S(2)}, u32[]{:S(2)}) collective-permute-start(bf16[64,640]{0,1:T(8,128)(2,1)S(1)} %pad_maximum_fusion.1), channel_id=1, source_target_pairs={{0,8},{2,26},{4,12},{6,30},{8,16},{10,2},{12,20},{14,6},{16,24},{1... | collective-permute-start | bytes 245768 | tf_op jit(solution)/shard_map/ppermute | solution.py:449
  23.6 5.5 %collective-permute-start.6 = (bf16[136,512]{1,0:T(8,128)(2,1)S(1)}, bf16[136,512]{1,0:T(8,128)(2,1)S(1)}, u32[]{:S(2)}, u32[]{:S(2)}) collective-permute-start(bf16[136,512]{1,0:T(8,128)(2,1)S(1)} %pad_maximum_fusion.2.refs_0_), channel_id=1, source_target_pairs={{0,128},{2,3},{4,132},{6,7},{8,136},{10,11},{12,140},{14,15},{16,1... | collective-permute-start | bytes 417800 | tf_op jit(solution)/shard_map/ppermute | solution.py:449
  26.6 5.1 %collective-permute-start.5 = (bf16[136,512]{1,0:T(8,128)(2,1)S(1)}, bf16[136,512]{1,0:T(8,128)(2,1)S(1)}, u32[]{:S(2)}, u32[]{:S(2)}) collective-permute-start(bf16[136,512]{1,0:T(8,128)(2,1)S(1)} %pad_maximum_fusion.2.refs_0_), channel_id=1, source_target_pairs={{0,192},{2,35},{4,196},{6,39},{8,200},{10,43},{12,204},{14,47},{16... | collective-permute-start | bytes 417800 | tf_op jit(solution)/shard_map/ppermute | solution.py:449
  27.4 4.3 %collective-permute-start.4 = (bf16[136,512]{1,0:T(8,128)(2,1)S(1)}, bf16[136,512]{1,0:T(8,128)(2,1)S(1)}, u32[]{:S(2)}, u32[]{:S(2)}) collective-permute-start(bf16[136,512]{1,0:T(8,128)(2,1)S(1)} %pad_maximum_fusion.2.refs_0_), channel_id=1, source_target_pairs={{0,64},{2,34},{4,68},{6,38},{8,72},{10,42},{12,76},{14,46},{16,80}... | collective-permute-start | bytes 417800 | tf_op jit(solution)/shard_map/ppermute | solution.py:449
  31.8 10.3 %collective-permute-start.10 = (bf16[544,512]{1,0:T(8,128)(2,1)S(1)}, bf16[544,512]{1,0:T(8,128)(2,1)S(1)}, u32[]{:S(2)}, u32[]{:S(2)}) collective-permute-start(bf16[544,512]{1,0:T(8,128)(2,1)S(1)} %pack.1.refs_0_), channel_id=1, source_target_pairs={{0,32},{2,66},{4,36},{6,70},{8,40},{10,74},{12,44},{14,78},{16,48}... | collective-permute-start | bytes 1671176 | tf_op jit(solution)/shard_map/ppermute | solution.py:449
  33.0 14.3 %collective-permute-start.9 = (bf16[544,512]{1,0:T(8,128)(2,1)S(1)}, bf16[544,512]{1,0:T(8,128)(2,1)S(1)}, u32[]{:S(2)}, u32[]{:S(2)}) collective-permute-start(bf16[544,512]{1,0:T(8,128)(2,1)S(1)} %pack.1.refs_0_), channel_id=1, source_target_pairs={{0,33},{2,194},{4,37},{6,198},{8,41},{10,202},{12,45},{14,206},{16... | collective-permute-start | bytes 1671176 | tf_op jit(solution)/shard_map/ppermute | solution.py:449
  37.4 12.5 %collective-permute-start.8 = (bf16[544,512]{1,0:T(8,128)(2,1)S(1)}, bf16[544,512]{1,0:T(8,128)(2,1)S(1)}, u32[]{:S(2)}, u32[]{:S(2)}) collective-permute-start(bf16[544,512]{1,0:T(8,128)(2,1)S(1)} %pack.1.refs_0_), channel_id=1, source_target_pairs={{0,1},{2,130},{4,5},{6,134},{8,9},{10,138},{12,13},{14,142},{16,17... | collective-permute-start | bytes 1671176 | tf_op jit(solution)/shard_map/ppermute | solution.py:449
  55.0 13.1 %collective-permute-start.11 = (f32[1024,512]{1,0:T(8,128)S(1)}, f32[1024,512]{1,0:T(8,128)S(1)}, u32[]{:S(2)}, u32[]{:S(2)}) collective-permute-start(f32[1024,512]{1,0:T(8,128)S(1)} %get-tuple-element.106), channel_id=1, source_target_pairs={{0,2},{2,0},{4,6},{6,4},{8,10},{10,8},{12,14},{14,12},{16,18},{18,... | collective-permute-start | bytes 6291464 | tf_op jit(solution)/shard_map/ppermute | solution.py:449
  65.8 2.4 %copy-start = (f32[1024,512]{1,0:T(8,128)S(1)}, f32[1024,512]{1,0:T(8,128)}, u32[]{:S(2)}) copy-start(f32[1024,512]{1,0:T(8,128)} %refs_2_.1) | copy-start | bytes 6291460
  65.8 2.4 %copy-start.1 = (f32[1024,512]{1,0:T(8,128)S(1)}, f32[1024,512]{1,0:T(8,128)}, u32[]{:S(2)}) copy-start(f32[1024,512]{1,0:T(8,128)} %refs_3_.1) | copy-start | bytes 6291460
  65.8 2.8 %copy-start.2 = (f32[1024,512]{1,0:T(8,128)S(1)}, f32[1024,512]{1,0:T(8,128)}, u32[]{:S(2)}) copy-start(f32[1024,512]{1,0:T(8,128)} %refs_4_.1) | copy-start | bytes 6291460
  70.4 3.7 %collective-permute-start.13 = (bf16[1024,512]{1,0:T(8,128)(2,1)S(1)}, bf16[1024,512]{1,0:T(8,128)(2,1)S(1)}, u32[]{:S(2)}, u32[]{:S(2)}) collective-permute-start(bf16[1024,512]{1,0:T(8,128)(2,1)S(1)} %get-tuple-element.117.refs_3_.wb), channel_id=1, source_target_pairs={{0,2},{2,0},{4,6},{6,4},{8,10},{10,8},{12,14},{14,12},{16,18},{18,... | collective-permute-start | bytes 3145736 | tf_op jit(solution)/shard_map/ppermute | solution.py:449
  70.5 14.9 %collective-permute-start.12 = (bf16[512,512]{1,0:T(8,128)(2,1)S(1)}, bf16[512,512]{1,0:T(8,128)(2,1)S(1)}, u32[]{:S(2)}, u32[]{:S(2)}) collective-permute-start(bf16[512,512]{1,0:T(8,128)(2,1)S(1)} %terms.2), channel_id=1, source_target_pairs={{0,32},{2,35},{4,36},{6,39},{8,40},{10,43},{12,44},{14,47},{16,48}... | collective-permute-start | bytes 1572872 | tf_op jit(solution)/shard_map/ppermute | solution.py:449
  77.7 15.3 %collective-permute-start.15 = (bf16[256,512]{1,0:T(8,128)(2,1)S(1)}, bf16[256,512]{1,0:T(8,128)(2,1)S(1)}, u32[]{:S(2)}, u32[]{:S(2)}) collective-permute-start(bf16[256,512]{1,0:T(8,128)(2,1)S(1)} %get-tuple-element.169), channel_id=1, source_target_pairs={{0,96},{2,227},{4,100},{6,231},{8,104},{10,235},{12,108},{14,239},... | collective-permute-start | bytes 786440 | tf_op jit(solution)/shard_map/ppermute | solution.py:449
  80.3 12.8 %collective-permute-start.14 = (bf16[256,512]{1,0:T(8,128)(2,1)S(1)}, bf16[256,512]{1,0:T(8,128)(2,1)S(1)}, u32[]{:S(2)}, u32[]{:S(2)}) collective-permute-start(bf16[256,512]{1,0:T(8,128)(2,1)S(1)} %get-tuple-element.170), channel_id=1, source_target_pairs={{0,32},{2,35},{4,36},{6,39},{8,40},{10,43},{12,44},{14,47},{16,48}... | collective-permute-start | bytes 786440 | tf_op jit(solution)/shard_map/ppermute | solution.py:449
  85.7 7.4 %collective-permute-start.16 = (bf16[256,512]{1,0:T(8,128)(2,1)S(1)}, bf16[256,512]{1,0:T(8,128)(2,1)S(1)}, u32[]{:S(2)}, u32[]{:S(2)}) collective-permute-start(bf16[256,512]{1,0:T(8,128)(2,1)S(1)} %slice.105), channel_id=1, source_target_pairs={{0,64},{2,194},{4,68},{6,198},{8,72},{10,202},{12,76},{14,206},{16... | collective-permute-start | bytes 786440 | tf_op jit(solution)/shard_map/ppermute | solution.py:449
  86.7 8.3 %collective-permute-start.17 = (bf16[256,512]{1,0:T(8,128)(2,1)S(1)}, bf16[256,512]{1,0:T(8,128)(2,1)S(1)}, u32[]{:S(2)}, u32[]{:S(2)}) collective-permute-start(bf16[256,512]{1,0:T(8,128)(2,1)S(1)} %slice.104), channel_id=1, source_target_pairs={{0,64},{2,194},{4,68},{6,198},{8,72},{10,202},{12,76},{14,206},{16... | collective-permute-start | bytes 786440 | tf_op jit(solution)/shard_map/ppermute | solution.py:449
  95.0 15.1 %collective-permute-start.24 = (f32[1024,512]{1,0:T(8,128)S(1)}, f32[1024,512]{1,0:T(8,128)S(1)}, u32[]{:S(2)}, u32[]{:S(2)}) collective-permute-start(f32[1024,512]{1,0:T(8,128)S(1)} %get-tuple-element.152), channel_id=1, source_target_pairs={{0,2},{2,0},{4,6},{6,4},{8,10},{10,8},{12,14},{14,12},{16,18},{18,... | collective-permute-start | bytes 6291464 | tf_op jit(solution)/shard_map/ppermute | solution.py:449
  95.5 10.2 %collective-permute-start.20 = (bf16[4,2,16,512]{3,2,1,0:T(8,128)(2,1)S(1)}, bf16[4,2,16,512]{3,2,1,0:T(8,128)(2,1)S(1)}, u32[]{:S(2)}, u32[]{:S(2)}) collective-permute-start(bf16[4,2,16,512]{3,2,1,0:T(8,128)(2,1)S(1)} %get-tuple-element.166), channel_id=1, source_target_pairs={{0,216},{2,74},{4,220},{6,78},{8,192},{10,82},{12,196},{14,86},{16... | collective-permute-start | bytes 393224 | tf_op jit(solution)/shard_map/ppermute | solution.py:449
  95.6 10.1 %collective-permute-start.19 = (bf16[4,2,16,512]{3,2,1,0:T(8,128)(2,1)S(1)}, bf16[4,2,16,512]{3,2,1,0:T(8,128)(2,1)S(1)}, u32[]{:S(2)}, u32[]{:S(2)}) collective-permute-start(bf16[4,2,16,512]{3,2,1,0:T(8,128)(2,1)S(1)} %get-tuple-element.167), channel_id=1, source_target_pairs={{0,24},{2,10},{4,28},{6,14},{8,0},{10,18},{12,4},{14,22},{16,8},{1... | collective-permute-start | bytes 393224 | tf_op jit(solution)/shard_map/ppermute | solution.py:449
  98.3 7.4 %collective-permute-start.18 = (bf16[4,2,16,512]{3,2,1,0:T(8,128)(2,1)S(1)}, bf16[4,2,16,512]{3,2,1,0:T(8,128)(2,1)S(1)}, u32[]{:S(2)}, u32[]{:S(2)}) collective-permute-start(bf16[4,2,16,512]{3,2,1,0:T(8,128)(2,1)S(1)} %get-tuple-element.168), channel_id=1, source_target_pairs={{0,192},{2,66},{4,196},{6,70},{8,200},{10,74},{12,204},{14,78},{16... | collective-permute-start | bytes 393224 | tf_op jit(solution)/shard_map/ppermute | solution.py:449
  105.8 7.6 %collective-permute-start.23 = (f32[2,16,512]{2,1,0:T(8,128)S(1)}, f32[2,16,512]{2,1,0:T(8,128)S(1)}, u32[]{:S(2)}, u32[]{:S(2)}) collective-permute-start(f32[2,16,512]{2,1,0:T(8,128)S(1)} %get-tuple-element.171), channel_id=1, source_target_pairs={{0,26},{2,8},{4,30},{6,12},{8,2},{10,16},{12,6},{14,20},{16,10},{1... | collective-permute-start | bytes 196616 | tf_op jit(solution)/shard_map/ppermute | solution.py:449
  107.0 6.3 %collective-permute-start.22 = (f32[2,16,512]{2,1,0:T(8,128)S(1)}, f32[2,16,512]{2,1,0:T(8,128)S(1)}, u32[]{:S(2)}, u32[]{:S(2)}) collective-permute-start(f32[2,16,512]{2,1,0:T(8,128)S(1)} %get-tuple-element.172), channel_id=1, source_target_pairs={{0,28},{2,6},{4,0},{6,10},{8,4},{10,14},{12,8},{14,18},{16,12},{18... | collective-permute-start | bytes 196616 | tf_op jit(solution)/shard_map/ppermute | solution.py:449
  107.0 6.3 %collective-permute-start.21 = (f32[2,16,512]{2,1,0:T(8,128)S(1)}, f32[2,16,512]{2,1,0:T(8,128)S(1)}, u32[]{:S(2)}, u32[]{:S(2)}) collective-permute-start(f32[2,16,512]{2,1,0:T(8,128)S(1)} %get-tuple-element.173), channel_id=1, source_target_pairs={{0,30},{2,4},{4,2},{6,8},{8,6},{10,12},{12,10},{14,16},{16,14},{18... | collective-permute-start | bytes 196616 | tf_op jit(solution)/shard_map/ppermute | solution.py:449

commit v3 on v2

--- a/solution.py
+++ b/solution.py
@@ -197,9 +197,13 @@
     )(part, wb, wb_other, *into)
 
 
-def code_kernel(q_ref, pos_ref, out_ref):
-    ids = pos_ref[...]
-    out_ref[:, :D] = q_ref[...]
+def code_kernel(q_ref, pos_ref, out_ref, ids_ref, sems):
+    rows = pltpu.make_async_copy(q_ref, out_ref.at[:, :D], sems.at[0])
+    slots = pltpu.make_async_copy(pos_ref, ids_ref, sems.at[1])
+    slots.start()
+    rows.start()
+    slots.wait()
+    ids = ids_ref[...]
     digits = [ids & 255, (ids >> 8) & 255, ids >> 16]
     lane = lax.broadcasted_iota(i32, (SLOTS, LINE), 1) - lax.broadcasted_iota(i32, (SLOTS, LINE), 0)
     coded = jnp.zeros((ROWS, LINE), f32)
@@ -207,14 +211,16 @@
         put = (lane == i * SLOTS).astype(f32).astype(bf16)
         coded = coded + contract_first(digit.astype(f32).astype(bf16), put)
     out_ref[:, D:] = coded.astype(bf16)
+    rows.wait()
 
 
 def code(queries, positives):
     return pl.pallas_call(
         code_kernel,
         out_shape=jax.ShapeDtypeStruct((ROWS, D + LINE), bf16),
-        in_specs=[spec()] * 2,
+        in_specs=[spec(space=pl.ANY)] * 2,
         out_specs=spec(),
+        scratch_shapes=[pltpu.VMEM((SLOTS, ROWS), i32), pltpu.SemaphoreType.DMA((2,))],
         compiler_params=params(),
         cost_estimate=cost(size=4 * ROWS * D),
         name="code",
@@ -519,28 +525,26 @@
 
     part = swap(theirs)
     mine = gradient(own, q)
-    out0 = terms(*step0, beside, bf16)
-    part, mine, out0 = after(part, mine, out0)
+    out0 = send(terms(*step0, beside, bf16), over_y)
+    part, mine = after(part, mine)
     weight, first, second, wb = update(past_steps + 1, False, mine, part, weight, first, second)
 
     wb_other = swap(wb)
-    wb, out0, *step0 = after(wb, out0, *step0)
-    out0 = send(out0, over_y)
-    part0 = terms(*step0, here, f32)
+    wb, *step0 = after(wb, *step0)
+    part0 = terms(*step0, here, f32) + out0.astype(f32)
+    half0 = send(part0[BLOCK:].astype(bf16), first_x)
     wb_other, part0 = after(wb_other, part0)
     own, other, out1 = plane_terms(most, q, pos, wb, wb_other, beside, bf16)
+    half0, out1 = after(half0, out1)
 
     out1, own, other = after(out1, own, other)
     got = [send(out1[:BLOCK], over_y), send(out1[BLOCK:], then(over_y, first_x))]
     own, other, part1 = plane_terms(most, q, pos, wb, wb_other, here, f32, (own, other))
-    out0, part1 = after(out0, part1)
     got.append(send(part1[BLOCK:].astype(bf16), first_x))
-    part0 = part0 + out0.astype(f32)
-    half0 = send(part0[BLOCK:].astype(bf16), first_x)
-
-    part1, part0, other = after(part1, part0, other)
+
+    part1, other = after(part1, other)
     theirs = rest_gradient(most, q, pos, wb_other, other, 1)
-    *got, half0, theirs, own = after(*got, half0, theirs, own)
+    *got, theirs, own = after(*got, theirs, own)
     part = swap(theirs)
     pair0 = part0[:BLOCK] + half0.astype(f32)
     pair1 = part1[:BLOCK] + got[0].astype(f32) + got[1].astype(f32) + got[2].astype(f32)

time: 114 us -> 121 us (1.061)
  waiting for transfers between devices: 19.7 us -> 27 us
    ppermute x25, waiting for transfers between devices: 19.7 us -> 27 us  [send(): return lax.ppermute(array, AXES, moved(move))]
  transfers between devices with their start and end apart: 25 -> 25, of which waited for: 8 -> 11; matrix products, arithmetic and copies ran while one was open for 3% -> 3% of each run, Pallas kernels for 28% -> 27%
where the time goes in v3:
time: 121 us
  starting transfers between devices  48.6 us (40%)
  Pallas kernels  39.3 us (32%)
  waiting for transfers between devices  27 us (22%)
  other arithmetic  3.25 us (3%)
  local copies, waits for them, and re-layouts  2.18 us (2%)
    ppermute x25, starting transfers between devices, send(): return lax.ppermute(array, AXES, moved(move))  48.6 us
    ppermute x25, waiting for transfers between devices, send(): return lax.ppermute(array, AXES, moved(move))  27 us
    pallas_call x4, Pallas kernels, first_residuals(): pl.pallas_call(lambda *refs: part_kernel(*refs, late=late), out_shape=sha...  12.8 us
    pallas_call x2, Pallas kernels, rest_gradient(): pl.pallas_call(lambda most, q, pos, wb, old, resid, out: rest_kernel(most...  8.91 us
    pallas_call x2, Pallas kernels, plane_terms(): pl.pallas_call(lambda *refs: plane_kernel(*refs, blocks=blocks), out_shap...  6.99 us
    pallas_call x2, Pallas kernels, update(): pl.pallas_call(lambda *refs: kernel(count, *refs), out_shape=(full, full,...  4.94 us
    pallas_call x2, Pallas kernels, terms(): pl.pallas_call(lambda *refs: terms_kernel(*refs, blocks=blocks), out_shap...  3.03 us
  transfers between devices with their start and end apart: 25, of which 11 were waited for; matrix products, arithmetic and copies ran while one was open for 3% of the time, Pallas kernels for 27%

profile of v3, /device:TPU:1, one launch (start us, length us, event | category | flops | bytes accessed | tf_op | source)
XLA Modules:
  0.0 121.3 jit_solution(15870130716072195298)
XLA Ops:
  2.4 4.5 %collective-permute-start.2 = (bf16[16,640]{0,1:T(8,128)(2,1)S(1)}, bf16[16,640]{0,1:T(8,128)(2,1)S(1)}, u32[]{:S(2)}, u32[]{:S(2)}) collective-permute-start(bf16[16,640]{0,1:T(8,128)(2,1)S(1)} %copy.32), channel_id=1, source_target_pairs={{0,26},{2,8},{4,30},{6,12},{8,2},{10,16},{12,6},{14,20},{16,10},{1... | collective-permute-start | bytes 61448 | tf_op jit(solution)/shard_map/ppermute | solution.py:455
  6.9 2.1 %collective-permute-start.1 = (bf16[16,640]{0,1:T(8,128)(2,1)S(1)}, bf16[16,640]{0,1:T(8,128)(2,1)S(1)}, u32[]{:S(2)}, u32[]{:S(2)}) collective-permute-start(bf16[16,640]{0,1:T(8,128)(2,1)S(1)} %copy.32), channel_id=1, source_target_pairs={{0,4},{2,30},{4,8},{6,2},{8,12},{10,6},{12,16},{14,10},{16,20},{18... | collective-permute-start | bytes 61448 | tf_op jit(solution)/shard_map/ppermute | solution.py:455
  10.4 1.7 %convert_element_type.34.refs_1_.refs_2_ = bf16[1024,512]{1,0:T(8,128)(2,1)S(1)} convert(f32[1024,512]{1,0:T(8,128)} %refs_2_.1) | non-fusion elementwise | flops 524288 | bytes 3145728 | tf_op jit(solution)/shard_map/convert_element_type | solution.py:514
  13.7 1.8 %collective-permute-done = bf16[16,640]{0,1:T(8,128)(2,1)S(1)} collective-permute-done((bf16[16,640]{0,1:T(8,128)(2,1)S(1)}, bf16[16,640]{0,1:T(8,128)(2,1)S(1)}, u32[]{:S(2)}, u32[]{:S(2)}) %collective-permute-start) | collective-permute-done | bytes 20512 | tf_op jit(solution)/shard_map/ppermute | solution.py:455
  15.7 3.5 %collective-permute-start.3 = (bf16[64,640]{0,1:T(8,128)(2,1)S(1)}, bf16[64,640]{0,1:T(8,128)(2,1)S(1)}, u32[]{:S(2)}, u32[]{:S(2)}) collective-permute-start(bf16[64,640]{0,1:T(8,128)(2,1)S(1)} %pad_maximum_fusion.1), channel_id=1, source_target_pairs={{0,8},{2,26},{4,12},{6,30},{8,16},{10,2},{12,20},{14,6},{16,24},{1... | collective-permute-start | bytes 245768 | tf_op jit(solution)/shard_map/ppermute | solution.py:455
  19.2 3.9 %collective-permute-done.3 = bf16[64,640]{0,1:T(8,128)(2,1)S(1)} collective-permute-done((bf16[64,640]{0,1:T(8,128)(2,1)S(1)}, bf16[64,640]{0,1:T(8,128)(2,1)S(1)}, u32[]{:S(2)}, u32[]{:S(2)}) %collective-permute-start.3) | collective-permute-done | bytes 81952 | tf_op jit(solution)/shard_map/ppermute | solution.py:455
  23.6 3.0 %collective-permute-start.6 = (bf16[136,512]{1,0:T(8,128)(2,1)S(1)}, bf16[136,512]{1,0:T(8,128)(2,1)S(1)}, u32[]{:S(2)}, u32[]{:S(2)}) collective-permute-start(bf16[136,512]{1,0:T(8,128)(2,1)S(1)} %pad_maximum_fusion.2.refs_0_), channel_id=1, source_target_pairs={{0,128},{2,3},{4,132},{6,7},{8,136},{10,11},{12,140},{14,15},{16,1... | collective-permute-start | bytes 417800 | tf_op jit(solution)/shard_map/ppermute | solution.py:455
  27.4 1.7 %collective-permute-done.6.refs_3_ = bf16[136,512]{1,0:T(8,128)(2,1)S(1)} collective-permute-done((bf16[136,512]{1,0:T(8,128)(2,1)S(1)}, bf16[136,512]{1,0:T(8,128)(2,1)S(1)}, u32[]{:S(2)}, u32[]{:S(2)}) %collective-permute-start.6) | collective-permute-done | bytes 139296 | tf_op jit(solution)/shard_map/ppermute | solution.py:455
  29.1 2.6 %collective-permute-done.5.refs_2_ = bf16[136,512]{1,0:T(8,128)(2,1)S(1)} collective-permute-done((bf16[136,512]{1,0:T(8,128)(2,1)S(1)}, bf16[136,512]{1,0:T(8,128)(2,1)S(1)}, u32[]{:S(2)}, u32[]{:S(2)}) %collective-permute-start.5) | collective-permute-done | bytes 139296 | tf_op jit(solution)/shard_map/ppermute | solution.py:455
  33.1 1.8 %collective-permute-start.9 = (bf16[544,512]{1,0:T(8,128)(2,1)S(1)}, bf16[544,512]{1,0:T(8,128)(2,1)S(1)}, u32[]{:S(2)}, u32[]{:S(2)}) collective-permute-start(bf16[544,512]{1,0:T(8,128)(2,1)S(1)} %pack.1.refs_0_), channel_id=1, source_target_pairs={{0,33},{2,194},{4,37},{6,198},{8,41},{10,202},{12,45},{14,206},{16... | collective-permute-start | bytes 1671176 | tf_op jit(solution)/shard_map/ppermute | solution.py:455
  34.9 2.6 %part.4 = (bf16[2048,512]{1,0:T(8,128)(2,1)S(1)}, s32[2,8,2048]{2,1,0:T(8,128)S(1)}, bf16[1024,2048]{1,0:T(8,128)(2,1)S(1)}, bf16[1024,2048]{1,0:T(8,128)(2,1)S(1)}, f32[8,128]{1,0:T(8,128)S(1)}) custom-call(bf16[544,512]{1,0:T(8,128)(2,1)S(1)} %pack.1.refs_0_, bf16[1024,512]{1,0:T(8,128)(2,1)S(1)} %convert_element_type.34.refs_1_.refs_2_, ...), custom_call_target="tpu_custom_call" | custom-call | flops 1073741824 | bytes 2097152 | tf_op jit(solution)/shard_map/part/pallas_call | solution.py:188
  38.2 3.8 %collective-permute-done.10.refs_0_ = bf16[544,512]{1,0:T(8,128)(2,1)S(1)} collective-permute-done((bf16[544,512]{1,0:T(8,128)(2,1)S(1)}, bf16[544,512]{1,0:T(8,128)(2,1)S(1)}, u32[]{:S(2)}, u32[]{:S(2)}) %collective-permute-start.10) | collective-permute-done | bytes 557088 | tf_op jit(solution)/shard_map/ppermute | solution.py:455
  42.0 2.6 %part.5 = (bf16[2048,512]{1,0:T(8,128)(2,1)S(1)}, s32[2,8,2048]{2,1,0:T(8,128)S(1)}, bf16[1024,2048]{1,0:T(8,128)(2,1)S(1)}, bf16[1024,2048]{1,0:T(8,128)(2,1)S(1)}, f32[8,128]{1,0:T(8,128)S(1)}) custom-call(bf16[544,512]{1,0:T(8,128)(2,1)S(1)} %collective-permute-done.10.refs_0_, ...), custom_call_target="tpu_custom_call", output_to_operand_aliasing={{0}: (3, {}), {1}: (4, {}), {2}: (5, {}), {3}: (6, {}), {4}... | custom-call | flops 1073741824 | bytes 2097152 | tf_op jit(solution)/shard_map/part/pallas_call | solution.py:188
  44.6 2.7 %collective-permute-done.9.refs_0_ = bf16[544,512]{1,0:T(8,128)(2,1)S(1)} collective-permute-done((bf16[544,512]{1,0:T(8,128)(2,1)S(1)}, bf16[544,512]{1,0:T(8,128)(2,1)S(1)}, u32[]{:S(2)}, u32[]{:S(2)}) %collective-permute-start.9) | collective-permute-done | bytes 557088 | tf_op jit(solution)/shard_map/ppermute | solution.py:455
  47.3 2.6 %part.6 = (bf16[2048,512]{1,0:T(8,128)(2,1)S(1)}, s32[2,8,2048]{2,1,0:T(8,128)S(1)}, bf16[1024,2048]{1,0:T(8,128)(2,1)S(1)}, bf16[1024,2048]{1,0:T(8,128)(2,1)S(1)}, f32[8,128]{1,0:T(8,128)S(1)}) custom-call(bf16[544,512]{1,0:T(8,128)(2,1)S(1)} %collective-permute-done.9.refs_0_, ...), custom_call_target="tpu_custom_call", output_to_operand_aliasing={{0}: (3, {}), {1}: (4, {}), {2}: (5, {}), {3}: (6, {}), {4}... | custom-call | flops 1073741824 | bytes 2097152 | tf_op jit(solution)/shard_map/part/pallas_call | solution.py:188
  50.0 5.1 %part.7 = (bf16[2048,512]{1,0:T(8,128)(2,1)S(1)}, s32[2,8,2048]{2,1,0:T(8,128)S(1)}, bf16[1024,2048]{1,0:T(8,128)(2,1)S(1)}, bf16[1024,2048]{1,0:T(8,128)(2,1)S(...) custom-call(bf16[544,512]{1,0:T(8,128)(2,1)S(1)} %collective-permute, ...), custom_call_target="tpu_custom_call", output_to_operand_aliasing={{0}: (3, {}), {1}: (4, {}), {2}: (5, {}), {3}: (6, {}), {4}... | custom-call | flops 2147483648 | bytes 2097152 | tf_op jit(solution)/shard_map/part/pallas_call | solution.py:188
  55.1 9.2 %collective-permute-start.11 = (f32[1024,512]{1,0:T(8,128)S(1)}, f32[1024,512]{1,0:T(8,128)S(1)}, u32[]{:S(2)}, u32[]{:S(2)}) collective-permute-start(f32[1024,512]{1,0:T(8,128)S(1)} %get-tuple-element.102), channel_id=1, source_target_pairs={{0,2},{2,0},{4,6},{6,4},{8,10},{10,8},{12,14},{14,12},{16,18},{18,... | collective-permute-start | bytes 6291464 | tf_op jit(solution)/shard_map/ppermute | solution.py:455
  64.3 2.3 %grad.1.refs_0_ = f32[1024,512]{1,0:T(8,128)S(1)} custom-call(bf16[1024,2048]{1,0:T(8,128)(2,1)S(1)} %get-tuple-element.109.resid_ref.refs_0_, bf16[2048,512]{1,0:T(8,128)(2,1)S(1)} %get-tuple-element.104.q_ref.refs_1_.q), custom_call_target="tpu_custom_call" | custom-call | flops 2147483648 | bytes 8388608 | tf_op jit(solution)/shard_map/grad/pallas_call | solution.py:377
  68.1 1.8 %adamw.2 = (f32[1024,512]{1,0:T(8,128)S(1)}, f32[1024,512]{1,0:T(8,128)S(1)}, f32[1024,512]{1,0:T(8,128)S(1)}, bf16[1024,512]{1,0:T(8,128)(2,1)S(1)}) custom-call(f32[1024,512]{1,0:T(8,128)S(1)} %grad.1.refs_0_, f32[1024,512]{1,0:T(8,128)S(1)} %collective-permute-done.11.refs_1_, f32[1024,512]{1,0:T(8,128)S(1)} %copy-done, f32[1024,512]{1,0:T(8,128)S(1)} %copy-done.1, ...), custom_call_target="tpu_custom_call" | custom-call | flops 10485760 | bytes 6291456 | tf_op jit(solution)/shard_map/adamw/pallas_call | solution.py:428
  71.9 2.0 %collective-permute-start.13 = (bf16[512,512]{1,0:T(8,128)(2,1)S(1)}, bf16[512,512]{1,0:T(8,128)(2,1)S(1)}, u32[]{:S(2)}, u32[]{:S(2)}) collective-permute-start(bf16[512,512]{1,0:T(8,128)(2,1)S(1)} %terms.3), channel_id=1, source_target_pairs={{0,32},{2,35},{4,36},{6,39},{8,40},{10,43},{12,44},{14,47},{16,48}... | collective-permute-start | bytes 1572872 | tf_op jit(solution)/shard_map/ppermute | solution.py:455
  73.9 1.5 %terms.2 = f32[512,512]{1,0:T(8,128)S(1)} custom-call(bf16[1024,2048]{1,0:T(8,128)(2,1)S(1)} %get-tuple-element.109.resid_ref.refs_0_, bf16[1024,2048]{1,0:T(8,128)(2,1)S(1)} %get-tuple-element.110.refs_1_, bf16[1024,512]{1,0:T(8,128)(2,1)S(1)} %convert_element_type.34.refs_1_.refs_2_, bf16[1024,512]{1,0:T(8,128)(2,1)S(1)} %collective-permute-done.7.refs_2_.refs_3_), custom_call_target="tpu_custom_call" | custom-call | flops 1073741824 | bytes 4194304 | tf_op jit(solution)/shard_map/terms/pallas_call | solution.py:335
  75.4 5.8 %collective-permute-done.13 = bf16[512,512]{1,0:T(8,128)(2,1)S(1)} collective-permute-done((bf16[512,512]{1,0:T(8,128)(2,1)S(1)}, bf16[512,512]{1,0:T(8,128)(2,1)S(1)}, u32[]{:S(2)}, u32[]{:S(2)}) %collective-permute-start.13) | collective-permute-done | bytes 524320 | tf_op jit(solution)/shard_map/ppermute | solution.py:455
  81.4 1.8 %collective-permute-start.14 = (bf16[256,512]{1,0:T(8,128)(2,1)S(1)}, bf16[256,512]{1,0:T(8,128)(2,1)S(1)}, u32[]{:S(2)}, u32[]{:S(2)}) collective-permute-start(bf16[256,512]{1,0:T(8,128)(2,1)S(1)} %slice.105), channel_id=1, source_target_pairs={{0,64},{2,194},{4,68},{6,198},{8,72},{10,202},{12,76},{14,206},{16... | collective-permute-start | bytes 786440 | tf_op jit(solution)/shard_map/ppermute | solution.py:455
  83.2 3.5 %plane.2 = (bf16[1024,2048]{1,0:T(8,128)(2,1)S(1)}, bf16[1024,2048]{1,0:T(8,128)(2,1)S(1)}, bf16[512,512]{1,0:T(8,128)(2,1)S(1)}) custom-call(f32[8,128]{1,0:T(8,128)S(1)} %get-tuple-element.114.refs_0_.most, bf16[2048,512]{1,0:T(8,128)(2,1)S(1)} %get-tuple-element.104.q_ref.refs_1_.q, s32[2,8,2048]{2,1,0:T(8,128)S(1)} %get-tuple-element.115.refs_2_.pos, ...), custom_call_target="tpu_custom_call" | custom-call | flops 2147483648 | bytes 4194304 | tf_op jit(solution)/shard_map/plane/pallas_call | solution.py:318
  88.0 3.5 %collective-permute-start.16 = (bf16[256,512]{1,0:T(8,128)(2,1)S(1)}, bf16[256,512]{1,0:T(8,128)(2,1)S(1)}, u32[]{:S(2)}, u32[]{:S(2)}) collective-permute-start(bf16[256,512]{1,0:T(8,128)(2,1)S(1)} %get-tuple-element.161), channel_id=1, source_target_pairs={{0,96},{2,227},{4,100},{6,231},{8,104},{10,235},{12,108},{14,239},... | collective-permute-start | bytes 786440 | tf_op jit(solution)/shard_map/ppermute | solution.py:455
  92.2 3.5 %plane.3 = (bf16[1024,2048]{1,0:T(8,128)(2,1)S(1)}, bf16[1024,2048]{1,0:T(8,128)(2,1)S(1)}, f32[512,512]{1,0:T(8,128)S(1)}) custom-call(f32[8,128]{1,0:T(8,128)S(1)} %get-tuple-element.114.refs_0_.most, bf16[2048,512]{1,0:T(8,128)(2,1)S(1)} %get-tuple-element.104.q_ref.refs_1_.q, ...), custom_call_target="tpu_custom_call", output_to_operand_aliasing={{0}: (5, {}), {1}: (6, {})} | custom-call | flops 2147483648 | bytes 4194304 | tf_op jit(solution)/shard_map/plane/pallas_call | solution.py:318
  96.7 4.6 %rest.2 = (bf16[1024,2048]{1,0:T(8,128)(2,1)S(1)}, f32[1024,512]{1,0:T(8,128)S(1)}) custom-call(f32[8,128]{1,0:T(8,128)S(1)} %get-tuple-element.114.refs_0_.most, bf16[2048,512]{1,0:T(8,128)(2,1)S(1)} %get-tuple-element.104.q_ref.refs_1_.q, s32[2,8,2048]{2,1,0:T(8,128)S(1)} %get-tuple-element.115.refs_2_.pos, ...), custom_call_target="tpu_custom_call", output_to_operand_aliasing={{0}: (4, {})} | custom-call | flops 3221225472 | bytes 8388608 | tf_op jit(solution)/shard_map/rest/pallas_call | solution.py:360
  102.8 3.3 %collective-permute-start.19 = (bf16[4,2,16,512]{3,2,1,0:T(8,128)(2,1)S(1)}, bf16[4,2,16,512]{3,2,1,0:T(8,128)(2,1)S(1)}, u32[]{:S(2)}, u32[]{:S(2)}) collective-permute-start(bf16[4,2,16,512]{3,2,1,0:T(8,128)(2,1)S(1)} %get-tuple-element.159), channel_id=1, source_target_pairs={{0,24},{2,10},{4,28},{6,14},{8,0},{10,18},{12,4},{14,22},{16,8},{1... | collective-permute-start | bytes 393224 | tf_op jit(solution)/shard_map/ppermute | solution.py:455
  106.1 2.4 %collective-permute-start.18 = (bf16[4,2,16,512]{3,2,1,0:T(8,128)(2,1)S(1)}, bf16[4,2,16,512]{3,2,1,0:T(8,128)(2,1)S(1)}, u32[]{:S(2)}, u32[]{:S(2)}) collective-permute-start(bf16[4,2,16,512]{3,2,1,0:T(8,128)(2,1)S(1)} %get-tuple-element.160), channel_id=1, source_target_pairs={{0,192},{2,66},{4,196},{6,70},{8,200},{10,74},{12,204},{14,78},{16... | collective-permute-start | bytes 393224 | tf_op jit(solution)/shard_map/ppermute | solution.py:455
  108.6 4.3 %rest.3 = (bf16[1024,2048]{1,0:T(8,128)(2,1)S(1)}, f32[1024,512]{1,0:T(8,128)S(1)}) custom-call(f32[8,128]{1,0:T(8,128)S(1)} %get-tuple-element.114.refs_0_.most, bf16[2048,512]{1,0:T(8,128)(2,1)S(1)} %get-tuple-element.104.q_ref.refs_1_.q, s32[2,8,2048]{2,1,0:T(8,128)S(1)} %get-tuple-element.115.refs_2_.pos, ...), custom_call_target="tpu_custom_call", output_to_operand_aliasing={{0}: (4, {})} | custom-call | flops 3221225472 | bytes 8388608 | tf_op jit(solution)/shard_map/rest/pallas_call | solution.py:360
  114.3 3.1 %collective-permute-start.21 = (f32[2,16,512]{2,1,0:T(8,128)S(1)}, f32[2,16,512]{2,1,0:T(8,128)S(1)}, u32[]{:S(2)}, u32[]{:S(2)}) collective-permute-start(f32[2,16,512]{2,1,0:T(8,128)S(1)} %get-tuple-element.165), channel_id=1, source_target_pairs={{0,30},{2,4},{4,2},{6,8},{8,6},{10,12},{12,10},{14,16},{16,14},{18... | collective-permute-start | bytes 196616 | tf_op jit(solution)/shard_map/ppermute | solution.py:455
  117.4 3.2 %adamw.3 = (f32[1024,512]{1,0:T(8,128)}, f32[1024,512]{1,0:T(8,128)}, f32[1024,512]{1,0:T(8,128)}) custom-call(f32[1024,512]{1,0:T(8,128)S(1)} %get-tuple-element.143.refs_0_, f32[1024,512]{1,0:T(8,128)S(1)} %collective-permute-done.24.refs_1_, f32[1024,512]{1,0:T(8,128)S(1)} %get-tuple-element.145.refs_2_, f32[1024,512]{1,0:T(8,128)S(1)} %get-tuple-element.146.refs_3_, ...), custom_call_target="tpu_custom_call" | custom-call | flops 10485760 | bytes 6291456 | tf_op jit(solution)/shard_map/adamw/pallas_call | solution.py:428
  (65 shorter events, 18.4 us)
Async XLA Ops:
  0.6 0.7 copy-start.3
  1.3 0.7 copy-start.4
  2.4 10.2 %collective-permute-start.2 = (bf16[16,640]{0,1:T(8,128)(2,1)S(1)}, bf16[16,640]{0,1:T(8,128)(2,1)S(1)}, u32[]{:S(2)}, u32[]{:S(2)}) collective-permute-start(bf16[16,640]{0,1:T(8,128)(2,1)S(1)} %copy.32), channel_id=1, source_target_pairs={{0,26},{2,8},{4,30},{6,12},{8,2},{10,16},{12,6},{14,20},{16,10},{1... | collective-permute-start | bytes 61448 | tf_op jit(solution)/shard_map/ppermute | solution.py:455
  6.9 6.8 %collective-permute-start.1 = (bf16[16,640]{0,1:T(8,128)(2,1)S(1)}, bf16[16,640]{0,1:T(8,128)(2,1)S(1)}, u32[]{:S(2)}, u32[]{:S(2)}) collective-permute-start(bf16[16,640]{0,1:T(8,128)(2,1)S(1)} %copy.32), channel_id=1, source_target_pairs={{0,4},{2,30},{4,8},{6,2},{8,12},{10,6},{12,16},{14,10},{16,20},{18... | collective-permute-start | bytes 61448 | tf_op jit(solution)/shard_map/ppermute | solution.py:455
  9.0 6.5 %collective-permute-start = (bf16[16,640]{0,1:T(8,128)(2,1)S(1)}, bf16[16,640]{0,1:T(8,128)(2,1)S(1)}, u32[]{:S(2)}, u32[]{:S(2)}) collective-permute-start(bf16[16,640]{0,1:T(8,128)(2,1)S(1)} %copy.32), channel_id=1, source_target_pairs={{0,30},{2,4},{4,2},{6,8},{8,6},{10,12},{12,10},{14,16},{16,14},{18... | collective-permute-start | bytes 61448 | tf_op jit(solution)/shard_map/ppermute | solution.py:455
  12.1 22.8 %collective-permute-start.7 = (bf16[1024,512]{1,0:T(8,128)(2,1)S(1)}, bf16[1024,512]{1,0:T(8,128)(2,1)S(1)}, u32[]{:S(2)}, u32[]{:S(2)}) collective-permute-start(bf16[1024,512]{1,0:T(8,128)(2,1)S(1)} %convert_element_type.34.refs_1_.refs_2_), channel_id=1, source_target_pairs={{0,2},{2,0},{4,6},{6,4},{8,10},{10,8},{12,14},{14,12},{16,18},{18,... | collective-permute-start | bytes 3145736 | tf_op jit(solution)/shard_map/ppermute | solution.py:455
  15.7 7.4 %collective-permute-start.3 = (bf16[64,640]{0,1:T(8,128)(2,1)S(1)}, bf16[64,640]{0,1:T(8,128)(2,1)S(1)}, u32[]{:S(2)}, u32[]{:S(2)}) collective-permute-start(bf16[64,640]{0,1:T(8,128)(2,1)S(1)} %pad_maximum_fusion.1), channel_id=1, source_target_pairs={{0,8},{2,26},{4,12},{6,30},{8,16},{10,2},{12,20},{14,6},{16,24},{1... | collective-permute-start | bytes 245768 | tf_op jit(solution)/shard_map/ppermute | solution.py:455
  23.6 5.5 %collective-permute-start.6 = (bf16[136,512]{1,0:T(8,128)(2,1)S(1)}, bf16[136,512]{1,0:T(8,128)(2,1)S(1)}, u32[]{:S(2)}, u32[]{:S(2)}) collective-permute-start(bf16[136,512]{1,0:T(8,128)(2,1)S(1)} %pad_maximum_fusion.2.refs_0_), channel_id=1, source_target_pairs={{0,128},{2,3},{4,132},{6,7},{8,136},{10,11},{12,140},{14,15},{16,1... | collective-permute-start | bytes 417800 | tf_op jit(solution)/shard_map/ppermute | solution.py:455
  26.6 5.1 %collective-permute-start.5 = (bf16[136,512]{1,0:T(8,128)(2,1)S(1)}, bf16[136,512]{1,0:T(8,128)(2,1)S(1)}, u32[]{:S(2)}, u32[]{:S(2)}) collective-permute-start(bf16[136,512]{1,0:T(8,128)(2,1)S(1)} %pad_maximum_fusion.2.refs_0_), channel_id=1, source_target_pairs={{0,192},{2,35},{4,196},{6,39},{8,200},{10,43},{12,204},{14,47},{16... | collective-permute-start | bytes 417800 | tf_op jit(solution)/shard_map/ppermute | solution.py:455
  27.4 4.3 %collective-permute-start.4 = (bf16[136,512]{1,0:T(8,128)(2,1)S(1)}, bf16[136,512]{1,0:T(8,128)(2,1)S(1)}, u32[]{:S(2)}, u32[]{:S(2)}) collective-permute-start(bf16[136,512]{1,0:T(8,128)(2,1)S(1)} %pad_maximum_fusion.2.refs_0_), channel_id=1, source_target_pairs={{0,64},{2,34},{4,68},{6,38},{8,72},{10,42},{12,76},{14,46},{16,80}... | collective-permute-start | bytes 417800 | tf_op jit(solution)/shard_map/ppermute | solution.py:455
  31.8 10.3 %collective-permute-start.10 = (bf16[544,512]{1,0:T(8,128)(2,1)S(1)}, bf16[544,512]{1,0:T(8,128)(2,1)S(1)}, u32[]{:S(2)}, u32[]{:S(2)}) collective-permute-start(bf16[544,512]{1,0:T(8,128)(2,1)S(1)} %pack.1.refs_0_), channel_id=1, source_target_pairs={{0,32},{2,66},{4,36},{6,70},{8,40},{10,74},{12,44},{14,78},{16,48}... | collective-permute-start | bytes 1671176 | tf_op jit(solution)/shard_map/ppermute | solution.py:455
  33.1 14.3 %collective-permute-start.9 = (bf16[544,512]{1,0:T(8,128)(2,1)S(1)}, bf16[544,512]{1,0:T(8,128)(2,1)S(1)}, u32[]{:S(2)}, u32[]{:S(2)}) collective-permute-start(bf16[544,512]{1,0:T(8,128)(2,1)S(1)} %pack.1.refs_0_), channel_id=1, source_target_pairs={{0,33},{2,194},{4,37},{6,198},{8,41},{10,202},{12,45},{14,206},{16... | collective-permute-start | bytes 1671176 | tf_op jit(solution)/shard_map/ppermute | solution.py:455
  37.5 12.5 %collective-permute-start.8 = (bf16[544,512]{1,0:T(8,128)(2,1)S(1)}, bf16[544,512]{1,0:T(8,128)(2,1)S(1)}, u32[]{:S(2)}, u32[]{:S(2)}) collective-permute-start(bf16[544,512]{1,0:T(8,128)(2,1)S(1)} %pack.1.refs_0_), channel_id=1, source_target_pairs={{0,1},{2,130},{4,5},{6,134},{8,9},{10,138},{12,13},{14,142},{16,17... | collective-permute-start | bytes 1671176 | tf_op jit(solution)/shard_map/ppermute | solution.py:455
  55.1 13.0 %collective-permute-start.11 = (f32[1024,512]{1,0:T(8,128)S(1)}, f32[1024,512]{1,0:T(8,128)S(1)}, u32[]{:S(2)}, u32[]{:S(2)}) collective-permute-start(f32[1024,512]{1,0:T(8,128)S(1)} %get-tuple-element.102), channel_id=1, source_target_pairs={{0,2},{2,0},{4,6},{6,4},{8,10},{10,8},{12,14},{14,12},{16,18},{18,... | collective-permute-start | bytes 6291464 | tf_op jit(solution)/shard_map/ppermute | solution.py:455
  64.3 3.8 %copy-start = (f32[1024,512]{1,0:T(8,128)S(1)}, f32[1024,512]{1,0:T(8,128)}, u32[]{:S(2)}) copy-start(f32[1024,512]{1,0:T(8,128)} %refs_2_.1) | copy-start | bytes 6291460
  64.3 3.8 %copy-start.1 = (f32[1024,512]{1,0:T(8,128)S(1)}, f32[1024,512]{1,0:T(8,128)}, u32[]{:S(2)}) copy-start(f32[1024,512]{1,0:T(8,128)} %refs_3_.1) | copy-start | bytes 6291460
  64.3 3.8 %copy-start.2 = (f32[1024,512]{1,0:T(8,128)S(1)}, f32[1024,512]{1,0:T(8,128)}, u32[]{:S(2)}) copy-start(f32[1024,512]{1,0:T(8,128)} %refs_4_.1) | copy-start | bytes 6291460
  69.9 13.3 %collective-permute-start.12 = (bf16[1024,512]{1,0:T(8,128)(2,1)S(1)}, bf16[1024,512]{1,0:T(8,128)(2,1)S(1)}, u32[]{:S(2)}, u32[]{:S(2)}) collective-permute-start(bf16[1024,512]{1,0:T(8,128)(2,1)S(1)} %get-tuple-element.116.refs_3_.wb), channel_id=1, source_target_pairs={{0,2},{2,0},{4,6},{6,4},{8,10},{10,8},{12,14},{14,12},{16,18},{18,... | collective-permute-start | bytes 3145736 | tf_op jit(solution)/shard_map/ppermute | solution.py:455
  71.9 9.3 %collective-permute-start.13 = (bf16[512,512]{1,0:T(8,128)(2,1)S(1)}, bf16[512,512]{1,0:T(8,128)(2,1)S(1)}, u32[]{:S(2)}, u32[]{:S(2)}) collective-permute-start(bf16[512,512]{1,0:T(8,128)(2,1)S(1)} %terms.3), channel_id=1, source_target_pairs={{0,32},{2,35},{4,36},{6,39},{8,40},{10,43},{12,44},{14,47},{16,48}... | collective-permute-start | bytes 1572872 | tf_op jit(solution)/shard_map/ppermute | solution.py:455
  81.4 6.5 %collective-permute-start.14 = (bf16[256,512]{1,0:T(8,128)(2,1)S(1)}, bf16[256,512]{1,0:T(8,128)(2,1)S(1)}, u32[]{:S(2)}, u32[]{:S(2)}) collective-permute-start(bf16[256,512]{1,0:T(8,128)(2,1)S(1)} %slice.105), channel_id=1, source_target_pairs={{0,64},{2,194},{4,68},{6,198},{8,72},{10,202},{12,76},{14,206},{16... | collective-permute-start | bytes 786440 | tf_op jit(solution)/shard_map/ppermute | solution.py:455
  88.0 13.3 %collective-permute-start.16 = (bf16[256,512]{1,0:T(8,128)(2,1)S(1)}, bf16[256,512]{1,0:T(8,128)(2,1)S(1)}, u32[]{:S(2)}, u32[]{:S(2)}) collective-permute-start(bf16[256,512]{1,0:T(8,128)(2,1)S(1)} %get-tuple-element.161), channel_id=1, source_target_pairs={{0,96},{2,227},{4,100},{6,231},{8,104},{10,235},{12,108},{14,239},... | collective-permute-start | bytes 786440 | tf_op jit(solution)/shard_map/ppermute | solution.py:455
  91.5 9.8 %collective-permute-start.15 = (bf16[256,512]{1,0:T(8,128)(2,1)S(1)}, bf16[256,512]{1,0:T(8,128)(2,1)S(1)}, u32[]{:S(2)}, u32[]{:S(2)}) collective-permute-start(bf16[256,512]{1,0:T(8,128)(2,1)S(1)} %get-tuple-element.162), channel_id=1, source_target_pairs={{0,32},{2,35},{4,36},{6,39},{8,40},{10,43},{12,44},{14,47},{16,48}... | collective-permute-start | bytes 786440 | tf_op jit(solution)/shard_map/ppermute | solution.py:455
  95.7 6.5 %collective-permute-start.17 = (bf16[256,512]{1,0:T(8,128)(2,1)S(1)}, bf16[256,512]{1,0:T(8,128)(2,1)S(1)}, u32[]{:S(2)}, u32[]{:S(2)}) collective-permute-start(bf16[256,512]{1,0:T(8,128)(2,1)S(1)} %slice.104), channel_id=1, source_target_pairs={{0,64},{2,194},{4,68},{6,198},{8,72},{10,202},{12,76},{14,206},{16... | collective-permute-start | bytes 786440 | tf_op jit(solution)/shard_map/ppermute | solution.py:455
  102.2 15.2 %collective-permute-start.24 = (f32[1024,512]{1,0:T(8,128)S(1)}, f32[1024,512]{1,0:T(8,128)S(1)}, u32[]{:S(2)}, u32[]{:S(2)}) collective-permute-start(f32[1024,512]{1,0:T(8,128)S(1)} %get-tuple-element.144), channel_id=1, source_target_pairs={{0,2},{2,0},{4,6},{6,4},{8,10},{10,8},{12,14},{14,12},{16,18},{18,... | collective-permute-start | bytes 6291464 | tf_op jit(solution)/shard_map/ppermute | solution.py:455
  102.7 10.2 %collective-permute-start.20 = (bf16[4,2,16,512]{3,2,1,0:T(8,128)(2,1)S(1)}, bf16[4,2,16,512]{3,2,1,0:T(8,128)(2,1)S(1)}, u32[]{:S(2)}, u32[]{:S(2)}) collective-permute-start(bf16[4,2,16,512]{3,2,1,0:T(8,128)(2,1)S(1)} %get-tuple-element.158), channel_id=1, source_target_pairs={{0,216},{2,74},{4,220},{6,78},{8,192},{10,82},{12,196},{14,86},{16... | collective-permute-start | bytes 393224 | tf_op jit(solution)/shard_map/ppermute | solution.py:455
  102.8 10.2 %collective-permute-start.19 = (bf16[4,2,16,512]{3,2,1,0:T(8,128)(2,1)S(1)}, bf16[4,2,16,512]{3,2,1,0:T(8,128)(2,1)S(1)}, u32[]{:S(2)}, u32[]{:S(2)}) collective-permute-start(bf16[4,2,16,512]{3,2,1,0:T(8,128)(2,1)S(1)} %get-tuple-element.159), channel_id=1, source_target_pairs={{0,24},{2,10},{4,28},{6,14},{8,0},{10,18},{12,4},{14,22},{16,8},{1... | collective-permute-start | bytes 393224 | tf_op jit(solution)/shard_map/ppermute | solution.py:455
  106.1 6.8 %collective-permute-start.18 = (bf16[4,2,16,512]{3,2,1,0:T(8,128)(2,1)S(1)}, bf16[4,2,16,512]{3,2,1,0:T(8,128)(2,1)S(1)}, u32[]{:S(2)}, u32[]{:S(2)}) collective-permute-start(bf16[4,2,16,512]{3,2,1,0:T(8,128)(2,1)S(1)} %get-tuple-element.160), channel_id=1, source_target_pairs={{0,192},{2,66},{4,196},{6,70},{8,200},{10,74},{12,204},{14,78},{16... | collective-permute-start | bytes 393224 | tf_op jit(solution)/shard_map/ppermute | solution.py:455
  113.0 7.5 %collective-permute-start.23 = (f32[2,16,512]{2,1,0:T(8,128)S(1)}, f32[2,16,512]{2,1,0:T(8,128)S(1)}, u32[]{:S(2)}, u32[]{:S(2)}) collective-permute-start(f32[2,16,512]{2,1,0:T(8,128)S(1)} %get-tuple-element.163), channel_id=1, source_target_pairs={{0,26},{2,8},{4,30},{6,12},{8,2},{10,16},{12,6},{14,20},{16,10},{1... | collective-permute-start | bytes 196616 | tf_op jit(solution)/shard_map/ppermute | solution.py:455
  114.3 6.3 %collective-permute-start.22 = (f32[2,16,512]{2,1,0:T(8,128)S(1)}, f32[2,16,512]{2,1,0:T(8,128)S(1)}, u32[]{:S(2)}, u32[]{:S(2)}) collective-permute-start(f32[2,16,512]{2,1,0:T(8,128)S(1)} %get-tuple-element.164), channel_id=1, source_target_pairs={{0,28},{2,6},{4,0},{6,10},{8,4},{10,14},{12,8},{14,18},{16,12},{18... | collective-permute-start | bytes 196616 | tf_op jit(solution)/shard_map/ppermute | solution.py:455
  114.3 6.3 %collective-permute-start.21 = (f32[2,16,512]{2,1,0:T(8,128)S(1)}, f32[2,16,512]{2,1,0:T(8,128)S(1)}, u32[]{:S(2)}, u32[]{:S(2)}) collective-permute-start(f32[2,16,512]{2,1,0:T(8,128)S(1)} %get-tuple-element.165), channel_id=1, source_target_pairs={{0,30},{2,4},{4,2},{6,8},{8,6},{10,12},{12,10},{14,16},{16,14},{18... | collective-permute-start | bytes 196616 | tf_op jit(solution)/shard_map/ppermute | solution.py:455

commit v4 on v2

--- a/solution.py
+++ b/solution.py
@@ -337,7 +337,7 @@
     )(own, other, wb_own, wb_other)
 
 
-def rest_kernel(most, q_ref, pos_ref, wb_ref, resid_ref, out_ref, *, half):
+def rest_kernel(most, q_ref, pos_ref, wb_ref, old_ref, resid_ref, *out_ref, half):
     blocks = remaining()
 
     @pl.loop(0, len(blocks) // 2)
@@ -346,21 +346,23 @@
             fill_block(q_ref, pos_ref, wb_ref, resid_ref, half, chosen(blocks, 2 * i + k))
 
     finish(most, pos_ref, ((half, resid_ref),), blocks)
-    fill_grad(resid_ref, q_ref, out_ref)
-
-
-def rest_gradient(most, q, pos, wb, resid, half):
+    for ref in out_ref:
+        fill_grad(resid_ref, q_ref, ref)
+
+
+def rest(most, q, pos, wb, resid, half, grad):
     size = LAB * 4 * BLOCK
-    return pl.pallas_call(
-        lambda most, q, pos, wb, old, resid, out: rest_kernel(most, q, pos, wb, resid, out, half=half),
-        out_shape=(jax.ShapeDtypeStruct((LAB, NQ), bf16), jax.ShapeDtypeStruct((LAB, D), f32)),
+    shapes = (jax.ShapeDtypeStruct((LAB, NQ), bf16), jax.ShapeDtypeStruct((LAB, D), f32))[: 1 + grad]
+    return pl.pallas_call(
+        lambda *refs: rest_kernel(*refs, half=half),
+        out_shape=shapes,
         in_specs=[spec()] * 5,
-        out_specs=(spec(),) * 2,
+        out_specs=(spec(),) * len(shapes),
         input_output_aliases={4: 0},
         compiler_params=params(),
-        cost_estimate=cost(6 * size * D, 8 * size, 2 * size),
+        cost_estimate=cost((2 + 4 * grad) * size * D, 8 * size, 2 * size),
         name="rest",
-    )(most, q, pos, wb, resid)[1]
+    )(most, q, pos, wb, resid)[-1]
 
 
 def grad_kernel(resid_ref, q_ref, out_ref):
@@ -538,8 +540,9 @@
     part0 = part0 + out0.astype(f32)
     half0 = send(part0[BLOCK:].astype(bf16), first_x)
 
-    part1, part0, other = after(part1, part0, other)
-    theirs = rest_gradient(most, q, pos, wb_other, other, 1)
+    part1, part0, other, own = after(part1, part0, other, own)
+    theirs = rest(most, q, pos, wb_other, other, 1, True)
+    own = rest(most, q, pos, wb, own, 0, False)
     *got, half0, theirs, own = after(*got, half0, theirs, own)
     part = swap(theirs)
     pair0 = part0[:BLOCK] + half0.astype(f32)
@@ -549,7 +552,7 @@
     far = lines.astype(bf16)
     got = [send(far[1, :4], second_x), send(far[0, 4:], onward(4)), send(far[1, 4:], then(second_x, onward(4)))]
     lines, own = after(lines, own)
-    mine = rest_gradient(most, q, pos, wb, own, 0)
+    mine = gradient(own, q)
     *got, mine = after(*got, mine)
     line = lines[0, :4] + got[0].astype(f32) + got[1].astype(f32) + got[2].astype(f32)
 

time: 114 us -> 115 us (level)
    pallas_call x1 -> x2, Pallas kernels: 2.32 us -> 4.66 us  [gradient(): pl.pallas_call(grad_kernel, out_shape=jax.ShapeDtypeStruct((LAB, D), f32)...]
    pallas_call x2, Pallas kernels: 8.91 us -> 6.58 us  [rest(): pl.pallas_call(lambda *refs: rest_kernel(*refs, half=half), out_shape=sha...]
  transfers between devices with their start and end apart: 25 -> 25, of which waited for: 8 -> 9; matrix products, arithmetic and copies ran while one was open for 3% -> 3% of each run, Pallas kernels for 28% -> 28%
where the time goes in v4:
time: 115 us; the launch traced here: 114 us
  starting transfers between devices  48.5 us (42%)
  Pallas kernels  39.3 us (34%)
  waiting for transfers between devices  19.3 us (17%)
  other arithmetic  3.25 us (3%)
  local copies, waits for them, and re-layouts  2.67 us (2%)
    ppermute x25, starting transfers between devices, send(): return lax.ppermute(array, AXES, moved(move))  48.5 us
    ppermute x25, waiting for transfers between devices, send(): return lax.ppermute(array, AXES, moved(move))  19.3 us
    pallas_call x4, Pallas kernels, first_residuals(): pl.pallas_call(lambda *refs: part_kernel(*refs, late=late), out_shape=sha...  12.8 us
    pallas_call x2, Pallas kernels, plane_terms(): pl.pallas_call(lambda *refs: plane_kernel(*refs, blocks=blocks), out_shap...  7 us
    pallas_call x2, Pallas kernels, rest(): pl.pallas_call(lambda *refs: rest_kernel(*refs, half=half), out_shape=sha...  6.58 us
    pallas_call x2, Pallas kernels, update(): pl.pallas_call(lambda *refs: kernel(count, *refs), out_shape=(full, full,...  4.94 us
    pallas_call x2, Pallas kernels, gradient(): pl.pallas_call(grad_kernel, out_shape=jax.ShapeDtypeStruct((LAB, D), f32)...  4.66 us
    pallas_call x2, Pallas kernels, terms(): pl.pallas_call(lambda *refs: terms_kernel(*refs, blocks=blocks), out_shap...  3.03 us
  transfers between devices with their start and end apart: 25, of which 9 were waited for; matrix products, arithmetic and copies ran while one was open for 3% of the time, Pallas kernels for 28%

profile of v4, /device:TPU:1, one launch (start us, length us, event | category | flops | bytes accessed | tf_op | source)
XLA Modules:
  0.0 114.1 jit_solution(7763035326672416893)
XLA Ops:
  2.4 4.5 %collective-permute-start.2 = (bf16[16,640]{0,1:T(8,128)(2,1)S(1)}, bf16[16,640]{0,1:T(8,128)(2,1)S(1)}, u32[]{:S(2)}, u32[]{:S(2)}) collective-permute-start(bf16[16,640]{0,1:T(8,128)(2,1)S(1)} %copy.32), channel_id=1, source_target_pairs={{0,26},{2,8},{4,30},{6,12},{8,2},{10,16},{12,6},{14,20},{16,10},{1... | collective-permute-start | bytes 61448 | tf_op jit(solution)/shard_map/ppermute | solution.py:451
  6.9 2.1 %collective-permute-start.1 = (bf16[16,640]{0,1:T(8,128)(2,1)S(1)}, bf16[16,640]{0,1:T(8,128)(2,1)S(1)}, u32[]{:S(2)}, u32[]{:S(2)}) collective-permute-start(bf16[16,640]{0,1:T(8,128)(2,1)S(1)} %copy.32), channel_id=1, source_target_pairs={{0,4},{2,30},{4,8},{6,2},{8,12},{10,6},{12,16},{14,10},{16,20},{18... | collective-permute-start | bytes 61448 | tf_op jit(solution)/shard_map/ppermute | solution.py:451
  10.4 1.7 %convert_element_type.34.refs_1_.refs_2_ = bf16[1024,512]{1,0:T(8,128)(2,1)S(1)} convert(f32[1024,512]{1,0:T(8,128)} %refs_2_.1) | non-fusion elementwise | flops 524288 | bytes 3145728 | tf_op jit(solution)/shard_map/convert_element_type | solution.py:510
  13.7 1.8 %collective-permute-done = bf16[16,640]{0,1:T(8,128)(2,1)S(1)} collective-permute-done((bf16[16,640]{0,1:T(8,128)(2,1)S(1)}, bf16[16,640]{0,1:T(8,128)(2,1)S(1)}, u32[]{:S(2)}, u32[]{:S(2)}) %collective-permute-start) | collective-permute-done | bytes 20512 | tf_op jit(solution)/shard_map/ppermute | solution.py:451
  15.7 3.5 %collective-permute-start.3 = (bf16[64,640]{0,1:T(8,128)(2,1)S(1)}, bf16[64,640]{0,1:T(8,128)(2,1)S(1)}, u32[]{:S(2)}, u32[]{:S(2)}) collective-permute-start(bf16[64,640]{0,1:T(8,128)(2,1)S(1)} %pad_maximum_fusion.1), channel_id=1, source_target_pairs={{0,8},{2,26},{4,12},{6,30},{8,16},{10,2},{12,20},{14,6},{16,24},{1... | collective-permute-start | bytes 245768 | tf_op jit(solution)/shard_map/ppermute | solution.py:451
  19.2 3.9 %collective-permute-done.3 = bf16[64,640]{0,1:T(8,128)(2,1)S(1)} collective-permute-done((bf16[64,640]{0,1:T(8,128)(2,1)S(1)}, bf16[64,640]{0,1:T(8,128)(2,1)S(1)}, u32[]{:S(2)}, u32[]{:S(2)}) %collective-permute-start.3) | collective-permute-done | bytes 81952 | tf_op jit(solution)/shard_map/ppermute | solution.py:451
  23.6 3.0 %collective-permute-start.6 = (bf16[136,512]{1,0:T(8,128)(2,1)S(1)}, bf16[136,512]{1,0:T(8,128)(2,1)S(1)}, u32[]{:S(2)}, u32[]{:S(2)}) collective-permute-start(bf16[136,512]{1,0:T(8,128)(2,1)S(1)} %pad_maximum_fusion.2.refs_0_), channel_id=1, source_target_pairs={{0,128},{2,3},{4,132},{6,7},{8,136},{10,11},{12,140},{14,15},{16,1... | collective-permute-start | bytes 417800 | tf_op jit(solution)/shard_map/ppermute | solution.py:451
  27.4 1.7 %collective-permute-done.6.refs_3_ = bf16[136,512]{1,0:T(8,128)(2,1)S(1)} collective-permute-done((bf16[136,512]{1,0:T(8,128)(2,1)S(1)}, bf16[136,512]{1,0:T(8,128)(2,1)S(1)}, u32[]{:S(2)}, u32[]{:S(2)}) %collective-permute-start.6) | collective-permute-done | bytes 139296 | tf_op jit(solution)/shard_map/ppermute | solution.py:451
  29.1 2.6 %collective-permute-done.5.refs_2_ = bf16[136,512]{1,0:T(8,128)(2,1)S(1)} collective-permute-done((bf16[136,512]{1,0:T(8,128)(2,1)S(1)}, bf16[136,512]{1,0:T(8,128)(2,1)S(1)}, u32[]{:S(2)}, u32[]{:S(2)}) %collective-permute-start.5) | collective-permute-done | bytes 139296 | tf_op jit(solution)/shard_map/ppermute | solution.py:451
  33.0 1.8 %collective-permute-start.9 = (bf16[544,512]{1,0:T(8,128)(2,1)S(1)}, bf16[544,512]{1,0:T(8,128)(2,1)S(1)}, u32[]{:S(2)}, u32[]{:S(2)}) collective-permute-start(bf16[544,512]{1,0:T(8,128)(2,1)S(1)} %pack.1.refs_0_), channel_id=1, source_target_pairs={{0,33},{2,194},{4,37},{6,198},{8,41},{10,202},{12,45},{14,206},{16... | collective-permute-start | bytes 1671176 | tf_op jit(solution)/shard_map/ppermute | solution.py:451
  34.9 2.6 %part.4 = (bf16[2048,512]{1,0:T(8,128)(2,1)S(1)}, s32[2,8,2048]{2,1,0:T(8,128)S(1)}, bf16[1024,2048]{1,0:T(8,128)(2,1)S(1)}, bf16[1024,2048]{1,0:T(8,128)(2,1)S(1)}, f32[8,128]{1,0:T(8,128)S(1)}) custom-call(bf16[544,512]{1,0:T(8,128)(2,1)S(1)} %pack.1.refs_0_, bf16[1024,512]{1,0:T(8,128)(2,1)S(1)} %convert_element_type.34.refs_1_.refs_2_, ...), custom_call_target="tpu_custom_call" | custom-call | flops 1073741824 | bytes 2097152 | tf_op jit(solution)/shard_map/part/pallas_call | solution.py:188
  38.2 3.8 %collective-permute-done.10.refs_0_ = bf16[544,512]{1,0:T(8,128)(2,1)S(1)} collective-permute-done((bf16[544,512]{1,0:T(8,128)(2,1)S(1)}, bf16[544,512]{1,0:T(8,128)(2,1)S(1)}, u32[]{:S(2)}, u32[]{:S(2)}) %collective-permute-start.10) | collective-permute-done | bytes 557088 | tf_op jit(solution)/shard_map/ppermute | solution.py:451
  42.0 2.6 %part.5 = (bf16[2048,512]{1,0:T(8,128)(2,1)S(1)}, s32[2,8,2048]{2,1,0:T(8,128)S(1)}, bf16[1024,2048]{1,0:T(8,128)(2,1)S(1)}, bf16[1024,2048]{1,0:T(8,128)(2,1)S(1)}, f32[8,128]{1,0:T(8,128)S(1)}) custom-call(bf16[544,512]{1,0:T(8,128)(2,1)S(1)} %collective-permute-done.10.refs_0_, ...), custom_call_target="tpu_custom_call", output_to_operand_aliasing={{0}: (3, {}), {1}: (4, {}), {2}: (5, {}), {3}: (6, {}), {4}... | custom-call | flops 1073741824 | bytes 2097152 | tf_op jit(solution)/shard_map/part/pallas_call | solution.py:188
  44.6 2.7 %collective-permute-done.9.refs_0_ = bf16[544,512]{1,0:T(8,128)(2,1)S(1)} collective-permute-done((bf16[544,512]{1,0:T(8,128)(2,1)S(1)}, bf16[544,512]{1,0:T(8,128)(2,1)S(1)}, u32[]{:S(2)}, u32[]{:S(2)}) %collective-permute-start.9) | collective-permute-done | bytes 557088 | tf_op jit(solution)/shard_map/ppermute | solution.py:451
  47.3 2.6 %part.6 = (bf16[2048,512]{1,0:T(8,128)(2,1)S(1)}, s32[2,8,2048]{2,1,0:T(8,128)S(1)}, bf16[1024,2048]{1,0:T(8,128)(2,1)S(1)}, bf16[1024,2048]{1,0:T(8,128)(2,1)S(1)}, f32[8,128]{1,0:T(8,128)S(1)}) custom-call(bf16[544,512]{1,0:T(8,128)(2,1)S(1)} %collective-permute-done.9.refs_0_, ...), custom_call_target="tpu_custom_call", output_to_operand_aliasing={{0}: (3, {}), {1}: (4, {}), {2}: (5, {}), {3}: (6, {}), {4}... | custom-call | flops 1073741824 | bytes 2097152 | tf_op jit(solution)/shard_map/part/pallas_call | solution.py:188
  49.9 5.1 %part.7 = (bf16[2048,512]{1,0:T(8,128)(2,1)S(1)}, s32[2,8,2048]{2,1,0:T(8,128)S(1)}, bf16[1024,2048]{1,0:T(8,128)(2,1)S(1)}, bf16[1024,2048]{1,0:T(8,128)(2,1)S(...) custom-call(bf16[544,512]{1,0:T(8,128)(2,1)S(1)} %collective-permute, ...), custom_call_target="tpu_custom_call", output_to_operand_aliasing={{0}: (3, {}), {1}: (4, {}), {2}: (5, {}), {3}: (6, {}), {4}... | custom-call | flops 2147483648 | bytes 2097152 | tf_op jit(solution)/shard_map/part/pallas_call | solution.py:188
  55.0 9.2 %collective-permute-start.11 = (f32[1024,512]{1,0:T(8,128)S(1)}, f32[1024,512]{1,0:T(8,128)S(1)}, u32[]{:S(2)}, u32[]{:S(2)}) collective-permute-start(f32[1024,512]{1,0:T(8,128)S(1)} %get-tuple-element.106), channel_id=1, source_target_pairs={{0,2},{2,0},{4,6},{6,4},{8,10},{10,8},{12,14},{14,12},{16,18},{18,... | collective-permute-start | bytes 6291464 | tf_op jit(solution)/shard_map/ppermute | solution.py:451
  65.8 2.3 %grad.2.refs_0_ = f32[1024,512]{1,0:T(8,128)S(1)} custom-call(bf16[1024,2048]{1,0:T(8,128)(2,1)S(1)} %get-tuple-element.118.resid_ref.refs_0_, bf16[2048,512]{1,0:T(8,128)(2,1)S(1)} %get-tuple-element.108.q_ref.refs_1_), custom_call_target="tpu_custom_call" | custom-call | flops 2147483648 | bytes 8388608 | tf_op jit(solution)/shard_map/grad/pallas_call | solution.py:373
  68.7 1.8 %adamw.2 = (f32[1024,512]{1,0:T(8,128)S(1)}, f32[1024,512]{1,0:T(8,128)S(1)}, f32[1024,512]{1,0:T(8,128)S(1)}, bf16[1024,512]{1,0:T(8,128)(2,1)S(1)}) custom-call(f32[1024,512]{1,0:T(8,128)S(1)} %grad.2.refs_0_, f32[1024,512]{1,0:T(8,128)S(1)} %collective-permute-done.11.refs_1_, f32[1024,512]{1,0:T(8,128)S(1)} %copy-done, f32[1024,512]{1,0:T(8,128)S(1)} %copy-done.1, ...), custom_call_target="tpu_custom_call" | custom-call | flops 10485760 | bytes 6291456 | tf_op jit(solution)/shard_map/adamw/pallas_call | solution.py:424
  70.5 2.0 %collective-permute-start.12 = (bf16[512,512]{1,0:T(8,128)(2,1)S(1)}, bf16[512,512]{1,0:T(8,128)(2,1)S(1)}, u32[]{:S(2)}, u32[]{:S(2)}) collective-permute-start(bf16[512,512]{1,0:T(8,128)(2,1)S(1)} %terms.2), channel_id=1, source_target_pairs={{0,32},{2,35},{4,36},{6,39},{8,40},{10,43},{12,44},{14,47},{16,48}... | collective-permute-start | bytes 1572872 | tf_op jit(solution)/shard_map/ppermute | solution.py:451
  74.1 3.5 %plane.2 = (bf16[1024,2048]{1,0:T(8,128)(2,1)S(1)}, bf16[1024,2048]{1,0:T(8,128)(2,1)S(1)}, bf16[512,512]{1,0:T(8,128)(2,1)S(1)}) custom-call(f32[8,128]{1,0:T(8,128)S(1)} %get-tuple-element.115.refs_0_, bf16[2048,512]{1,0:T(8,128)(2,1)S(1)} %get-tuple-element.108.q_ref.refs_1_, s32[2,8,2048]{2,1,0:T(8,128)S(1)} %get-tuple-element.116.refs_2_, ...), custom_call_target="tpu_custom_call" | custom-call | flops 2147483648 | bytes 4194304 | tf_op jit(solution)/shard_map/plane/pallas_call | solution.py:312
  77.7 2.6 %collective-permute-start.15 = (bf16[256,512]{1,0:T(8,128)(2,1)S(1)}, bf16[256,512]{1,0:T(8,128)(2,1)S(1)}, u32[]{:S(2)}, u32[]{:S(2)}) collective-permute-start(bf16[256,512]{1,0:T(8,128)(2,1)S(1)} %get-tuple-element.169), channel_id=1, source_target_pairs={{0,96},{2,227},{4,100},{6,231},{8,104},{10,235},{12,108},{14,239},... | collective-permute-start | bytes 786440 | tf_op jit(solution)/shard_map/ppermute | solution.py:451
  81.9 3.5 %plane.3 = (bf16[1024,2048]{1,0:T(8,128)(2,1)S(1)}, bf16[1024,2048]{1,0:T(8,128)(2,1)S(1)}, f32[512,512]{1,0:T(8,128)S(1)}) custom-call(f32[8,128]{1,0:T(8,128)S(1)} %get-tuple-element.115.refs_0_, bf16[2048,512]{1,0:T(8,128)(2,1)S(1)} %get-tuple-element.108.q_ref.refs_1_, ...), custom_call_target="tpu_custom_call", output_to_operand_aliasing={{0}: (5, {}), {1}: (6, {})} | custom-call | flops 2147483648 | bytes 4194304 | tf_op jit(solution)/shard_map/plane/pallas_call | solution.py:312
  86.7 1.8 %collective-permute-start.17 = (bf16[256,512]{1,0:T(8,128)(2,1)S(1)}, bf16[256,512]{1,0:T(8,128)(2,1)S(1)}, u32[]{:S(2)}, u32[]{:S(2)}) collective-permute-start(bf16[256,512]{1,0:T(8,128)(2,1)S(1)} %slice.104), channel_id=1, source_target_pairs={{0,64},{2,194},{4,68},{6,198},{8,72},{10,202},{12,76},{14,206},{16... | collective-permute-start | bytes 786440 | tf_op jit(solution)/shard_map/ppermute | solution.py:451
  88.4 2.2 %rest.3.resid_ref = bf16[1024,2048]{1,0:T(8,128)(2,1)S(1)} custom-call(f32[8,128]{1,0:T(8,128)S(1)} %get-tuple-element.115.refs_0_, bf16[2048,512]{1,0:T(8,128)(2,1)S(1)} %get-tuple-element.108.q_ref.refs_1_, s32[2,8,2048]{2,1,0:T(8,128)S(1)} %get-tuple-element.116.refs_2_, ...), custom_call_target="tpu_custom_call", output_to_operand_aliasing={{}: (4, {})} | custom-call | flops 1073741824 | bytes 8388608 | tf_op jit(solution)/shard_map/rest/pallas_call | solution.py:356
  90.7 4.4 %rest.2 = (bf16[1024,2048]{1,0:T(8,128)(2,1)S(1)}, f32[1024,512]{1,0:T(8,128)S(1)}) custom-call(f32[8,128]{1,0:T(8,128)S(1)} %get-tuple-element.115.refs_0_, bf16[2048,512]{1,0:T(8,128)(2,1)S(1)} %get-tuple-element.108.q_ref.refs_1_, s32[2,8,2048]{2,1,0:T(8,128)S(1)} %get-tuple-element.116.refs_2_, ...), custom_call_target="tpu_custom_call", output_to_operand_aliasing={{0}: (4, {})} | custom-call | flops 3221225472 | bytes 8388608 | tf_op jit(solution)/shard_map/rest/pallas_call | solution.py:356
  95.7 2.8 %collective-permute-start.19 = (bf16[4,2,16,512]{3,2,1,0:T(8,128)(2,1)S(1)}, bf16[4,2,16,512]{3,2,1,0:T(8,128)(2,1)S(1)}, u32[]{:S(2)}, u32[]{:S(2)}) collective-permute-start(bf16[4,2,16,512]{3,2,1,0:T(8,128)(2,1)S(1)} %get-tuple-element.167), channel_id=1, source_target_pairs={{0,24},{2,10},{4,28},{6,14},{8,0},{10,18},{12,4},{14,22},{16,8},{1... | collective-permute-start | bytes 393224 | tf_op jit(solution)/shard_map/ppermute | solution.py:451
  98.5 2.9 %collective-permute-start.18 = (bf16[4,2,16,512]{3,2,1,0:T(8,128)(2,1)S(1)}, bf16[4,2,16,512]{3,2,1,0:T(8,128)(2,1)S(1)}, u32[]{:S(2)}, u32[]{:S(2)}) collective-permute-start(bf16[4,2,16,512]{3,2,1,0:T(8,128)(2,1)S(1)} %get-tuple-element.168), channel_id=1, source_target_pairs={{0,192},{2,66},{4,196},{6,70},{8,200},{10,74},{12,204},{14,78},{16... | collective-permute-start | bytes 393224 | tf_op jit(solution)/shard_map/ppermute | solution.py:451
  101.4 2.3 %grad.3.refs_0_ = f32[1024,512]{1,0:T(8,128)S(1)} custom-call(bf16[1024,2048]{1,0:T(8,128)(2,1)S(1)} %rest.3.resid_ref, bf16[2048,512]{1,0:T(8,128)(2,1)S(1)} %get-tuple-element.108.q_ref.refs_1_), custom_call_target="tpu_custom_call" | custom-call | flops 2147483648 | bytes 8388608 | tf_op jit(solution)/shard_map/grad/pallas_call | solution.py:373
  105.5 1.7 %collective-permute-start.23 = (f32[2,16,512]{2,1,0:T(8,128)S(1)}, f32[2,16,512]{2,1,0:T(8,128)S(1)}, u32[]{:S(2)}, u32[]{:S(2)}) collective-permute-start(f32[2,16,512]{2,1,0:T(8,128)S(1)} %get-tuple-element.171), channel_id=1, source_target_pairs={{0,26},{2,8},{4,30},{6,12},{8,2},{10,16},{12,6},{14,20},{16,10},{1... | collective-permute-start | bytes 196616 | tf_op jit(solution)/shard_map/ppermute | solution.py:451
  107.1 3.0 %collective-permute-start.21 = (f32[2,16,512]{2,1,0:T(8,128)S(1)}, f32[2,16,512]{2,1,0:T(8,128)S(1)}, u32[]{:S(2)}, u32[]{:S(2)}) collective-permute-start(f32[2,16,512]{2,1,0:T(8,128)S(1)} %get-tuple-element.173), channel_id=1, source_target_pairs={{0,30},{2,4},{4,2},{6,8},{8,6},{10,12},{12,10},{14,16},{16,14},{18... | collective-permute-start | bytes 196616 | tf_op jit(solution)/shard_map/ppermute | solution.py:451
  110.2 3.2 %adamw.3 = (f32[1024,512]{1,0:T(8,128)}, f32[1024,512]{1,0:T(8,128)}, f32[1024,512]{1,0:T(8,128)}) custom-call(f32[1024,512]{1,0:T(8,128)S(1)} %grad.3.refs_0_, f32[1024,512]{1,0:T(8,128)S(1)} %collective-permute-done.24.refs_1_, f32[1024,512]{1,0:T(8,128)S(1)} %get-tuple-element.153.refs_2_, f32[1024,512]{1,0:T(8,128)S(1)} %get-tuple-element.154.refs_3_, ...), custom_call_target="tpu_custom_call" | custom-call | flops 10485760 | bytes 6291456 | tf_op jit(solution)/shard_map/adamw/pallas_call | solution.py:424
  (65 shorter events, 17.8 us)
Async XLA Ops:
  0.6 0.7 copy-start.3
  1.3 0.7 copy-start.4
  2.4 10.2 %collective-permute-start.2 = (bf16[16,640]{0,1:T(8,128)(2,1)S(1)}, bf16[16,640]{0,1:T(8,128)(2,1)S(1)}, u32[]{:S(2)}, u32[]{:S(2)}) collective-permute-start(bf16[16,640]{0,1:T(8,128)(2,1)S(1)} %copy.32), channel_id=1, source_target_pairs={{0,26},{2,8},{4,30},{6,12},{8,2},{10,16},{12,6},{14,20},{16,10},{1... | collective-permute-start | bytes 61448 | tf_op jit(solution)/shard_map/ppermute | solution.py:451
  6.9 6.8 %collective-permute-start.1 = (bf16[16,640]{0,1:T(8,128)(2,1)S(1)}, bf16[16,640]{0,1:T(8,128)(2,1)S(1)}, u32[]{:S(2)}, u32[]{:S(2)}) collective-permute-start(bf16[16,640]{0,1:T(8,128)(2,1)S(1)} %copy.32), channel_id=1, source_target_pairs={{0,4},{2,30},{4,8},{6,2},{8,12},{10,6},{12,16},{14,10},{16,20},{18... | collective-permute-start | bytes 61448 | tf_op jit(solution)/shard_map/ppermute | solution.py:451
  9.0 6.5 %collective-permute-start = (bf16[16,640]{0,1:T(8,128)(2,1)S(1)}, bf16[16,640]{0,1:T(8,128)(2,1)S(1)}, u32[]{:S(2)}, u32[]{:S(2)}) collective-permute-start(bf16[16,640]{0,1:T(8,128)(2,1)S(1)} %copy.32), channel_id=1, source_target_pairs={{0,30},{2,4},{4,2},{6,8},{8,6},{10,12},{12,10},{14,16},{16,14},{18... | collective-permute-start | bytes 61448 | tf_op jit(solution)/shard_map/ppermute | solution.py:451
  12.1 22.8 %collective-permute-start.7 = (bf16[1024,512]{1,0:T(8,128)(2,1)S(1)}, bf16[1024,512]{1,0:T(8,128)(2,1)S(1)}, u32[]{:S(2)}, u32[]{:S(2)}) collective-permute-start(bf16[1024,512]{1,0:T(8,128)(2,1)S(1)} %convert_element_type.34.refs_1_.refs_2_), channel_id=1, source_target_pairs={{0,2},{2,0},{4,6},{6,4},{8,10},{10,8},{12,14},{14,12},{16,18},{18,... | collective-permute-start | bytes 3145736 | tf_op jit(solution)/shard_map/ppermute | solution.py:451
  15.7 7.4 %collective-permute-start.3 = (bf16[64,640]{0,1:T(8,128)(2,1)S(1)}, bf16[64,640]{0,1:T(8,128)(2,1)S(1)}, u32[]{:S(2)}, u32[]{:S(2)}) collective-permute-start(bf16[64,640]{0,1:T(8,128)(2,1)S(1)} %pad_maximum_fusion.1), channel_id=1, source_target_pairs={{0,8},{2,26},{4,12},{6,30},{8,16},{10,2},{12,20},{14,6},{16,24},{1... | collective-permute-start | bytes 245768 | tf_op jit(solution)/shard_map/ppermute | solution.py:451
  23.6 5.5 %collective-permute-start.6 = (bf16[136,512]{1,0:T(8,128)(2,1)S(1)}, bf16[136,512]{1,0:T(8,128)(2,1)S(1)}, u32[]{:S(2)}, u32[]{:S(2)}) collective-permute-start(bf16[136,512]{1,0:T(8,128)(2,1)S(1)} %pad_maximum_fusion.2.refs_0_), channel_id=1, source_target_pairs={{0,128},{2,3},{4,132},{6,7},{8,136},{10,11},{12,140},{14,15},{16,1... | collective-permute-start | bytes 417800 | tf_op jit(solution)/shard_map/ppermute | solution.py:451
  26.6 5.1 %collective-permute-start.5 = (bf16[136,512]{1,0:T(8,128)(2,1)S(1)}, bf16[136,512]{1,0:T(8,128)(2,1)S(1)}, u32[]{:S(2)}, u32[]{:S(2)}) collective-permute-start(bf16[136,512]{1,0:T(8,128)(2,1)S(1)} %pad_maximum_fusion.2.refs_0_), channel_id=1, source_target_pairs={{0,192},{2,35},{4,196},{6,39},{8,200},{10,43},{12,204},{14,47},{16... | collective-permute-start | bytes 417800 | tf_op jit(solution)/shard_map/ppermute | solution.py:451
  27.4 4.3 %collective-permute-start.4 = (bf16[136,512]{1,0:T(8,128)(2,1)S(1)}, bf16[136,512]{1,0:T(8,128)(2,1)S(1)}, u32[]{:S(2)}, u32[]{:S(2)}) collective-permute-start(bf16[136,512]{1,0:T(8,128)(2,1)S(1)} %pad_maximum_fusion.2.refs_0_), channel_id=1, source_target_pairs={{0,64},{2,34},{4,68},{6,38},{8,72},{10,42},{12,76},{14,46},{16,80}... | collective-permute-start | bytes 417800 | tf_op jit(solution)/shard_map/ppermute | solution.py:451
  31.8 10.3 %collective-permute-start.10 = (bf16[544,512]{1,0:T(8,128)(2,1)S(1)}, bf16[544,512]{1,0:T(8,128)(2,1)S(1)}, u32[]{:S(2)}, u32[]{:S(2)}) collective-permute-start(bf16[544,512]{1,0:T(8,128)(2,1)S(1)} %pack.1.refs_0_), channel_id=1, source_target_pairs={{0,32},{2,66},{4,36},{6,70},{8,40},{10,74},{12,44},{14,78},{16,48}... | collective-permute-start | bytes 1671176 | tf_op jit(solution)/shard_map/ppermute | solution.py:451
  33.0 14.3 %collective-permute-start.9 = (bf16[544,512]{1,0:T(8,128)(2,1)S(1)}, bf16[544,512]{1,0:T(8,128)(2,1)S(1)}, u32[]{:S(2)}, u32[]{:S(2)}) collective-permute-start(bf16[544,512]{1,0:T(8,128)(2,1)S(1)} %pack.1.refs_0_), channel_id=1, source_target_pairs={{0,33},{2,194},{4,37},{6,198},{8,41},{10,202},{12,45},{14,206},{16... | collective-permute-start | bytes 1671176 | tf_op jit(solution)/shard_map/ppermute | solution.py:451
  37.4 12.5 %collective-permute-start.8 = (bf16[544,512]{1,0:T(8,128)(2,1)S(1)}, bf16[544,512]{1,0:T(8,128)(2,1)S(1)}, u32[]{:S(2)}, u32[]{:S(2)}) collective-permute-start(bf16[544,512]{1,0:T(8,128)(2,1)S(1)} %pack.1.refs_0_), channel_id=1, source_target_pairs={{0,1},{2,130},{4,5},{6,134},{8,9},{10,138},{12,13},{14,142},{16,17... | collective-permute-start | bytes 1671176 | tf_op jit(solution)/shard_map/ppermute | solution.py:451
  55.0 13.1 %collective-permute-start.11 = (f32[1024,512]{1,0:T(8,128)S(1)}, f32[1024,512]{1,0:T(8,128)S(1)}, u32[]{:S(2)}, u32[]{:S(2)}) collective-permute-start(f32[1024,512]{1,0:T(8,128)S(1)} %get-tuple-element.106), channel_id=1, source_target_pairs={{0,2},{2,0},{4,6},{6,4},{8,10},{10,8},{12,14},{14,12},{16,18},{18,... | collective-permute-start | bytes 6291464 | tf_op jit(solution)/shard_map/ppermute | solution.py:451
  65.8 2.4 %copy-start = (f32[1024,512]{1,0:T(8,128)S(1)}, f32[1024,512]{1,0:T(8,128)}, u32[]{:S(2)}) copy-start(f32[1024,512]{1,0:T(8,128)} %refs_2_.1) | copy-start | bytes 6291460
  65.8 2.4 %copy-start.1 = (f32[1024,512]{1,0:T(8,128)S(1)}, f32[1024,512]{1,0:T(8,128)}, u32[]{:S(2)}) copy-start(f32[1024,512]{1,0:T(8,128)} %refs_3_.1) | copy-start | bytes 6291460
  65.8 2.8 %copy-start.2 = (f32[1024,512]{1,0:T(8,128)S(1)}, f32[1024,512]{1,0:T(8,128)}, u32[]{:S(2)}) copy-start(f32[1024,512]{1,0:T(8,128)} %refs_4_.1) | copy-start | bytes 6291460
  70.4 3.7 %collective-permute-start.13 = (bf16[1024,512]{1,0:T(8,128)(2,1)S(1)}, bf16[1024,512]{1,0:T(8,128)(2,1)S(1)}, u32[]{:S(2)}, u32[]{:S(2)}) collective-permute-start(bf16[1024,512]{1,0:T(8,128)(2,1)S(1)} %get-tuple-element.117.refs_3_), channel_id=1, source_target_pairs={{0,2},{2,0},{4,6},{6,4},{8,10},{10,8},{12,14},{14,12},{16,18},{18,... | collective-permute-start | bytes 3145736 | tf_op jit(solution)/shard_map/ppermute | solution.py:451
  70.5 14.9 %collective-permute-start.12 = (bf16[512,512]{1,0:T(8,128)(2,1)S(1)}, bf16[512,512]{1,0:T(8,128)(2,1)S(1)}, u32[]{:S(2)}, u32[]{:S(2)}) collective-permute-start(bf16[512,512]{1,0:T(8,128)(2,1)S(1)} %terms.2), channel_id=1, source_target_pairs={{0,32},{2,35},{4,36},{6,39},{8,40},{10,43},{12,44},{14,47},{16,48}... | collective-permute-start | bytes 1572872 | tf_op jit(solution)/shard_map/ppermute | solution.py:451
  77.7 17.4 %collective-permute-start.15 = (bf16[256,512]{1,0:T(8,128)(2,1)S(1)}, bf16[256,512]{1,0:T(8,128)(2,1)S(1)}, u32[]{:S(2)}, u32[]{:S(2)}) collective-permute-start(bf16[256,512]{1,0:T(8,128)(2,1)S(1)} %get-tuple-element.169), channel_id=1, source_target_pairs={{0,96},{2,227},{4,100},{6,231},{8,104},{10,235},{12,108},{14,239},... | collective-permute-start | bytes 786440 | tf_op jit(solution)/shard_map/ppermute | solution.py:451
  80.3 14.8 %collective-permute-start.14 = (bf16[256,512]{1,0:T(8,128)(2,1)S(1)}, bf16[256,512]{1,0:T(8,128)(2,1)S(1)}, u32[]{:S(2)}, u32[]{:S(2)}) collective-permute-start(bf16[256,512]{1,0:T(8,128)(2,1)S(1)} %get-tuple-element.170), channel_id=1, source_target_pairs={{0,32},{2,35},{4,36},{6,39},{8,40},{10,43},{12,44},{14,47},{16,48}... | collective-permute-start | bytes 786440 | tf_op jit(solution)/shard_map/ppermute | solution.py:451
  85.7 9.4 %collective-permute-start.16 = (bf16[256,512]{1,0:T(8,128)(2,1)S(1)}, bf16[256,512]{1,0:T(8,128)(2,1)S(1)}, u32[]{:S(2)}, u32[]{:S(2)}) collective-permute-start(bf16[256,512]{1,0:T(8,128)(2,1)S(1)} %slice.105), channel_id=1, source_target_pairs={{0,64},{2,194},{4,68},{6,198},{8,72},{10,202},{12,76},{14,206},{16... | collective-permute-start | bytes 786440 | tf_op jit(solution)/shard_map/ppermute | solution.py:451
  86.7 8.4 %collective-permute-start.17 = (bf16[256,512]{1,0:T(8,128)(2,1)S(1)}, bf16[256,512]{1,0:T(8,128)(2,1)S(1)}, u32[]{:S(2)}, u32[]{:S(2)}) collective-permute-start(bf16[256,512]{1,0:T(8,128)(2,1)S(1)} %slice.104), channel_id=1, source_target_pairs={{0,64},{2,194},{4,68},{6,198},{8,72},{10,202},{12,76},{14,206},{16... | collective-permute-start | bytes 786440 | tf_op jit(solution)/shard_map/ppermute | solution.py:451
  95.1 15.1 %collective-permute-start.24 = (f32[1024,512]{1,0:T(8,128)S(1)}, f32[1024,512]{1,0:T(8,128)S(1)}, u32[]{:S(2)}, u32[]{:S(2)}) collective-permute-start(f32[1024,512]{1,0:T(8,128)S(1)} %get-tuple-element.152), channel_id=1, source_target_pairs={{0,2},{2,0},{4,6},{6,4},{8,10},{10,8},{12,14},{14,12},{16,18},{18,... | collective-permute-start | bytes 6291464 | tf_op jit(solution)/shard_map/ppermute | solution.py:451
  95.6 8.4 %collective-permute-start.20 = (bf16[4,2,16,512]{3,2,1,0:T(8,128)(2,1)S(1)}, bf16[4,2,16,512]{3,2,1,0:T(8,128)(2,1)S(1)}, u32[]{:S(2)}, u32[]{:S(2)}) collective-permute-start(bf16[4,2,16,512]{3,2,1,0:T(8,128)(2,1)S(1)} %get-tuple-element.166), channel_id=1, source_target_pairs={{0,216},{2,74},{4,220},{6,78},{8,192},{10,82},{12,196},{14,86},{16... | collective-permute-start | bytes 393224 | tf_op jit(solution)/shard_map/ppermute | solution.py:451
  95.7 8.4 %collective-permute-start.19 = (bf16[4,2,16,512]{3,2,1,0:T(8,128)(2,1)S(1)}, bf16[4,2,16,512]{3,2,1,0:T(8,128)(2,1)S(1)}, u32[]{:S(2)}, u32[]{:S(2)}) collective-permute-start(bf16[4,2,16,512]{3,2,1,0:T(8,128)(2,1)S(1)} %get-tuple-element.167), channel_id=1, source_target_pairs={{0,24},{2,10},{4,28},{6,14},{8,0},{10,18},{12,4},{14,22},{16,8},{1... | collective-permute-start | bytes 393224 | tf_op jit(solution)/shard_map/ppermute | solution.py:451
  98.5 6.9 %collective-permute-start.18 = (bf16[4,2,16,512]{3,2,1,0:T(8,128)(2,1)S(1)}, bf16[4,2,16,512]{3,2,1,0:T(8,128)(2,1)S(1)}, u32[]{:S(2)}, u32[]{:S(2)}) collective-permute-start(bf16[4,2,16,512]{3,2,1,0:T(8,128)(2,1)S(1)} %get-tuple-element.168), channel_id=1, source_target_pairs={{0,192},{2,66},{4,196},{6,70},{8,200},{10,74},{12,204},{14,78},{16... | collective-permute-start | bytes 393224 | tf_op jit(solution)/shard_map/ppermute | solution.py:451
  105.5 7.9 %collective-permute-start.23 = (f32[2,16,512]{2,1,0:T(8,128)S(1)}, f32[2,16,512]{2,1,0:T(8,128)S(1)}, u32[]{:S(2)}, u32[]{:S(2)}) collective-permute-start(f32[2,16,512]{2,1,0:T(8,128)S(1)} %get-tuple-element.171), channel_id=1, source_target_pairs={{0,26},{2,8},{4,30},{6,12},{8,2},{10,16},{12,6},{14,20},{16,10},{1... | collective-permute-start | bytes 196616 | tf_op jit(solution)/shard_map/ppermute | solution.py:451
  107.1 6.3 %collective-permute-start.22 = (f32[2,16,512]{2,1,0:T(8,128)S(1)}, f32[2,16,512]{2,1,0:T(8,128)S(1)}, u32[]{:S(2)}, u32[]{:S(2)}) collective-permute-start(f32[2,16,512]{2,1,0:T(8,128)S(1)} %get-tuple-element.172), channel_id=1, source_target_pairs={{0,28},{2,6},{4,0},{6,10},{8,4},{10,14},{12,8},{14,18},{16,12},{18... | collective-permute-start | bytes 196616 | tf_op jit(solution)/shard_map/ppermute | solution.py:451
  107.1 6.3 %collective-permute-start.21 = (f32[2,16,512]{2,1,0:T(8,128)S(1)}, f32[2,16,512]{2,1,0:T(8,128)S(1)}, u32[]{:S(2)}, u32[]{:S(2)}) collective-permute-start(f32[2,16,512]{2,1,0:T(8,128)S(1)} %get-tuple-element.173), channel_id=1, source_target_pairs={{0,30},{2,4},{4,2},{6,8},{8,6},{10,12},{12,10},{14,16},{16,14},{18... | collective-permute-start | bytes 196616 | tf_op jit(solution)/shard_map/ppermute | solution.py:451

commit v5 on v2

--- a/solution.py
+++ b/solution.py
@@ -484,8 +484,7 @@
 
 def gather(queries, positives):
     line = code(queries, positives)
-    line = jnp.concatenate([line] + [send(line, back(by)) for by in (1, 2, 3)], axis=0)
-    line = jnp.concatenate([line, send(line, back(4))], axis=0)
+    line = jnp.concatenate([line] + [send(line, back(by)) for by in range(1, NZ)], axis=0)
     coded = line[:, D : D + 3 * SLOTS].T
     coded = jnp.concatenate([coded[i * SLOTS : (i + 1) * SLOTS] for i in range(3)], axis=1)
     coded = jnp.pad(coded, ((0, 0), (0, D - 3 * LINE)))

time: 114 us -> 131 us (1.15)
  waiting for transfers between devices: 19.7 us -> 28.5 us
  starting transfers between devices: 48.1 us -> 56.5 us
    ppermute x25 -> x28, waiting for transfers between devices: 19.7 us -> 28.5 us  [send(): return lax.ppermute(array, AXES, moved(move))]
    ppermute x25 -> x28, starting transfers between devices: 48.1 us -> 56.5 us  [send(): return lax.ppermute(array, AXES, moved(move))]
    unnamed x10, local copies, waits for them, and re-layouts: 1.89 us -> 0.5 us
  transfers between devices with their start and end apart: 25 -> 28, of which waited for: 8 -> 12; matrix products, arithmetic and copies ran while one was open for 3% -> 2% of each run, Pallas kernels for 28% -> 25%
where the time goes in v5:
time: 131 us; the launch traced here: 130 us
  starting transfers between devices  56.5 us (43%)
  Pallas kernels  39.1 us (30%)
  waiting for transfers between devices  28.5 us (22%)
  other arithmetic  3.04 us (2%)
  local copies, waits for them, and re-layouts  2.37 us (2%)
    ppermute x28, starting transfers between devices, send(): return lax.ppermute(array, AXES, moved(move))  56.5 us
    ppermute x28, waiting for transfers between devices, send(): return lax.ppermute(array, AXES, moved(move))  28.5 us
    pallas_call x4, Pallas kernels, first_residuals(): pl.pallas_call(lambda *refs: part_kernel(*refs, late=late), out_shape=sha...  12.8 us
    pallas_call x2, Pallas kernels, rest_gradient(): pl.pallas_call(lambda most, q, pos, wb, old, resid, out: rest_kernel(most...  8.7 us
    pallas_call x2, Pallas kernels, plane_terms(): pl.pallas_call(lambda *refs: plane_kernel(*refs, blocks=blocks), out_shap...  7.01 us
    pallas_call x2, Pallas kernels, update(): pl.pallas_call(lambda *refs: kernel(count, *refs), out_shape=(full, full,...  4.94 us
    pallas_call x2, Pallas kernels, terms(): pl.pallas_call(lambda *refs: terms_kernel(*refs, blocks=blocks), out_shap...  3.03 us
  transfers between devices with their start and end apart: 28, of which 12 were waited for; matrix products, arithmetic and copies ran while one was open for 2% of the time, Pallas kernels for 25%

profile of v5, /device:TPU:1, one launch (start us, length us, event | category | flops | bytes accessed | tf_op | source)
XLA Modules:
  0.0 130.4 jit_solution(8705795038861686280)
XLA Ops:
  2.4 3.3 %collective-permute-start.10 = (bf16[1024,512]{1,0:T(8,128)(2,1)S(1)}, bf16[1024,512]{1,0:T(8,128)(2,1)S(1)}, u32[]{:S(2)}, u32[]{:S(2)}) collective-permute-start(bf16[1024,512]{1,0:T(8,128)(2,1)S(1)} %convert_element_type.34.refs_1_.refs_2_), channel_id=1, source_target_pairs={{0,2},{2,0},{4,6},{6,4},{8,10},{10,8},{12,14},{14,12},{16,18},{18,... | collective-permute-start | bytes 3145736 | tf_op jit(solution)/shard_map/ppermute | solution.py:449
  6.1 5.2 %collective-permute-start.6 = (bf16[16,640]{0,1:T(8,128)(2,1)S(1)}, bf16[16,640]{0,1:T(8,128)(2,1)S(1)}, u32[]{:S(2)}, u32[]{:S(2)}) collective-permute-start(bf16[16,640]{0,1:T(8,128)(2,1)S(1)} %copy.35), channel_id=1, source_target_pairs={{0,18},{2,16},{4,22},{6,20},{8,26},{10,24},{12,30},{14,28},{16,2},... | collective-permute-start | bytes 61448 | tf_op jit(solution)/shard_map/ppermute | solution.py:449
  11.2 2.1 %collective-permute-start.4 = (bf16[16,640]{0,1:T(8,128)(2,1)S(1)}, bf16[16,640]{0,1:T(8,128)(2,1)S(1)}, u32[]{:S(2)}, u32[]{:S(2)}) collective-permute-start(bf16[16,640]{0,1:T(8,128)(2,1)S(1)} %copy.35), channel_id=1, source_target_pairs={{0,22},{2,12},{4,26},{6,16},{8,30},{10,20},{12,2},{14,24},{16,6},{... | collective-permute-start | bytes 61448 | tf_op jit(solution)/shard_map/ppermute | solution.py:449
  13.3 2.3 %collective-permute-start.3 = (bf16[16,640]{0,1:T(8,128)(2,1)S(1)}, bf16[16,640]{0,1:T(8,128)(2,1)S(1)}, u32[]{:S(2)}, u32[]{:S(2)}) collective-permute-start(bf16[16,640]{0,1:T(8,128)(2,1)S(1)} %copy.35), channel_id=1, source_target_pairs={{0,8},{2,26},{4,12},{6,30},{8,16},{10,2},{12,20},{14,6},{16,24},{1... | collective-permute-start | bytes 61448 | tf_op jit(solution)/shard_map/ppermute | solution.py:449
  16.0 8.6 %collective-permute-start.2 = (bf16[16,640]{0,1:T(8,128)(2,1)S(1)}, bf16[16,640]{0,1:T(8,128)(2,1)S(1)}, u32[]{:S(2)}, u32[]{:S(2)}) collective-permute-start(bf16[16,640]{0,1:T(8,128)(2,1)S(1)} %copy.35), channel_id=1, source_target_pairs={{0,26},{2,8},{4,30},{6,12},{8,2},{10,16},{12,6},{14,20},{16,10},{1... | collective-permute-start | bytes 61448 | tf_op jit(solution)/shard_map/ppermute | solution.py:449
  24.6 6.1 %collective-permute-done.5 = bf16[16,640]{0,1:T(8,128)(2,1)S(1)} collective-permute-done((bf16[16,640]{0,1:T(8,128)(2,1)S(1)}, bf16[16,640]{0,1:T(8,128)(2,1)S(1)}, u32[]{:S(2)}, u32[]{:S(2)}) %collective-permute-start.5) | collective-permute-done | bytes 20512 | tf_op jit(solution)/shard_map/ppermute | solution.py:449
  31.1 3.9 %collective-permute-start = (bf16[16,640]{0,1:T(8,128)(2,1)S(1)}, bf16[16,640]{0,1:T(8,128)(2,1)}, u32[]{:S(2)}, u32[]{:S(2)}) collective-permute-start(bf16[16,640]{0,1:T(8,128)(2,1)S(1)} %copy.35), channel_id=1, source_target_pairs={{0,30},{2,4},{4,2},{6,8},{8,6},{10,12},{12,10},{14,16},{16,14},{18... | collective-permute-start | bytes 61448 | tf_op jit(solution)/shard_map/ppermute | solution.py:449
  35.0 2.6 %collective-permute-done.3 = bf16[16,640]{0,1:T(8,128)(2,1)S(1)} collective-permute-done((bf16[16,640]{0,1:T(8,128)(2,1)S(1)}, bf16[16,640]{0,1:T(8,128)(2,1)S(1)}, u32[]{:S(2)}, u32[]{:S(2)}) %collective-permute-start.3) | collective-permute-done | bytes 20512 | tf_op jit(solution)/shard_map/ppermute | solution.py:449
  37.9 2.6 %collective-permute-done.1 = bf16[16,640]{0,1:T(8,128)(2,1)S(1)} collective-permute-done((bf16[16,640]{0,1:T(8,128)(2,1)S(1)}, bf16[16,640]{0,1:T(8,128)(2,1)S(1)}, u32[]{:S(2)}, u32[]{:S(2)}) %collective-permute-start.1) | collective-permute-done | bytes 20512 | tf_op jit(solution)/shard_map/ppermute | solution.py:449
  42.8 3.0 %collective-permute-start.9 = (bf16[136,512]{1,0:T(8,128)(2,1)S(1)}, bf16[136,512]{1,0:T(8,128)(2,1)S(1)}, u32[]{:S(2)}, u32[]{:S(2)}) collective-permute-start(bf16[136,512]{1,0:T(8,128)(2,1)S(1)} %pad_maximum_fusion.1.refs_0_), channel_id=1, source_target_pairs={{0,128},{2,3},{4,132},{6,7},{8,136},{10,11},{12,140},{14,15},{16,1... | collective-permute-start | bytes 417800 | tf_op jit(solution)/shard_map/ppermute | solution.py:449
  46.6 1.9 %collective-permute-done.9.refs_3_ = bf16[136,512]{1,0:T(8,128)(2,1)S(1)} collective-permute-done((bf16[136,512]{1,0:T(8,128)(2,1)S(1)}, bf16[136,512]{1,0:T(8,128)(2,1)S(1)}, u32[]{:S(2)}, u32[]{:S(2)}) %collective-permute-start.9) | collective-permute-done | bytes 139296 | tf_op jit(solution)/shard_map/ppermute | solution.py:449
  48.5 2.8 %collective-permute-done.8.refs_2_ = bf16[136,512]{1,0:T(8,128)(2,1)S(1)} collective-permute-done((bf16[136,512]{1,0:T(8,128)(2,1)S(1)}, bf16[136,512]{1,0:T(8,128)(2,1)S(1)}, u32[]{:S(2)}, u32[]{:S(2)}) %collective-permute-start.8) | collective-permute-done | bytes 139296 | tf_op jit(solution)/shard_map/ppermute | solution.py:449
  52.3 1.8 %collective-permute-start.12 = (bf16[544,512]{1,0:T(8,128)(2,1)S(1)}, bf16[544,512]{1,0:T(8,128)(2,1)S(1)}, u32[]{:S(2)}, u32[]{:S(2)}) collective-permute-start(bf16[544,512]{1,0:T(8,128)(2,1)S(1)} %pack.1.refs_0_), channel_id=1, source_target_pairs={{0,33},{2,194},{4,37},{6,198},{8,41},{10,202},{12,45},{14,206},{16... | collective-permute-start | bytes 1671176 | tf_op jit(solution)/shard_map/ppermute | solution.py:449
  54.1 2.6 %part.4 = (bf16[2048,512]{1,0:T(8,128)(2,1)S(1)}, s32[2,8,2048]{2,1,0:T(8,128)S(1)}, bf16[1024,2048]{1,0:T(8,128)(2,1)S(1)}, bf16[1024,2048]{1,0:T(8,128)(2,1)S(1)}, f32[8,128]{1,0:T(8,128)S(1)}) custom-call(bf16[544,512]{1,0:T(8,128)(2,1)S(1)} %pack.1.refs_0_, bf16[1024,512]{1,0:T(8,128)(2,1)S(1)} %convert_element_type.34.refs_1_.refs_2_, ...), custom_call_target="tpu_custom_call" | custom-call | flops 1073741824 | bytes 2097152 | tf_op jit(solution)/shard_map/part/pallas_call | solution.py:188
  57.4 2.6 %collective-permute-done.13.refs_0_ = bf16[544,512]{1,0:T(8,128)(2,1)S(1)} collective-permute-done((bf16[544,512]{1,0:T(8,128)(2,1)S(1)}, bf16[544,512]{1,0:T(8,128)(2,1)S(1)}, u32[]{:S(2)}, u32[]{:S(2)}) %collective-permute-start.13) | collective-permute-done | bytes 557088 | tf_op jit(solution)/shard_map/ppermute | solution.py:449
  60.1 2.8 %part.5 = (bf16[2048,512]{1,0:T(8,128)(2,1)S(1)}, s32[2,8,2048]{2,1,0:T(8,128)S(1)}, bf16[1024,2048]{1,0:T(8,128)(2,1)S(1)}, bf16[1024,2048]{1,0:T(8,128)(2,1)S(1)}, f32[8,128]{1,0:T(8,128)S(1)}) custom-call(bf16[544,512]{1,0:T(8,128)(2,1)S(1)} %collective-permute-done.13.refs_0_, ...), custom_call_target="tpu_custom_call", output_to_operand_aliasing={{0}: (3, {}), {1}: (4, {}), {2}: (5, {}), {3}: (6, {}), {4}... | custom-call | flops 1073741824 | bytes 2097152 | tf_op jit(solution)/shard_map/part/pallas_call | solution.py:188
  62.8 5.3 %collective-permute-done.12.refs_0_ = bf16[544,512]{1,0:T(8,128)(2,1)S(1)} collective-permute-done((bf16[544,512]{1,0:T(8,128)(2,1)S(1)}, bf16[544,512]{1,0:T(8,128)(2,1)S(1)}, u32[]{:S(2)}, u32[]{:S(2)}) %collective-permute-start.12) | collective-permute-done | bytes 557088 | tf_op jit(solution)/shard_map/ppermute | solution.py:449
  68.2 2.6 %part.6 = (bf16[2048,512]{1,0:T(8,128)(2,1)S(1)}, s32[2,8,2048]{2,1,0:T(8,128)S(1)}, bf16[1024,2048]{1,0:T(8,128)(2,1)S(1)}, bf16[1024,2048]{1,0:T(8,128)(2,1)S(1)}, f32[8,128]{1,0:T(8,128)S(1)}) custom-call(bf16[544,512]{1,0:T(8,128)(2,1)S(1)} %collective-permute-done.12.refs_0_, ...), custom_call_target="tpu_custom_call", output_to_operand_aliasing={{0}: (3, {}), {1}: (4, {}), {2}: (5, {}), {3}: (6, {}), {4}... | custom-call | flops 1073741824 | bytes 2097152 | tf_op jit(solution)/shard_map/part/pallas_call | solution.py:188
  70.8 4.9 %part.7 = (bf16[2048,512]{1,0:T(8,128)(2,1)S(1)}, s32[2,8,2048]{2,1,0:T(8,128)S(1)}, bf16[1024,2048]{1,0:T(8,128)(2,1)S(1)}, bf16[1024,2048]{1,0:T(8,128)(2,1)S(...) custom-call(bf16[544,512]{1,0:T(8,128)(2,1)S(1)} %collective-permute, ...), custom_call_target="tpu_custom_call", output_to_operand_aliasing={{0}: (3, {}), {1}: (4, {}), {2}: (5, {}), {3}: (6, {}), {4}... | custom-call | flops 2147483648 | bytes 2097152 | tf_op jit(solution)/shard_map/part/pallas_call | solution.py:188
  75.7 2.0 %collective-permute-start.14 = (f32[1024,512]{1,0:T(8,128)S(1)}, f32[1024,512]{1,0:T(8,128)S(1)}, u32[]{:S(2)}, u32[]{:S(2)}) collective-permute-start(f32[1024,512]{1,0:T(8,128)S(1)} %get-tuple-element.106), channel_id=1, source_target_pairs={{0,2},{2,0},{4,6},{6,4},{8,10},{10,8},{12,14},{14,12},{16,18},{18,... | collective-permute-start | bytes 6291464 | tf_op jit(solution)/shard_map/ppermute | solution.py:449
  79.3 2.3 %grad.1.refs_0_ = f32[1024,512]{1,0:T(8,128)S(1)} custom-call(bf16[1024,2048]{1,0:T(8,128)(2,1)S(1)} %get-tuple-element.118.resid_ref.refs_0_, bf16[2048,512]{1,0:T(8,128)(2,1)S(1)} %get-tuple-element.108.q_ref.refs_1_.q), custom_call_target="tpu_custom_call" | custom-call | flops 2147483648 | bytes 8388608 | tf_op jit(solution)/shard_map/grad/pallas_call | solution.py:371
  84.0 2.0 %collective-permute-start.15 = (bf16[512,512]{1,0:T(8,128)(2,1)S(1)}, bf16[512,512]{1,0:T(8,128)(2,1)S(1)}, u32[]{:S(2)}, u32[]{:S(2)}) collective-permute-start(bf16[512,512]{1,0:T(8,128)(2,1)S(1)} %terms.2), channel_id=1, source_target_pairs={{0,32},{2,35},{4,36},{6,39},{8,40},{10,43},{12,44},{14,47},{16,48}... | collective-permute-start | bytes 1572872 | tf_op jit(solution)/shard_map/ppermute | solution.py:449
  87.5 3.5 %plane.2 = (bf16[1024,2048]{1,0:T(8,128)(2,1)S(1)}, bf16[1024,2048]{1,0:T(8,128)(2,1)S(1)}, bf16[512,512]{1,0:T(8,128)(2,1)S(1)}) custom-call(f32[8,128]{1,0:T(8,128)S(1)} %get-tuple-element.115.refs_0_.most, bf16[2048,512]{1,0:T(8,128)(2,1)S(1)} %get-tuple-element.108.q_ref.refs_1_.q, s32[2,8,2048]{2,1,0:T(8,128)S(1)} %get-tuple-element.116.refs_2_.pos, ...), custom_call_target="tpu_custom_call" | custom-call | flops 2147483648 | bytes 4194304 | tf_op jit(solution)/shard_map/plane/pallas_call | solution.py:312
  91.1 2.6 %collective-permute-start.18 = (bf16[256,512]{1,0:T(8,128)(2,1)S(1)}, bf16[256,512]{1,0:T(8,128)(2,1)S(1)}, u32[]{:S(2)}, u32[]{:S(2)}) collective-permute-start(bf16[256,512]{1,0:T(8,128)(2,1)S(1)} %get-tuple-element.169), channel_id=1, source_target_pairs={{0,96},{2,227},{4,100},{6,231},{8,104},{10,235},{12,108},{14,239},... | collective-permute-start | bytes 786440 | tf_op jit(solution)/shard_map/ppermute | solution.py:449
  95.3 3.5 %plane.3 = (bf16[1024,2048]{1,0:T(8,128)(2,1)S(1)}, bf16[1024,2048]{1,0:T(8,128)(2,1)S(1)}, f32[512,512]{1,0:T(8,128)S(1)}) custom-call(f32[8,128]{1,0:T(8,128)S(1)} %get-tuple-element.115.refs_0_.most, bf16[2048,512]{1,0:T(8,128)(2,1)S(1)} %get-tuple-element.108.q_ref.refs_1_.q, ...), custom_call_target="tpu_custom_call", output_to_operand_aliasing={{0}: (5, {}), {1}: (6, {})} | custom-call | flops 2147483648 | bytes 4194304 | tf_op jit(solution)/shard_map/plane/pallas_call | solution.py:312
  102.1 4.4 %rest.2 = (bf16[1024,2048]{1,0:T(8,128)(2,1)S(1)}, f32[1024,512]{1,0:T(8,128)S(1)}) custom-call(f32[8,128]{1,0:T(8,128)S(1)} %get-tuple-element.115.refs_0_.most, bf16[2048,512]{1,0:T(8,128)(2,1)S(1)} %get-tuple-element.108.q_ref.refs_1_.q, s32[2,8,2048]{2,1,0:T(8,128)S(1)} %get-tuple-element.116.refs_2_.pos, ...), custom_call_target="tpu_custom_call", output_to_operand_aliasing={{0}: (4, {})} | custom-call | flops 3221225472 | bytes 8388608 | tf_op jit(solution)/shard_map/rest/pallas_call | solution.py:354
  106.4 2.2 %collective-permute-done.20 = bf16[256,512]{1,0:T(8,128)(2,1)S(1)} collective-permute-done((bf16[256,512]{1,0:T(8,128)(2,1)S(1)}, bf16[256,512]{1,0:T(8,128)(2,1)S(1)}, u32[]{:S(2)}, u32[]{:S(2)}) %collective-permute-start.20) | collective-permute-done | bytes 262176 | tf_op jit(solution)/shard_map/ppermute | solution.py:449
  109.2 3.5 %collective-permute-start.22 = (bf16[4,2,16,512]{3,2,1,0:T(8,128)(2,1)S(1)}, bf16[4,2,16,512]{3,2,1,0:T(8,128)(2,1)S(1)}, u32[]{:S(2)}, u32[]{:S(2)}) collective-permute-start(bf16[4,2,16,512]{3,2,1,0:T(8,128)(2,1)S(1)} %get-tuple-element.167), channel_id=1, source_target_pairs={{0,24},{2,10},{4,28},{6,14},{8,0},{10,18},{12,4},{14,22},{16,8},{1... | collective-permute-start | bytes 393224 | tf_op jit(solution)/shard_map/ppermute | solution.py:449
  112.6 4.0 %collective-permute-start.21 = (bf16[4,2,16,512]{3,2,1,0:T(8,128)(2,1)S(1)}, bf16[4,2,16,512]{3,2,1,0:T(8,128)(2,1)S(1)}, u32[]{:S(2)}, u32[]{:S(2)}) collective-permute-start(bf16[4,2,16,512]{3,2,1,0:T(8,128)(2,1)S(1)} %get-tuple-element.168), channel_id=1, source_target_pairs={{0,192},{2,66},{4,196},{6,70},{8,200},{10,74},{12,204},{14,78},{16... | collective-permute-start | bytes 393224 | tf_op jit(solution)/shard_map/ppermute | solution.py:449
  116.6 4.3 %rest.3 = (bf16[1024,2048]{1,0:T(8,128)(2,1)S(1)}, f32[1024,512]{1,0:T(8,128)S(1)}) custom-call(f32[8,128]{1,0:T(8,128)S(1)} %get-tuple-element.115.refs_0_.most, bf16[2048,512]{1,0:T(8,128)(2,1)S(1)} %get-tuple-element.108.q_ref.refs_1_.q, s32[2,8,2048]{2,1,0:T(8,128)S(1)} %get-tuple-element.116.refs_2_.pos, ...), custom_call_target="tpu_custom_call", output_to_operand_aliasing={{0}: (4, {})} | custom-call | flops 3221225472 | bytes 8388608 | tf_op jit(solution)/shard_map/rest/pallas_call | solution.py:354
  121.1 2.4 %collective-permute-start.26 = (f32[2,16,512]{2,1,0:T(8,128)S(1)}, f32[2,16,512]{2,1,0:T(8,128)S(1)}, u32[]{:S(2)}, u32[]{:S(2)}) collective-permute-start(f32[2,16,512]{2,1,0:T(8,128)S(1)} %get-tuple-element.171), channel_id=1, source_target_pairs={{0,26},{2,8},{4,30},{6,12},{8,2},{10,16},{12,6},{14,20},{16,10},{1... | collective-permute-start | bytes 196616 | tf_op jit(solution)/shard_map/ppermute | solution.py:449
  125.5 3.2 %adamw.3 = (f32[1024,512]{1,0:T(8,128)}, f32[1024,512]{1,0:T(8,128)}, f32[1024,512]{1,0:T(8,128)}) custom-call(f32[1024,512]{1,0:T(8,128)S(1)} %get-tuple-element.151.refs_0_, f32[1024,512]{1,0:T(8,128)S(1)} %collective-permute-done.27.refs_1_, f32[1024,512]{1,0:T(8,128)S(1)} %get-tuple-element.153.refs_2_, f32[1024,512]{1,0:T(8,128)S(1)} %get-tuple-element.154.refs_3_, ...), custom_call_target="tpu_custom_call" | custom-call | flops 10485760 | bytes 6291456 | tf_op jit(solution)/shard_map/adamw/pallas_call | solution.py:422
  (69 shorter events, 22.6 us)
Async XLA Ops:
  0.6 5.1 %copy-start.4 = (s32[16,8]{0,1:T(8,128)S(1)}, s32[16,8]{0,1:T(8,128)}, u32[]{:S(2)}) copy-start(s32[16,8]{0,1:T(8,128)} %param.6) | copy-start | bytes 1540
  0.6 5.1 %copy-start.3 = (bf16[16,512]{1,0:T(8,128)(2,1)S(1)}, bf16[16,512]{1,0:T(8,128)(2,1)}, u32[]{:S(2)}) copy-start(bf16[16,512]{1,0:T(8,128)(2,1)} %q_ref.1) | copy-start | bytes 49156
  2.4 51.7 %collective-permute-start.10 = (bf16[1024,512]{1,0:T(8,128)(2,1)S(1)}, bf16[1024,512]{1,0:T(8,128)(2,1)S(1)}, u32[]{:S(2)}, u32[]{:S(2)}) collective-permute-start(bf16[1024,512]{1,0:T(8,128)(2,1)S(1)} %convert_element_type.34.refs_1_.refs_2_), channel_id=1, source_target_pairs={{0,2},{2,0},{4,6},{6,4},{8,10},{10,8},{12,14},{14,12},{16,18},{18,... | collective-permute-start | bytes 3145736 | tf_op jit(solution)/shard_map/ppermute | solution.py:449
  6.1 9.9 %collective-permute-start.6 = (bf16[16,640]{0,1:T(8,128)(2,1)S(1)}, bf16[16,640]{0,1:T(8,128)(2,1)S(1)}, u32[]{:S(2)}, u32[]{:S(2)}) collective-permute-start(bf16[16,640]{0,1:T(8,128)(2,1)S(1)} %copy.35), channel_id=1, source_target_pairs={{0,18},{2,16},{4,22},{6,20},{8,26},{10,24},{12,30},{14,28},{16,2},... | collective-permute-start | bytes 61448 | tf_op jit(solution)/shard_map/ppermute | solution.py:449
  11.2 19.4 %collective-permute-start.5 = (bf16[16,640]{0,1:T(8,128)(2,1)S(1)}, bf16[16,640]{0,1:T(8,128)(2,1)S(1)}, u32[]{:S(2)}, u32[]{:S(2)}) collective-permute-start(bf16[16,640]{0,1:T(8,128)(2,1)S(1)} %copy.35), channel_id=1, source_target_pairs={{0,12},{2,22},{4,16},{6,26},{8,20},{10,30},{12,24},{14,2},{16,28},... | collective-permute-start | bytes 61448 | tf_op jit(solution)/shard_map/ppermute | solution.py:449
  11.2 19.9 %collective-permute-start.4 = (bf16[16,640]{0,1:T(8,128)(2,1)S(1)}, bf16[16,640]{0,1:T(8,128)(2,1)S(1)}, u32[]{:S(2)}, u32[]{:S(2)}) collective-permute-start(bf16[16,640]{0,1:T(8,128)(2,1)S(1)} %copy.35), channel_id=1, source_target_pairs={{0,22},{2,12},{4,26},{6,16},{8,30},{10,20},{12,2},{14,24},{16,6},{... | collective-permute-start | bytes 61448 | tf_op jit(solution)/shard_map/ppermute | solution.py:449
  13.3 24.3 %collective-permute-start.3 = (bf16[16,640]{0,1:T(8,128)(2,1)S(1)}, bf16[16,640]{0,1:T(8,128)(2,1)S(1)}, u32[]{:S(2)}, u32[]{:S(2)}) collective-permute-start(bf16[16,640]{0,1:T(8,128)(2,1)S(1)} %copy.35), channel_id=1, source_target_pairs={{0,8},{2,26},{4,12},{6,30},{8,16},{10,2},{12,20},{14,6},{16,24},{1... | collective-permute-start | bytes 61448 | tf_op jit(solution)/shard_map/ppermute | solution.py:449
  16.0 21.9 %collective-permute-start.2 = (bf16[16,640]{0,1:T(8,128)(2,1)S(1)}, bf16[16,640]{0,1:T(8,128)(2,1)S(1)}, u32[]{:S(2)}, u32[]{:S(2)}) collective-permute-start(bf16[16,640]{0,1:T(8,128)(2,1)S(1)} %copy.35), channel_id=1, source_target_pairs={{0,26},{2,8},{4,30},{6,12},{8,2},{10,16},{12,6},{14,20},{16,10},{1... | collective-permute-start | bytes 61448 | tf_op jit(solution)/shard_map/ppermute | solution.py:449
  30.6 9.9 %collective-permute-start.1 = (bf16[16,640]{0,1:T(8,128)(2,1)S(1)}, bf16[16,640]{0,1:T(8,128)(2,1)S(1)}, u32[]{:S(2)}, u32[]{:S(2)}) collective-permute-start(bf16[16,640]{0,1:T(8,128)(2,1)S(1)} %copy.35), channel_id=1, source_target_pairs={{0,4},{2,30},{4,8},{6,2},{8,12},{10,6},{12,16},{14,10},{16,20},{18... | collective-permute-start | bytes 61448 | tf_op jit(solution)/shard_map/ppermute | solution.py:449
  31.1 10.1 %collective-permute-start = (bf16[16,640]{0,1:T(8,128)(2,1)S(1)}, bf16[16,640]{0,1:T(8,128)(2,1)}, u32[]{:S(2)}, u32[]{:S(2)}) collective-permute-start(bf16[16,640]{0,1:T(8,128)(2,1)S(1)} %copy.35), channel_id=1, source_target_pairs={{0,30},{2,4},{4,2},{6,8},{8,6},{10,12},{12,10},{14,16},{16,14},{18... | collective-permute-start | bytes 61448 | tf_op jit(solution)/shard_map/ppermute | solution.py:449
  42.8 5.7 %collective-permute-start.9 = (bf16[136,512]{1,0:T(8,128)(2,1)S(1)}, bf16[136,512]{1,0:T(8,128)(2,1)S(1)}, u32[]{:S(2)}, u32[]{:S(2)}) collective-permute-start(bf16[136,512]{1,0:T(8,128)(2,1)S(1)} %pad_maximum_fusion.1.refs_0_), channel_id=1, source_target_pairs={{0,128},{2,3},{4,132},{6,7},{8,136},{10,11},{12,140},{14,15},{16,1... | collective-permute-start | bytes 417800 | tf_op jit(solution)/shard_map/ppermute | solution.py:449
  45.8 5.4 %collective-permute-start.8 = (bf16[136,512]{1,0:T(8,128)(2,1)S(1)}, bf16[136,512]{1,0:T(8,128)(2,1)S(1)}, u32[]{:S(2)}, u32[]{:S(2)}) collective-permute-start(bf16[136,512]{1,0:T(8,128)(2,1)S(1)} %pad_maximum_fusion.1.refs_0_), channel_id=1, source_target_pairs={{0,192},{2,35},{4,196},{6,39},{8,200},{10,43},{12,204},{14,47},{16... | collective-permute-start | bytes 417800 | tf_op jit(solution)/shard_map/ppermute | solution.py:449
  46.6 4.6 %collective-permute-start.7 = (bf16[136,512]{1,0:T(8,128)(2,1)S(1)}, bf16[136,512]{1,0:T(8,128)(2,1)S(1)}, u32[]{:S(2)}, u32[]{:S(2)}) collective-permute-start(bf16[136,512]{1,0:T(8,128)(2,1)S(1)} %pad_maximum_fusion.1.refs_0_), channel_id=1, source_target_pairs={{0,64},{2,34},{4,68},{6,38},{8,72},{10,42},{12,76},{14,46},{16,80}... | collective-permute-start | bytes 417800 | tf_op jit(solution)/shard_map/ppermute | solution.py:449
  51.3 8.8 %collective-permute-start.13 = (bf16[544,512]{1,0:T(8,128)(2,1)S(1)}, bf16[544,512]{1,0:T(8,128)(2,1)S(1)}, u32[]{:S(2)}, u32[]{:S(2)}) collective-permute-start(bf16[544,512]{1,0:T(8,128)(2,1)S(1)} %pack.1.refs_0_), channel_id=1, source_target_pairs={{0,32},{2,66},{4,36},{6,70},{8,40},{10,74},{12,44},{14,78},{16,48}... | collective-permute-start | bytes 1671176 | tf_op jit(solution)/shard_map/ppermute | solution.py:449
  52.3 15.9 %collective-permute-start.12 = (bf16[544,512]{1,0:T(8,128)(2,1)S(1)}, bf16[544,512]{1,0:T(8,128)(2,1)S(1)}, u32[]{:S(2)}, u32[]{:S(2)}) collective-permute-start(bf16[544,512]{1,0:T(8,128)(2,1)S(1)} %pack.1.refs_0_), channel_id=1, source_target_pairs={{0,33},{2,194},{4,37},{6,198},{8,41},{10,202},{12,45},{14,206},{16... | collective-permute-start | bytes 1671176 | tf_op jit(solution)/shard_map/ppermute | solution.py:449
  56.7 14.1 %collective-permute-start.11 = (bf16[544,512]{1,0:T(8,128)(2,1)S(1)}, bf16[544,512]{1,0:T(8,128)(2,1)S(1)}, u32[]{:S(2)}, u32[]{:S(2)}) collective-permute-start(bf16[544,512]{1,0:T(8,128)(2,1)S(1)} %pack.1.refs_0_), channel_id=1, source_target_pairs={{0,1},{2,130},{4,5},{6,134},{8,9},{10,138},{12,13},{14,142},{16,17... | collective-permute-start | bytes 1671176 | tf_op jit(solution)/shard_map/ppermute | solution.py:449
  75.7 5.9 %collective-permute-start.14 = (f32[1024,512]{1,0:T(8,128)S(1)}, f32[1024,512]{1,0:T(8,128)S(1)}, u32[]{:S(2)}, u32[]{:S(2)}) collective-permute-start(f32[1024,512]{1,0:T(8,128)S(1)} %get-tuple-element.106), channel_id=1, source_target_pairs={{0,2},{2,0},{4,6},{6,4},{8,10},{10,8},{12,14},{14,12},{16,18},{18,... | collective-permute-start | bytes 6291464 | tf_op jit(solution)/shard_map/ppermute | solution.py:449
  79.3 2.4 %copy-start = (f32[1024,512]{1,0:T(8,128)S(1)}, f32[1024,512]{1,0:T(8,128)}, u32[]{:S(2)}) copy-start(f32[1024,512]{1,0:T(8,128)} %refs_2_.1) | copy-start | bytes 6291460
  79.3 2.8 %copy-start.2 = (f32[1024,512]{1,0:T(8,128)S(1)}, f32[1024,512]{1,0:T(8,128)}, u32[]{:S(2)}) copy-start(f32[1024,512]{1,0:T(8,128)} %refs_4_.1) | copy-start | bytes 6291460
  83.9 3.6 %collective-permute-start.16 = (bf16[1024,512]{1,0:T(8,128)(2,1)S(1)}, bf16[1024,512]{1,0:T(8,128)(2,1)S(1)}, u32[]{:S(2)}, u32[]{:S(2)}) collective-permute-start(bf16[1024,512]{1,0:T(8,128)(2,1)S(1)} %get-tuple-element.117.refs_3_.wb), channel_id=1, source_target_pairs={{0,2},{2,0},{4,6},{6,4},{8,10},{10,8},{12,14},{14,12},{16,18},{18,... | collective-permute-start | bytes 3145736 | tf_op jit(solution)/shard_map/ppermute | solution.py:449
  84.0 14.8 %collective-permute-start.15 = (bf16[512,512]{1,0:T(8,128)(2,1)S(1)}, bf16[512,512]{1,0:T(8,128)(2,1)S(1)}, u32[]{:S(2)}, u32[]{:S(2)}) collective-permute-start(bf16[512,512]{1,0:T(8,128)(2,1)S(1)} %terms.2), channel_id=1, source_target_pairs={{0,32},{2,35},{4,36},{6,39},{8,40},{10,43},{12,44},{14,47},{16,48}... | collective-permute-start | bytes 1572872 | tf_op jit(solution)/shard_map/ppermute | solution.py:449
  91.1 15.3 %collective-permute-start.18 = (bf16[256,512]{1,0:T(8,128)(2,1)S(1)}, bf16[256,512]{1,0:T(8,128)(2,1)S(1)}, u32[]{:S(2)}, u32[]{:S(2)}) collective-permute-start(bf16[256,512]{1,0:T(8,128)(2,1)S(1)} %get-tuple-element.169), channel_id=1, source_target_pairs={{0,96},{2,227},{4,100},{6,231},{8,104},{10,235},{12,108},{14,239},... | collective-permute-start | bytes 786440 | tf_op jit(solution)/shard_map/ppermute | solution.py:449
  93.7 12.8 %collective-permute-start.17 = (bf16[256,512]{1,0:T(8,128)(2,1)S(1)}, bf16[256,512]{1,0:T(8,128)(2,1)S(1)}, u32[]{:S(2)}, u32[]{:S(2)}) collective-permute-start(bf16[256,512]{1,0:T(8,128)(2,1)S(1)} %get-tuple-element.170), channel_id=1, source_target_pairs={{0,32},{2,35},{4,36},{6,39},{8,40},{10,43},{12,44},{14,47},{16,48}... | collective-permute-start | bytes 786440 | tf_op jit(solution)/shard_map/ppermute | solution.py:449
  99.1 7.4 %collective-permute-start.19 = (bf16[256,512]{1,0:T(8,128)(2,1)S(1)}, bf16[256,512]{1,0:T(8,128)(2,1)S(1)}, u32[]{:S(2)}, u32[]{:S(2)}) collective-permute-start(bf16[256,512]{1,0:T(8,128)(2,1)S(1)} %slice.105), channel_id=1, source_target_pairs={{0,64},{2,194},{4,68},{6,198},{8,72},{10,202},{12,76},{14,206},{16... | collective-permute-start | bytes 786440 | tf_op jit(solution)/shard_map/ppermute | solution.py:449
  100.3 8.3 %collective-permute-start.20 = (bf16[256,512]{1,0:T(8,128)(2,1)S(1)}, bf16[256,512]{1,0:T(8,128)(2,1)S(1)}, u32[]{:S(2)}, u32[]{:S(2)}) collective-permute-start(bf16[256,512]{1,0:T(8,128)(2,1)S(1)} %slice.104), channel_id=1, source_target_pairs={{0,64},{2,194},{4,68},{6,198},{8,72},{10,202},{12,76},{14,206},{16... | collective-permute-start | bytes 786440 | tf_op jit(solution)/shard_map/ppermute | solution.py:449
  108.6 16.9 %collective-permute-start.27 = (f32[1024,512]{1,0:T(8,128)S(1)}, f32[1024,512]{1,0:T(8,128)S(1)}, u32[]{:S(2)}, u32[]{:S(2)}) collective-permute-start(f32[1024,512]{1,0:T(8,128)S(1)} %get-tuple-element.152), channel_id=1, source_target_pairs={{0,2},{2,0},{4,6},{6,4},{8,10},{10,8},{12,14},{14,12},{16,18},{18,... | collective-permute-start | bytes 6291464 | tf_op jit(solution)/shard_map/ppermute | solution.py:449
  109.1 11.9 %collective-permute-start.23 = (bf16[4,2,16,512]{3,2,1,0:T(8,128)(2,1)S(1)}, bf16[4,2,16,512]{3,2,1,0:T(8,128)(2,1)S(1)}, u32[]{:S(2)}, u32[]{:S(2)}) collective-permute-start(bf16[4,2,16,512]{3,2,1,0:T(8,128)(2,1)S(1)} %get-tuple-element.166), channel_id=1, source_target_pairs={{0,216},{2,74},{4,220},{6,78},{8,192},{10,82},{12,196},{14,86},{16... | collective-permute-start | bytes 393224 | tf_op jit(solution)/shard_map/ppermute | solution.py:449
  109.2 11.8 %collective-permute-start.22 = (bf16[4,2,16,512]{3,2,1,0:T(8,128)(2,1)S(1)}, bf16[4,2,16,512]{3,2,1,0:T(8,128)(2,1)S(1)}, u32[]{:S(2)}, u32[]{:S(2)}) collective-permute-start(bf16[4,2,16,512]{3,2,1,0:T(8,128)(2,1)S(1)} %get-tuple-element.167), channel_id=1, source_target_pairs={{0,24},{2,10},{4,28},{6,14},{8,0},{10,18},{12,4},{14,22},{16,8},{1... | collective-permute-start | bytes 393224 | tf_op jit(solution)/shard_map/ppermute | solution.py:449
  112.6 8.4 %collective-permute-start.21 = (bf16[4,2,16,512]{3,2,1,0:T(8,128)(2,1)S(1)}, bf16[4,2,16,512]{3,2,1,0:T(8,128)(2,1)S(1)}, u32[]{:S(2)}, u32[]{:S(2)}) collective-permute-start(bf16[4,2,16,512]{3,2,1,0:T(8,128)(2,1)S(1)} %get-tuple-element.168), channel_id=1, source_target_pairs={{0,192},{2,66},{4,196},{6,70},{8,200},{10,74},{12,204},{14,78},{16... | collective-permute-start | bytes 393224 | tf_op jit(solution)/shard_map/ppermute | solution.py:449
  121.1 7.6 %collective-permute-start.26 = (f32[2,16,512]{2,1,0:T(8,128)S(1)}, f32[2,16,512]{2,1,0:T(8,128)S(1)}, u32[]{:S(2)}, u32[]{:S(2)}) collective-permute-start(f32[2,16,512]{2,1,0:T(8,128)S(1)} %get-tuple-element.171), channel_id=1, source_target_pairs={{0,26},{2,8},{4,30},{6,12},{8,2},{10,16},{12,6},{14,20},{16,10},{1... | collective-permute-start | bytes 196616 | tf_op jit(solution)/shard_map/ppermute | solution.py:449
  123.5 6.2 %collective-permute-start.25 = (f32[2,16,512]{2,1,0:T(8,128)S(1)}, f32[2,16,512]{2,1,0:T(8,128)S(1)}, u32[]{:S(2)}, u32[]{:S(2)}) collective-permute-start(f32[2,16,512]{2,1,0:T(8,128)S(1)} %get-tuple-element.172), channel_id=1, source_target_pairs={{0,28},{2,6},{4,0},{6,10},{8,4},{10,14},{12,8},{14,18},{16,12},{18... | collective-permute-start | bytes 196616 | tf_op jit(solution)/shard_map/ppermute | solution.py:449
  124.9 4.9 %collective-permute-start.24 = (f32[2,16,512]{2,1,0:T(8,128)S(1)}, f32[2,16,512]{2,1,0:T(8,128)S(1)}, u32[]{:S(2)}, u32[]{:S(2)}) collective-permute-start(f32[2,16,512]{2,1,0:T(8,128)S(1)} %get-tuple-element.173), channel_id=1, source_target_pairs={{0,30},{2,4},{4,2},{6,8},{8,6},{10,12},{12,10},{14,16},{16,14},{18... | collective-permute-start | bytes 196616 | tf_op jit(solution)/shard_map/ppermute | solution.py:449
  (1 other events, 2.4 us)

commit v6 on v2

--- a/solution.py
+++ b/solution.py
@@ -306,6 +306,47 @@
     fill_terms(own_ref, other_ref, wb_own, wb_other, out_ref, blocks)
 
 
+def own_kernel(most, q_ref, pos_ref, wb_ref, own_ref):
+    blocks = beside()
+    for i in range(2):
+        fill_block(q_ref, pos_ref, wb_ref, own_ref, 0, chosen(blocks, i))
+    finish(most, pos_ref, ((0, own_ref),), blocks)
+
+
+def own_beside(most, q, pos, wb):
+    size = LAB * 2 * BLOCK
+    return pl.pallas_call(
+        own_kernel,
+        out_shape=jax.ShapeDtypeStruct((LAB, NQ), bf16),
+        in_specs=[spec()] * 4,
+        out_specs=spec(),
+        compiler_params=params(),
+        cost_estimate=cost(2 * size * D, 4 * size, 2 * size),
+        name="own",
+    )(most, q, pos, wb)
+
+
+def beside_kernel(most, q_ref, pos_ref, wb_own, wb_other, own_ref, other_ref, out_ref):
+    blocks = beside()
+    for i in range(2):
+        fill_block(q_ref, pos_ref, wb_other, other_ref, 1, chosen(blocks, i))
+    finish(most, pos_ref, ((1, other_ref),), blocks)
+    fill_terms(own_ref, other_ref, wb_own, wb_other, out_ref, blocks)
+
+
+def beside_terms(most, q, pos, wb, wb_other, own):
+    size = LAB * 2 * BLOCK
+    return pl.pallas_call(
+        beside_kernel,
+        out_shape=(jax.ShapeDtypeStruct((LAB, NQ), bf16), jax.ShapeDtypeStruct((2 * BLOCK, D), bf16)),
+        in_specs=[spec()] * 6,
+        out_specs=(spec(),) * 2,
+        compiler_params=params(),
+        cost_estimate=cost(6 * size * D, 4 * size, 2 * size),
+        name="beside",
+    )(most, q, pos, wb, wb_other, own)
+
+
 def plane_terms(most, q, pos, wb, wb_other, blocks, kind, into=()):
     size = 2 * LAB * 2 * BLOCK
     resid = jax.ShapeDtypeStruct((LAB, NQ), bf16)
@@ -524,19 +565,20 @@
     weight, first, second, wb = update(past_steps + 1, False, mine, part, weight, first, second)
 
     wb_other = swap(wb)
-    wb, out0, *step0 = after(wb, out0, *step0)
+    wb, out0 = after(wb, out0)
     out0 = send(out0, over_y)
+    own = own_beside(most, q, pos, wb)
+    wb_other, own = after(wb_other, own)
+    other, out1 = beside_terms(most, q, pos, wb, wb_other, own)
+
+    out1, own, other, *step0 = after(out1, own, other, *step0)
+    got = [send(out1[:BLOCK], over_y), send(out1[BLOCK:], then(over_y, first_x))]
     part0 = terms(*step0, here, f32)
-    wb_other, part0 = after(wb_other, part0)
-    own, other, out1 = plane_terms(most, q, pos, wb, wb_other, beside, bf16)
-
-    out1, own, other = after(out1, own, other)
-    got = [send(out1[:BLOCK], over_y), send(out1[BLOCK:], then(over_y, first_x))]
-    own, other, part1 = plane_terms(most, q, pos, wb, wb_other, here, f32, (own, other))
-    out0, part1 = after(out0, part1)
-    got.append(send(part1[BLOCK:].astype(bf16), first_x))
+    out0, part0, own = after(out0, part0, own)
     part0 = part0 + out0.astype(f32)
     half0 = send(part0[BLOCK:].astype(bf16), first_x)
+    own, other, part1 = plane_terms(most, q, pos, wb, wb_other, here, f32, (own, other))
+    got.append(send(part1[BLOCK:].astype(bf16), first_x))
 
     part1, part0, other = after(part1, part0, other)
     theirs = rest_gradient(most, q, pos, wb_other, other, 1)

time: 114 us -> 116 us (1.018)
  starting transfers between devices: 48.1 us -> 49.6 us
    pallas_call x2 -> x1, Pallas kernels: 7.01 us -> 3.46 us  [plane_terms(): pl.pallas_call(lambda *refs: plane_kernel(*refs, blocks=blocks), out_shap...]
    pallas_call x0 -> x2, Pallas kernels: none -> 3.44 us  [the longest x1 2.49 us: beside_terms(): pl.pallas_call(beside_kernel, out_shape=(jax.ShapeDtypeStruct((LAB, NQ),...]
    ppermute x25, starting transfers between devices: 48.1 us -> 49.6 us  [send(): return lax.ppermute(array, AXES, moved(move))]
  transfers between devices with their start and end apart: 25 -> 25, of which waited for: 8 -> 9; matrix products, arithmetic and copies ran while one was open for 3% -> 3% of each run, Pallas kernels for 28% -> 28%
where the time goes in v6:
time: 116 us
  starting transfers between devices  49.6 us (43%)
  Pallas kernels  39 us (34%)
  waiting for transfers between devices  20.4 us (18%)
  other arithmetic  3.22 us (3%)
  local copies, waits for them, and re-layouts  2.66 us (2%)
    ppermute x25, starting transfers between devices, send(): return lax.ppermute(array, AXES, moved(move))  49.6 us
    ppermute x25, waiting for transfers between devices, send(): return lax.ppermute(array, AXES, moved(move))  20.4 us
    pallas_call x4, Pallas kernels, first_residuals(): pl.pallas_call(lambda *refs: part_kernel(*refs, late=late), out_shape=sha...  12.9 us
    pallas_call x2, Pallas kernels, rest_gradient(): pl.pallas_call(lambda most, q, pos, wb, old, resid, out: rest_kernel(most...  8.66 us
    pallas_call x2, Pallas kernels, update(): pl.pallas_call(lambda *refs: kernel(count, *refs), out_shape=(full, full,...  4.96 us
    pallas_call x1, Pallas kernels, plane_terms(): pl.pallas_call(lambda *refs: plane_kernel(*refs, blocks=blocks), out_shap...  3.46 us
    pallas_call x2, Pallas kernels, terms(): pl.pallas_call(lambda *refs: terms_kernel(*refs, blocks=blocks), out_shap...  3.04 us
    pallas_call x1, Pallas kernels, beside_terms(): pl.pallas_call(beside_kernel, out_shape=(jax.ShapeDtypeStruct((LAB, NQ),...  2.49 us
  transfers between devices with their start and end apart: 25, of which 9 were waited for; matrix products, arithmetic and copies ran while one was open for 3% of the time, Pallas kernels for 28%

profile of v6, /device:TPU:1, one launch (start us, length us, event | category | flops | bytes accessed | tf_op | source)
XLA Modules:
  0.0 115.8 jit_solution(10753424926434753389)
XLA Ops:
  2.4 4.5 %collective-permute-start.2 = (bf16[16,640]{0,1:T(8,128)(2,1)S(1)}, bf16[16,640]{0,1:T(8,128)(2,1)S(1)}, u32[]{:S(2)}, u32[]{:S(2)}) collective-permute-start(bf16[16,640]{0,1:T(8,128)(2,1)S(1)} %copy.32), channel_id=1, source_target_pairs={{0,26},{2,8},{4,30},{6,12},{8,2},{10,16},{12,6},{14,20},{16,10},{1... | collective-permute-start | bytes 61448 | tf_op jit(solution)/shard_map/ppermute | solution.py:490
  6.9 2.1 %collective-permute-start.1 = (bf16[16,640]{0,1:T(8,128)(2,1)S(1)}, bf16[16,640]{0,1:T(8,128)(2,1)S(1)}, u32[]{:S(2)}, u32[]{:S(2)}) collective-permute-start(bf16[16,640]{0,1:T(8,128)(2,1)S(1)} %copy.32), channel_id=1, source_target_pairs={{0,4},{2,30},{4,8},{6,2},{8,12},{10,6},{12,16},{14,10},{16,20},{18... | collective-permute-start | bytes 61448 | tf_op jit(solution)/shard_map/ppermute | solution.py:490
  10.4 1.7 %convert_element_type.34.refs_1_.refs_2_ = bf16[1024,512]{1,0:T(8,128)(2,1)S(1)} convert(f32[1024,512]{1,0:T(8,128)} %refs_2_.1) | non-fusion elementwise | flops 524288 | bytes 3145728 | tf_op jit(solution)/shard_map/convert_element_type | solution.py:549
  13.7 1.8 %collective-permute-done = bf16[16,640]{0,1:T(8,128)(2,1)S(1)} collective-permute-done((bf16[16,640]{0,1:T(8,128)(2,1)S(1)}, bf16[16,640]{0,1:T(8,128)(2,1)S(1)}, u32[]{:S(2)}, u32[]{:S(2)}) %collective-permute-start) | collective-permute-done | bytes 20512 | tf_op jit(solution)/shard_map/ppermute | solution.py:490
  15.7 3.5 %collective-permute-start.3 = (bf16[64,640]{0,1:T(8,128)(2,1)S(1)}, bf16[64,640]{0,1:T(8,128)(2,1)S(1)}, u32[]{:S(2)}, u32[]{:S(2)}) collective-permute-start(bf16[64,640]{0,1:T(8,128)(2,1)S(1)} %pad_maximum_fusion.1), channel_id=1, source_target_pairs={{0,8},{2,26},{4,12},{6,30},{8,16},{10,2},{12,20},{14,6},{16,24},{1... | collective-permute-start | bytes 245768 | tf_op jit(solution)/shard_map/ppermute | solution.py:490
  19.2 3.9 %collective-permute-done.3 = bf16[64,640]{0,1:T(8,128)(2,1)S(1)} collective-permute-done((bf16[64,640]{0,1:T(8,128)(2,1)S(1)}, bf16[64,640]{0,1:T(8,128)(2,1)S(1)}, u32[]{:S(2)}, u32[]{:S(2)}) %collective-permute-start.3) | collective-permute-done | bytes 81952 | tf_op jit(solution)/shard_map/ppermute | solution.py:490
  23.6 3.0 %collective-permute-start.6 = (bf16[136,512]{1,0:T(8,128)(2,1)S(1)}, bf16[136,512]{1,0:T(8,128)(2,1)S(1)}, u32[]{:S(2)}, u32[]{:S(2)}) collective-permute-start(bf16[136,512]{1,0:T(8,128)(2,1)S(1)} %pad_maximum_fusion.2.refs_0_), channel_id=1, source_target_pairs={{0,128},{2,3},{4,132},{6,7},{8,136},{10,11},{12,140},{14,15},{16,1... | collective-permute-start | bytes 417800 | tf_op jit(solution)/shard_map/ppermute | solution.py:490
  27.4 1.7 %collective-permute-done.6.refs_3_ = bf16[136,512]{1,0:T(8,128)(2,1)S(1)} collective-permute-done((bf16[136,512]{1,0:T(8,128)(2,1)S(1)}, bf16[136,512]{1,0:T(8,128)(2,1)S(1)}, u32[]{:S(2)}, u32[]{:S(2)}) %collective-permute-start.6) | collective-permute-done | bytes 139296 | tf_op jit(solution)/shard_map/ppermute | solution.py:490
  29.1 2.6 %collective-permute-done.5.refs_2_ = bf16[136,512]{1,0:T(8,128)(2,1)S(1)} collective-permute-done((bf16[136,512]{1,0:T(8,128)(2,1)S(1)}, bf16[136,512]{1,0:T(8,128)(2,1)S(1)}, u32[]{:S(2)}, u32[]{:S(2)}) %collective-permute-start.5) | collective-permute-done | bytes 139296 | tf_op jit(solution)/shard_map/ppermute | solution.py:490
  33.0 1.8 %collective-permute-start.9 = (bf16[544,512]{1,0:T(8,128)(2,1)S(1)}, bf16[544,512]{1,0:T(8,128)(2,1)S(1)}, u32[]{:S(2)}, u32[]{:S(2)}) collective-permute-start(bf16[544,512]{1,0:T(8,128)(2,1)S(1)} %pack.1.refs_0_), channel_id=1, source_target_pairs={{0,33},{2,194},{4,37},{6,198},{8,41},{10,202},{12,45},{14,206},{16... | collective-permute-start | bytes 1671176 | tf_op jit(solution)/shard_map/ppermute | solution.py:490
  34.9 2.6 %part.4 = (bf16[2048,512]{1,0:T(8,128)(2,1)S(1)}, s32[2,8,2048]{2,1,0:T(8,128)S(1)}, bf16[1024,2048]{1,0:T(8,128)(2,1)S(1)}, bf16[1024,2048]{1,0:T(8,128)(2,1)S(1)}, f32[8,128]{1,0:T(8,128)S(1)}) custom-call(bf16[544,512]{1,0:T(8,128)(2,1)S(1)} %pack.1.refs_0_, bf16[1024,512]{1,0:T(8,128)(2,1)S(1)} %convert_element_type.34.refs_1_.refs_2_, ...), custom_call_target="tpu_custom_call" | custom-call | flops 1073741824 | bytes 2097152 | tf_op jit(solution)/shard_map/part/pallas_call | solution.py:188
  38.2 3.8 %collective-permute-done.10.refs_0_ = bf16[544,512]{1,0:T(8,128)(2,1)S(1)} collective-permute-done((bf16[544,512]{1,0:T(8,128)(2,1)S(1)}, bf16[544,512]{1,0:T(8,128)(2,1)S(1)}, u32[]{:S(2)}, u32[]{:S(2)}) %collective-permute-start.10) | collective-permute-done | bytes 557088 | tf_op jit(solution)/shard_map/ppermute | solution.py:490
  42.0 2.6 %part.5 = (bf16[2048,512]{1,0:T(8,128)(2,1)S(1)}, s32[2,8,2048]{2,1,0:T(8,128)S(1)}, bf16[1024,2048]{1,0:T(8,128)(2,1)S(1)}, bf16[1024,2048]{1,0:T(8,128)(2,1)S(1)}, f32[8,128]{1,0:T(8,128)S(1)}) custom-call(bf16[544,512]{1,0:T(8,128)(2,1)S(1)} %collective-permute-done.10.refs_0_, ...), custom_call_target="tpu_custom_call", output_to_operand_aliasing={{0}: (3, {}), {1}: (4, {}), {2}: (5, {}), {3}: (6, {}), {4}... | custom-call | flops 1073741824 | bytes 2097152 | tf_op jit(solution)/shard_map/part/pallas_call | solution.py:188
  44.6 2.7 %collective-permute-done.9.refs_0_ = bf16[544,512]{1,0:T(8,128)(2,1)S(1)} collective-permute-done((bf16[544,512]{1,0:T(8,128)(2,1)S(1)}, bf16[544,512]{1,0:T(8,128)(2,1)S(1)}, u32[]{:S(2)}, u32[]{:S(2)}) %collective-permute-start.9) | collective-permute-done | bytes 557088 | tf_op jit(solution)/shard_map/ppermute | solution.py:490
  47.3 2.6 %part.6 = (bf16[2048,512]{1,0:T(8,128)(2,1)S(1)}, s32[2,8,2048]{2,1,0:T(8,128)S(1)}, bf16[1024,2048]{1,0:T(8,128)(2,1)S(1)}, bf16[1024,2048]{1,0:T(8,128)(2,1)S(1)}, f32[8,128]{1,0:T(8,128)S(1)}) custom-call(bf16[544,512]{1,0:T(8,128)(2,1)S(1)} %collective-permute-done.9.refs_0_, ...), custom_call_target="tpu_custom_call", output_to_operand_aliasing={{0}: (3, {}), {1}: (4, {}), {2}: (5, {}), {3}: (6, {}), {4}... | custom-call | flops 1073741824 | bytes 2097152 | tf_op jit(solution)/shard_map/part/pallas_call | solution.py:188
  49.9 5.1 %part.7 = (bf16[2048,512]{1,0:T(8,128)(2,1)S(1)}, s32[2,8,2048]{2,1,0:T(8,128)S(1)}, bf16[1024,2048]{1,0:T(8,128)(2,1)S(1)}, bf16[1024,2048]{1,0:T(8,128)(2,1)S(...) custom-call(bf16[544,512]{1,0:T(8,128)(2,1)S(1)} %collective-permute, ...), custom_call_target="tpu_custom_call", output_to_operand_aliasing={{0}: (3, {}), {1}: (4, {}), {2}: (5, {}), {3}: (6, {}), {4}... | custom-call | flops 2147483648 | bytes 2097152 | tf_op jit(solution)/shard_map/part/pallas_call | solution.py:188
  55.0 9.2 %collective-permute-start.11 = (f32[1024,512]{1,0:T(8,128)S(1)}, f32[1024,512]{1,0:T(8,128)S(1)}, u32[]{:S(2)}, u32[]{:S(2)}) collective-permute-start(f32[1024,512]{1,0:T(8,128)S(1)} %get-tuple-element.109), channel_id=1, source_target_pairs={{0,2},{2,0},{4,6},{6,4},{8,10},{10,8},{12,14},{14,12},{16,18},{18,... | collective-permute-start | bytes 6291464 | tf_op jit(solution)/shard_map/ppermute | solution.py:490
  65.8 2.3 %grad.1.refs_0_ = f32[1024,512]{1,0:T(8,128)S(1)} custom-call(bf16[1024,2048]{1,0:T(8,128)(2,1)S(1)} %get-tuple-element.122.resid_ref.refs_0_, bf16[2048,512]{1,0:T(8,128)(2,1)S(1)} %get-tuple-element.107.q_ref.refs_1_.q), custom_call_target="tpu_custom_call" | custom-call | flops 2147483648 | bytes 8388608 | tf_op jit(solution)/shard_map/grad/pallas_call | solution.py:412
  68.7 1.8 %adamw.2 = (f32[1024,512]{1,0:T(8,128)S(1)}, f32[1024,512]{1,0:T(8,128)S(1)}, f32[1024,512]{1,0:T(8,128)S(1)}, bf16[1024,512]{1,0:T(8,128)(2,1)S(1)}) custom-call(f32[1024,512]{1,0:T(8,128)S(1)} %grad.1.refs_0_, f32[1024,512]{1,0:T(8,128)S(1)} %collective-permute-done.11.refs_1_, f32[1024,512]{1,0:T(8,128)S(1)} %copy-done, f32[1024,512]{1,0:T(8,128)S(1)} %copy-done.1, ...), custom_call_target="tpu_custom_call" | custom-call | flops 10485760 | bytes 6291456 | tf_op jit(solution)/shard_map/adamw/pallas_call | solution.py:463
  70.5 2.0 %collective-permute-start.13 = (bf16[512,512]{1,0:T(8,128)(2,1)S(1)}, bf16[512,512]{1,0:T(8,128)(2,1)S(1)}, u32[]{:S(2)}, u32[]{:S(2)}) collective-permute-start(bf16[512,512]{1,0:T(8,128)(2,1)S(1)} %terms.2), channel_id=1, source_target_pairs={{0,32},{2,35},{4,36},{6,39},{8,40},{10,43},{12,44},{14,47},{16,48}... | collective-permute-start | bytes 1572872 | tf_op jit(solution)/shard_map/ppermute | solution.py:490
  73.5 2.5 %beside.1 = (bf16[1024,2048]{1,0:T(8,128)(2,1)S(1)}, bf16[512,512]{1,0:T(8,128)(2,1)S(1)}) custom-call(f32[8,128]{1,0:T(8,128)S(1)} %get-tuple-element.106.most.refs_0_, bf16[2048,512]{1,0:T(8,128)(2,1)S(1)} %get-tuple-element.107.q_ref.refs_1_.q, s32[2,8,2048]{2,1,0:T(8,128)S(1)} %get-tuple-element.108.pos_ref.refs_2_.pos, ...), custom_call_target="tpu_custom_call" | custom-call | flops 1610612736 | bytes 2097152 | tf_op jit(solution)/shard_map/beside/pallas_call | solution.py:339
  76.0 1.5 %terms.3 = f32[512,512]{1,0:T(8,128)S(1)} custom-call(bf16[1024,2048]{1,0:T(8,128)(2,1)S(1)} %get-tuple-element.122.resid_ref.refs_0_, bf16[1024,2048]{1,0:T(8,128)(2,1)S(1)} %get-tuple-element.123.refs_1_, bf16[1024,512]{1,0:T(8,128)(2,1)S(1)} %convert_element_type.34.refs_1_.refs_2_, bf16[1024,512]{1,0:T(8,128)(2,1)S(1)} %collective-permute-done.7.refs_2_.refs_3_), custom_call_target="tpu_custom_call" | custom-call | flops 1073741824 | bytes 4194304 | tf_op jit(solution)/shard_map/terms/pallas_call | solution.py:370
  77.6 2.3 %collective-permute-done.13 = bf16[512,512]{1,0:T(8,128)(2,1)S(1)} collective-permute-done((bf16[512,512]{1,0:T(8,128)(2,1)S(1)}, bf16[512,512]{1,0:T(8,128)(2,1)S(1)}, u32[]{:S(2)}, u32[]{:S(2)}) %collective-permute-start.13) | collective-permute-done | bytes 524320 | tf_op jit(solution)/shard_map/ppermute | solution.py:490
  79.9 3.5 %collective-permute-start.15 = (bf16[256,512]{1,0:T(8,128)(2,1)S(1)}, bf16[256,512]{1,0:T(8,128)(2,1)S(1)}, u32[]{:S(2)}, u32[]{:S(2)}) collective-permute-start(bf16[256,512]{1,0:T(8,128)(2,1)S(1)} %get-tuple-element.169), channel_id=1, source_target_pairs={{0,96},{2,227},{4,100},{6,231},{8,104},{10,235},{12,108},{14,239},... | collective-permute-start | bytes 786440 | tf_op jit(solution)/shard_map/ppermute | solution.py:490
  85.4 3.5 %plane.1 = (bf16[1024,2048]{1,0:T(8,128)(2,1)S(1)}, bf16[1024,2048]{1,0:T(8,128)(2,1)S(1)}, f32[512,512]{1,0:T(8,128)S(1)}) custom-call(f32[8,128]{1,0:T(8,128)S(1)} %get-tuple-element.106.most.refs_0_, bf16[2048,512]{1,0:T(8,128)(2,1)S(1)} %get-tuple-element.107.q_ref.refs_1_.q, ...), custom_call_target="tpu_custom_call", output_to_operand_aliasing={{0}: (5, {}), {1}: (6, {})} | custom-call | flops 2147483648 | bytes 4194304 | tf_op jit(solution)/shard_map/plane/pallas_call | solution.py:353
  88.9 2.0 %collective-permute-start.16 = (bf16[256,512]{1,0:T(8,128)(2,1)S(1)}, bf16[256,512]{1,0:T(8,128)(2,1)S(1)}, u32[]{:S(2)}, u32[]{:S(2)}) collective-permute-start(bf16[256,512]{1,0:T(8,128)(2,1)S(1)} %slice.105), channel_id=1, source_target_pairs={{0,64},{2,194},{4,68},{6,198},{8,72},{10,202},{12,76},{14,206},{16... | collective-permute-start | bytes 786440 | tf_op jit(solution)/shard_map/ppermute | solution.py:490
  90.9 4.3 %rest.2 = (bf16[1024,2048]{1,0:T(8,128)(2,1)S(1)}, f32[1024,512]{1,0:T(8,128)S(1)}) custom-call(f32[8,128]{1,0:T(8,128)S(1)} %get-tuple-element.106.most.refs_0_, bf16[2048,512]{1,0:T(8,128)(2,1)S(1)} %get-tuple-element.107.q_ref.refs_1_.q, s32[2,8,2048]{2,1,0:T(8,128)S(1)} %get-tuple-element.108.pos_ref.refs_2_.pos, ...), custom_call_target="tpu_custom_call", output_to_operand_aliasing={{0}: (4, {})} | custom-call | flops 3221225472 | bytes 8388608 | tf_op jit(solution)/shard_map/rest/pallas_call | solution.py:395
  96.1 4.1 %collective-permute-start.19 = (bf16[4,2,16,512]{3,2,1,0:T(8,128)(2,1)S(1)}, bf16[4,2,16,512]{3,2,1,0:T(8,128)(2,1)S(1)}, u32[]{:S(2)}, u32[]{:S(2)}) collective-permute-start(bf16[4,2,16,512]{3,2,1,0:T(8,128)(2,1)S(1)} %get-tuple-element.167), channel_id=1, source_target_pairs={{0,24},{2,10},{4,28},{6,14},{8,0},{10,18},{12,4},{14,22},{16,8},{1... | collective-permute-start | bytes 393224 | tf_op jit(solution)/shard_map/ppermute | solution.py:490
  100.2 2.9 %collective-permute-start.18 = (bf16[4,2,16,512]{3,2,1,0:T(8,128)(2,1)S(1)}, bf16[4,2,16,512]{3,2,1,0:T(8,128)(2,1)S(1)}, u32[]{:S(2)}, u32[]{:S(2)}) collective-permute-start(bf16[4,2,16,512]{3,2,1,0:T(8,128)(2,1)S(1)} %get-tuple-element.168), channel_id=1, source_target_pairs={{0,192},{2,66},{4,196},{6,70},{8,200},{10,74},{12,204},{14,78},{16... | collective-permute-start | bytes 393224 | tf_op jit(solution)/shard_map/ppermute | solution.py:490
  103.1 4.3 %rest.3 = (bf16[1024,2048]{1,0:T(8,128)(2,1)S(1)}, f32[1024,512]{1,0:T(8,128)S(1)}) custom-call(f32[8,128]{1,0:T(8,128)S(1)} %get-tuple-element.106.most.refs_0_, bf16[2048,512]{1,0:T(8,128)(2,1)S(1)} %get-tuple-element.107.q_ref.refs_1_.q, s32[2,8,2048]{2,1,0:T(8,128)S(1)} %get-tuple-element.108.pos_ref.refs_2_.pos, ...), custom_call_target="tpu_custom_call", output_to_operand_aliasing={{0}: (4, {})} | custom-call | flops 3221225472 | bytes 8388608 | tf_op jit(solution)/shard_map/rest/pallas_call | solution.py:395
  108.5 3.4 %collective-permute-start.21 = (f32[2,16,512]{2,1,0:T(8,128)S(1)}, f32[2,16,512]{2,1,0:T(8,128)S(1)}, u32[]{:S(2)}, u32[]{:S(2)}) collective-permute-start(f32[2,16,512]{2,1,0:T(8,128)S(1)} %get-tuple-element.173), channel_id=1, source_target_pairs={{0,30},{2,4},{4,2},{6,8},{8,6},{10,12},{12,10},{14,16},{16,14},{18... | collective-permute-start | bytes 196616 | tf_op jit(solution)/shard_map/ppermute | solution.py:490
  111.9 3.2 %adamw.3 = (f32[1024,512]{1,0:T(8,128)}, f32[1024,512]{1,0:T(8,128)}, f32[1024,512]{1,0:T(8,128)}) custom-call(f32[1024,512]{1,0:T(8,128)S(1)} %get-tuple-element.151.refs_0_, f32[1024,512]{1,0:T(8,128)S(1)} %collective-permute-done.24.refs_1_, f32[1024,512]{1,0:T(8,128)S(1)} %get-tuple-element.153.refs_2_, f32[1024,512]{1,0:T(8,128)S(1)} %get-tuple-element.154.refs_3_, ...), custom_call_target="tpu_custom_call" | custom-call | flops 10485760 | bytes 6291456 | tf_op jit(solution)/shard_map/adamw/pallas_call | solution.py:463
  (65 shorter events, 15.9 us)
Async XLA Ops:
  0.6 0.7 copy-start.3
  1.3 0.7 copy-start.4
  2.4 10.2 %collective-permute-start.2 = (bf16[16,640]{0,1:T(8,128)(2,1)S(1)}, bf16[16,640]{0,1:T(8,128)(2,1)S(1)}, u32[]{:S(2)}, u32[]{:S(2)}) collective-permute-start(bf16[16,640]{0,1:T(8,128)(2,1)S(1)} %copy.32), channel_id=1, source_target_pairs={{0,26},{2,8},{4,30},{6,12},{8,2},{10,16},{12,6},{14,20},{16,10},{1... | collective-permute-start | bytes 61448 | tf_op jit(solution)/shard_map/ppermute | solution.py:490
  6.9 6.8 %collective-permute-start.1 = (bf16[16,640]{0,1:T(8,128)(2,1)S(1)}, bf16[16,640]{0,1:T(8,128)(2,1)S(1)}, u32[]{:S(2)}, u32[]{:S(2)}) collective-permute-start(bf16[16,640]{0,1:T(8,128)(2,1)S(1)} %copy.32), channel_id=1, source_target_pairs={{0,4},{2,30},{4,8},{6,2},{8,12},{10,6},{12,16},{14,10},{16,20},{18... | collective-permute-start | bytes 61448 | tf_op jit(solution)/shard_map/ppermute | solution.py:490
  9.0 6.5 %collective-permute-start = (bf16[16,640]{0,1:T(8,128)(2,1)S(1)}, bf16[16,640]{0,1:T(8,128)(2,1)S(1)}, u32[]{:S(2)}, u32[]{:S(2)}) collective-permute-start(bf16[16,640]{0,1:T(8,128)(2,1)S(1)} %copy.32), channel_id=1, source_target_pairs={{0,30},{2,4},{4,2},{6,8},{8,6},{10,12},{12,10},{14,16},{16,14},{18... | collective-permute-start | bytes 61448 | tf_op jit(solution)/shard_map/ppermute | solution.py:490
  12.1 22.8 %collective-permute-start.7 = (bf16[1024,512]{1,0:T(8,128)(2,1)S(1)}, bf16[1024,512]{1,0:T(8,128)(2,1)S(1)}, u32[]{:S(2)}, u32[]{:S(2)}) collective-permute-start(bf16[1024,512]{1,0:T(8,128)(2,1)S(1)} %convert_element_type.34.refs_1_.refs_2_), channel_id=1, source_target_pairs={{0,2},{2,0},{4,6},{6,4},{8,10},{10,8},{12,14},{14,12},{16,18},{18,... | collective-permute-start | bytes 3145736 | tf_op jit(solution)/shard_map/ppermute | solution.py:490
  15.7 7.4 %collective-permute-start.3 = (bf16[64,640]{0,1:T(8,128)(2,1)S(1)}, bf16[64,640]{0,1:T(8,128)(2,1)S(1)}, u32[]{:S(2)}, u32[]{:S(2)}) collective-permute-start(bf16[64,640]{0,1:T(8,128)(2,1)S(1)} %pad_maximum_fusion.1), channel_id=1, source_target_pairs={{0,8},{2,26},{4,12},{6,30},{8,16},{10,2},{12,20},{14,6},{16,24},{1... | collective-permute-start | bytes 245768 | tf_op jit(solution)/shard_map/ppermute | solution.py:490
  23.6 5.5 %collective-permute-start.6 = (bf16[136,512]{1,0:T(8,128)(2,1)S(1)}, bf16[136,512]{1,0:T(8,128)(2,1)S(1)}, u32[]{:S(2)}, u32[]{:S(2)}) collective-permute-start(bf16[136,512]{1,0:T(8,128)(2,1)S(1)} %pad_maximum_fusion.2.refs_0_), channel_id=1, source_target_pairs={{0,128},{2,3},{4,132},{6,7},{8,136},{10,11},{12,140},{14,15},{16,1... | collective-permute-start | bytes 417800 | tf_op jit(solution)/shard_map/ppermute | solution.py:490
  26.6 5.1 %collective-permute-start.5 = (bf16[136,512]{1,0:T(8,128)(2,1)S(1)}, bf16[136,512]{1,0:T(8,128)(2,1)S(1)}, u32[]{:S(2)}, u32[]{:S(2)}) collective-permute-start(bf16[136,512]{1,0:T(8,128)(2,1)S(1)} %pad_maximum_fusion.2.refs_0_), channel_id=1, source_target_pairs={{0,192},{2,35},{4,196},{6,39},{8,200},{10,43},{12,204},{14,47},{16... | collective-permute-start | bytes 417800 | tf_op jit(solution)/shard_map/ppermute | solution.py:490
  27.4 4.3 %collective-permute-start.4 = (bf16[136,512]{1,0:T(8,128)(2,1)S(1)}, bf16[136,512]{1,0:T(8,128)(2,1)S(1)}, u32[]{:S(2)}, u32[]{:S(2)}) collective-permute-start(bf16[136,512]{1,0:T(8,128)(2,1)S(1)} %pad_maximum_fusion.2.refs_0_), channel_id=1, source_target_pairs={{0,64},{2,34},{4,68},{6,38},{8,72},{10,42},{12,76},{14,46},{16,80}... | collective-permute-start | bytes 417800 | tf_op jit(solution)/shard_map/ppermute | solution.py:490
  31.8 10.3 %collective-permute-start.10 = (bf16[544,512]{1,0:T(8,128)(2,1)S(1)}, bf16[544,512]{1,0:T(8,128)(2,1)S(1)}, u32[]{:S(2)}, u32[]{:S(2)}) collective-permute-start(bf16[544,512]{1,0:T(8,128)(2,1)S(1)} %pack.1.refs_0_), channel_id=1, source_target_pairs={{0,32},{2,66},{4,36},{6,70},{8,40},{10,74},{12,44},{14,78},{16,48}... | collective-permute-start | bytes 1671176 | tf_op jit(solution)/shard_map/ppermute | solution.py:490
  33.0 14.3 %collective-permute-start.9 = (bf16[544,512]{1,0:T(8,128)(2,1)S(1)}, bf16[544,512]{1,0:T(8,128)(2,1)S(1)}, u32[]{:S(2)}, u32[]{:S(2)}) collective-permute-start(bf16[544,512]{1,0:T(8,128)(2,1)S(1)} %pack.1.refs_0_), channel_id=1, source_target_pairs={{0,33},{2,194},{4,37},{6,198},{8,41},{10,202},{12,45},{14,206},{16... | collective-permute-start | bytes 1671176 | tf_op jit(solution)/shard_map/ppermute | solution.py:490
  37.4 12.5 %collective-permute-start.8 = (bf16[544,512]{1,0:T(8,128)(2,1)S(1)}, bf16[544,512]{1,0:T(8,128)(2,1)S(1)}, u32[]{:S(2)}, u32[]{:S(2)}) collective-permute-start(bf16[544,512]{1,0:T(8,128)(2,1)S(1)} %pack.1.refs_0_), channel_id=1, source_target_pairs={{0,1},{2,130},{4,5},{6,134},{8,9},{10,138},{12,13},{14,142},{16,17... | collective-permute-start | bytes 1671176 | tf_op jit(solution)/shard_map/ppermute | solution.py:490
  55.0 13.1 %collective-permute-start.11 = (f32[1024,512]{1,0:T(8,128)S(1)}, f32[1024,512]{1,0:T(8,128)S(1)}, u32[]{:S(2)}, u32[]{:S(2)}) collective-permute-start(f32[1024,512]{1,0:T(8,128)S(1)} %get-tuple-element.109), channel_id=1, source_target_pairs={{0,2},{2,0},{4,6},{6,4},{8,10},{10,8},{12,14},{14,12},{16,18},{18,... | collective-permute-start | bytes 6291464 | tf_op jit(solution)/shard_map/ppermute | solution.py:490
  65.8 2.4 %copy-start = (f32[1024,512]{1,0:T(8,128)S(1)}, f32[1024,512]{1,0:T(8,128)}, u32[]{:S(2)}) copy-start(f32[1024,512]{1,0:T(8,128)} %refs_2_.1) | copy-start | bytes 6291460
  65.8 2.4 %copy-start.1 = (f32[1024,512]{1,0:T(8,128)S(1)}, f32[1024,512]{1,0:T(8,128)}, u32[]{:S(2)}) copy-start(f32[1024,512]{1,0:T(8,128)} %refs_3_.1) | copy-start | bytes 6291460
  65.8 2.8 %copy-start.2 = (f32[1024,512]{1,0:T(8,128)S(1)}, f32[1024,512]{1,0:T(8,128)}, u32[]{:S(2)}) copy-start(f32[1024,512]{1,0:T(8,128)} %refs_4_.1) | copy-start | bytes 6291460
  70.4 3.1 %collective-permute-start.12 = (bf16[1024,512]{1,0:T(8,128)(2,1)S(1)}, bf16[1024,512]{1,0:T(8,128)(2,1)S(1)}, u32[]{:S(2)}, u32[]{:S(2)}) collective-permute-start(bf16[1024,512]{1,0:T(8,128)(2,1)S(1)} %get-tuple-element.116.wb_ref.wb_own.refs_3_.wb), channel_id=1, source_target_pairs={{0,2},{2,0},{4,6},{6,4},{8,10},{10,8},{12,14},{14,12},{16,18},{18,... | collective-permute-start | bytes 3145736 | tf_op jit(solution)/shard_map/ppermute | solution.py:490
  70.5 9.3 %collective-permute-start.13 = (bf16[512,512]{1,0:T(8,128)(2,1)S(1)}, bf16[512,512]{1,0:T(8,128)(2,1)S(1)}, u32[]{:S(2)}, u32[]{:S(2)}) collective-permute-start(bf16[512,512]{1,0:T(8,128)(2,1)S(1)} %terms.2), channel_id=1, source_target_pairs={{0,32},{2,35},{4,36},{6,39},{8,40},{10,43},{12,44},{14,47},{16,48}... | collective-permute-start | bytes 1572872 | tf_op jit(solution)/shard_map/ppermute | solution.py:490
  79.9 15.3 %collective-permute-start.15 = (bf16[256,512]{1,0:T(8,128)(2,1)S(1)}, bf16[256,512]{1,0:T(8,128)(2,1)S(1)}, u32[]{:S(2)}, u32[]{:S(2)}) collective-permute-start(bf16[256,512]{1,0:T(8,128)(2,1)S(1)} %get-tuple-element.169), channel_id=1, source_target_pairs={{0,96},{2,227},{4,100},{6,231},{8,104},{10,235},{12,108},{14,239},... | collective-permute-start | bytes 786440 | tf_op jit(solution)/shard_map/ppermute | solution.py:490
  83.4 11.8 %collective-permute-start.14 = (bf16[256,512]{1,0:T(8,128)(2,1)S(1)}, bf16[256,512]{1,0:T(8,128)(2,1)S(1)}, u32[]{:S(2)}, u32[]{:S(2)}) collective-permute-start(bf16[256,512]{1,0:T(8,128)(2,1)S(1)} %get-tuple-element.170), channel_id=1, source_target_pairs={{0,32},{2,35},{4,36},{6,39},{8,40},{10,43},{12,44},{14,47},{16,48}... | collective-permute-start | bytes 786440 | tf_op jit(solution)/shard_map/ppermute | solution.py:490
  84.3 10.9 %collective-permute-start.17 = (bf16[256,512]{1,0:T(8,128)(2,1)S(1)}, bf16[256,512]{1,0:T(8,128)(2,1)S(1)}, u32[]{:S(2)}, u32[]{:S(2)}) collective-permute-start(bf16[256,512]{1,0:T(8,128)(2,1)S(1)} %slice.104), channel_id=1, source_target_pairs={{0,64},{2,194},{4,68},{6,198},{8,72},{10,202},{12,76},{14,206},{16... | collective-permute-start | bytes 786440 | tf_op jit(solution)/shard_map/ppermute | solution.py:490
  88.9 6.7 %collective-permute-start.16 = (bf16[256,512]{1,0:T(8,128)(2,1)S(1)}, bf16[256,512]{1,0:T(8,128)(2,1)S(1)}, u32[]{:S(2)}, u32[]{:S(2)}) collective-permute-start(bf16[256,512]{1,0:T(8,128)(2,1)S(1)} %slice.105), channel_id=1, source_target_pairs={{0,64},{2,194},{4,68},{6,198},{8,72},{10,202},{12,76},{14,206},{16... | collective-permute-start | bytes 786440 | tf_op jit(solution)/shard_map/ppermute | solution.py:490
  95.6 16.3 %collective-permute-start.24 = (f32[1024,512]{1,0:T(8,128)S(1)}, f32[1024,512]{1,0:T(8,128)S(1)}, u32[]{:S(2)}, u32[]{:S(2)}) collective-permute-start(f32[1024,512]{1,0:T(8,128)S(1)} %get-tuple-element.152), channel_id=1, source_target_pairs={{0,2},{2,0},{4,6},{6,4},{8,10},{10,8},{12,14},{14,12},{16,18},{18,... | collective-permute-start | bytes 6291464 | tf_op jit(solution)/shard_map/ppermute | solution.py:490
  96.0 11.4 %collective-permute-start.20 = (bf16[4,2,16,512]{3,2,1,0:T(8,128)(2,1)S(1)}, bf16[4,2,16,512]{3,2,1,0:T(8,128)(2,1)S(1)}, u32[]{:S(2)}, u32[]{:S(2)}) collective-permute-start(bf16[4,2,16,512]{3,2,1,0:T(8,128)(2,1)S(1)} %get-tuple-element.166), channel_id=1, source_target_pairs={{0,216},{2,74},{4,220},{6,78},{8,192},{10,82},{12,196},{14,86},{16... | collective-permute-start | bytes 393224 | tf_op jit(solution)/shard_map/ppermute | solution.py:490
  96.1 11.3 %collective-permute-start.19 = (bf16[4,2,16,512]{3,2,1,0:T(8,128)(2,1)S(1)}, bf16[4,2,16,512]{3,2,1,0:T(8,128)(2,1)S(1)}, u32[]{:S(2)}, u32[]{:S(2)}) collective-permute-start(bf16[4,2,16,512]{3,2,1,0:T(8,128)(2,1)S(1)} %get-tuple-element.167), channel_id=1, source_target_pairs={{0,24},{2,10},{4,28},{6,14},{8,0},{10,18},{12,4},{14,22},{16,8},{1... | collective-permute-start | bytes 393224 | tf_op jit(solution)/shard_map/ppermute | solution.py:490
  100.2 7.2 %collective-permute-start.18 = (bf16[4,2,16,512]{3,2,1,0:T(8,128)(2,1)S(1)}, bf16[4,2,16,512]{3,2,1,0:T(8,128)(2,1)S(1)}, u32[]{:S(2)}, u32[]{:S(2)}) collective-permute-start(bf16[4,2,16,512]{3,2,1,0:T(8,128)(2,1)S(1)} %get-tuple-element.168), channel_id=1, source_target_pairs={{0,192},{2,66},{4,196},{6,70},{8,200},{10,74},{12,204},{14,78},{16... | collective-permute-start | bytes 393224 | tf_op jit(solution)/shard_map/ppermute | solution.py:490
  107.6 7.6 %collective-permute-start.23 = (f32[2,16,512]{2,1,0:T(8,128)S(1)}, f32[2,16,512]{2,1,0:T(8,128)S(1)}, u32[]{:S(2)}, u32[]{:S(2)}) collective-permute-start(f32[2,16,512]{2,1,0:T(8,128)S(1)} %get-tuple-element.171), channel_id=1, source_target_pairs={{0,26},{2,8},{4,30},{6,12},{8,2},{10,16},{12,6},{14,20},{16,10},{1... | collective-permute-start | bytes 196616 | tf_op jit(solution)/shard_map/ppermute | solution.py:490
  108.5 6.6 %collective-permute-start.22 = (f32[2,16,512]{2,1,0:T(8,128)S(1)}, f32[2,16,512]{2,1,0:T(8,128)S(1)}, u32[]{:S(2)}, u32[]{:S(2)}) collective-permute-start(f32[2,16,512]{2,1,0:T(8,128)S(1)} %get-tuple-element.172), channel_id=1, source_target_pairs={{0,28},{2,6},{4,0},{6,10},{8,4},{10,14},{12,8},{14,18},{16,12},{18... | collective-permute-start | bytes 196616 | tf_op jit(solution)/shard_map/ppermute | solution.py:490
  108.5 6.6 %collective-permute-start.21 = (f32[2,16,512]{2,1,0:T(8,128)S(1)}, f32[2,16,512]{2,1,0:T(8,128)S(1)}, u32[]{:S(2)}, u32[]{:S(2)}) collective-permute-start(f32[2,16,512]{2,1,0:T(8,128)S(1)} %get-tuple-element.173), channel_id=1, source_target_pairs={{0,30},{2,4},{4,2},{6,8},{8,6},{10,12},{12,10},{14,16},{16,14},{18... | collective-permute-start | bytes 196616 | tf_op jit(solution)/shard_map/ppermute | solution.py:490

commit v7 on v2

--- a/solution.py
+++ b/solution.py
@@ -145,7 +145,7 @@
             for j in range(SLOTS):
                 pos_ref[half, j : j + 1, at] = rows[j][k : k + 1]
 
-    @pl.loop(0, 2)
+    @pl.loop(0, 2, unroll=late == LAST)
     def _(pair):
         q = part_ref[pl.ds(pl.multiple_of(pair * BLOCK, BLOCK), BLOCK), :]
         ends = [span(late, 3 * pair), span(late, 1 + pair)]

time: 114 us -> 114 us (level)
  no operation moved by 1% of the time
where the time goes in v7:
time: 114 us
  starting transfers between devices  48.1 us (42%)
  Pallas kernels  38.8 us (34%)
  waiting for transfers between devices  19.9 us (17%)
  other arithmetic  3.26 us (3%)
  local copies, waits for them, and re-layouts  2.67 us (2%)
    ppermute x25, starting transfers between devices, send(): return lax.ppermute(array, AXES, moved(move))  48.1 us
    ppermute x25, waiting for transfers between devices, send(): return lax.ppermute(array, AXES, moved(move))  19.9 us
    pallas_call x4, Pallas kernels, first_residuals(): pl.pallas_call(lambda *refs: part_kernel(*refs, late=late), out_shape=sha...  12.6 us
    pallas_call x2, Pallas kernels, rest_gradient(): pl.pallas_call(lambda most, q, pos, wb, old, resid, out: rest_kernel(most...  8.68 us
    pallas_call x2, Pallas kernels, plane_terms(): pl.pallas_call(lambda *refs: plane_kernel(*refs, blocks=blocks), out_shap...  7.01 us
    pallas_call x2, Pallas kernels, update(): pl.pallas_call(lambda *refs: kernel(count, *refs), out_shape=(full, full,...  4.94 us
    pallas_call x2, Pallas kernels, terms(): pl.pallas_call(lambda *refs: terms_kernel(*refs, blocks=blocks), out_shap...  3.03 us
    pallas_call x1, Pallas kernels, gradient(): pl.pallas_call(grad_kernel, out_shape=jax.ShapeDtypeStruct((LAB, D), f32)...  2.32 us
  transfers between devices with their start and end apart: 25, of which 8 were waited for; matrix products, arithmetic and copies ran while one was open for 3% of the time, Pallas kernels for 28%

profile of v7, /device:TPU:1, one launch (start us, length us, event | category | flops | bytes accessed | tf_op | source)
XLA Modules:
  0.0 113.7 jit_solution(5878295578542538392)
XLA Ops:
  2.4 4.5 %collective-permute-start.2 = (bf16[16,640]{0,1:T(8,128)(2,1)S(1)}, bf16[16,640]{0,1:T(8,128)(2,1)S(1)}, u32[]{:S(2)}, u32[]{:S(2)}) collective-permute-start(bf16[16,640]{0,1:T(8,128)(2,1)S(1)} %copy.32), channel_id=1, source_target_pairs={{0,26},{2,8},{4,30},{6,12},{8,2},{10,16},{12,6},{14,20},{16,10},{1... | collective-permute-start | bytes 61448 | tf_op jit(solution)/shard_map/ppermute | solution.py:449
  6.9 2.1 %collective-permute-start.1 = (bf16[16,640]{0,1:T(8,128)(2,1)S(1)}, bf16[16,640]{0,1:T(8,128)(2,1)S(1)}, u32[]{:S(2)}, u32[]{:S(2)}) collective-permute-start(bf16[16,640]{0,1:T(8,128)(2,1)S(1)} %copy.32), channel_id=1, source_target_pairs={{0,4},{2,30},{4,8},{6,2},{8,12},{10,6},{12,16},{14,10},{16,20},{18... | collective-permute-start | bytes 61448 | tf_op jit(solution)/shard_map/ppermute | solution.py:449
  10.4 1.7 %convert_element_type.34.refs_1_.refs_2_ = bf16[1024,512]{1,0:T(8,128)(2,1)S(1)} convert(f32[1024,512]{1,0:T(8,128)} %refs_2_.1) | non-fusion elementwise | flops 524288 | bytes 3145728 | tf_op jit(solution)/shard_map/convert_element_type | solution.py:508
  13.7 1.8 %collective-permute-done = bf16[16,640]{0,1:T(8,128)(2,1)S(1)} collective-permute-done((bf16[16,640]{0,1:T(8,128)(2,1)S(1)}, bf16[16,640]{0,1:T(8,128)(2,1)S(1)}, u32[]{:S(2)}, u32[]{:S(2)}) %collective-permute-start) | collective-permute-done | bytes 20512 | tf_op jit(solution)/shard_map/ppermute | solution.py:449
  15.7 3.5 %collective-permute-start.3 = (bf16[64,640]{0,1:T(8,128)(2,1)S(1)}, bf16[64,640]{0,1:T(8,128)(2,1)S(1)}, u32[]{:S(2)}, u32[]{:S(2)}) collective-permute-start(bf16[64,640]{0,1:T(8,128)(2,1)S(1)} %pad_maximum_fusion.1), channel_id=1, source_target_pairs={{0,8},{2,26},{4,12},{6,30},{8,16},{10,2},{12,20},{14,6},{16,24},{1... | collective-permute-start | bytes 245768 | tf_op jit(solution)/shard_map/ppermute | solution.py:449
  19.2 3.9 %collective-permute-done.3 = bf16[64,640]{0,1:T(8,128)(2,1)S(1)} collective-permute-done((bf16[64,640]{0,1:T(8,128)(2,1)S(1)}, bf16[64,640]{0,1:T(8,128)(2,1)S(1)}, u32[]{:S(2)}, u32[]{:S(2)}) %collective-permute-start.3) | collective-permute-done | bytes 81952 | tf_op jit(solution)/shard_map/ppermute | solution.py:449
  23.6 3.0 %collective-permute-start.6 = (bf16[136,512]{1,0:T(8,128)(2,1)S(1)}, bf16[136,512]{1,0:T(8,128)(2,1)S(1)}, u32[]{:S(2)}, u32[]{:S(2)}) collective-permute-start(bf16[136,512]{1,0:T(8,128)(2,1)S(1)} %pad_maximum_fusion.2.refs_0_), channel_id=1, source_target_pairs={{0,128},{2,3},{4,132},{6,7},{8,136},{10,11},{12,140},{14,15},{16,1... | collective-permute-start | bytes 417800 | tf_op jit(solution)/shard_map/ppermute | solution.py:449
  27.4 1.7 %collective-permute-done.6.refs_3_ = bf16[136,512]{1,0:T(8,128)(2,1)S(1)} collective-permute-done((bf16[136,512]{1,0:T(8,128)(2,1)S(1)}, bf16[136,512]{1,0:T(8,128)(2,1)S(1)}, u32[]{:S(2)}, u32[]{:S(2)}) %collective-permute-start.6) | collective-permute-done | bytes 139296 | tf_op jit(solution)/shard_map/ppermute | solution.py:449
  29.1 2.6 %collective-permute-done.5.refs_2_ = bf16[136,512]{1,0:T(8,128)(2,1)S(1)} collective-permute-done((bf16[136,512]{1,0:T(8,128)(2,1)S(1)}, bf16[136,512]{1,0:T(8,128)(2,1)S(1)}, u32[]{:S(2)}, u32[]{:S(2)}) %collective-permute-start.5) | collective-permute-done | bytes 139296 | tf_op jit(solution)/shard_map/ppermute | solution.py:449
  33.0 1.8 %collective-permute-start.9 = (bf16[544,512]{1,0:T(8,128)(2,1)S(1)}, bf16[544,512]{1,0:T(8,128)(2,1)S(1)}, u32[]{:S(2)}, u32[]{:S(2)}) collective-permute-start(bf16[544,512]{1,0:T(8,128)(2,1)S(1)} %pack.1.refs_0_), channel_id=1, source_target_pairs={{0,33},{2,194},{4,37},{6,198},{8,41},{10,202},{12,45},{14,206},{16... | collective-permute-start | bytes 1671176 | tf_op jit(solution)/shard_map/ppermute | solution.py:449
  34.9 2.6 %part.4 = (bf16[2048,512]{1,0:T(8,128)(2,1)S(1)}, s32[2,8,2048]{2,1,0:T(8,128)S(1)}, bf16[1024,2048]{1,0:T(8,128)(2,1)S(1)}, bf16[1024,2048]{1,0:T(8,128)(2,1)S(1)}, f32[8,128]{1,0:T(8,128)S(1)}) custom-call(bf16[544,512]{1,0:T(8,128)(2,1)S(1)} %pack.1.refs_0_, bf16[1024,512]{1,0:T(8,128)(2,1)S(1)} %convert_element_type.34.refs_1_.refs_2_, ...), custom_call_target="tpu_custom_call" | custom-call | flops 1073741824 | bytes 2097152 | tf_op jit(solution)/shard_map/part/pallas_call | solution.py:188
  38.2 3.8 %collective-permute-done.10.refs_0_ = bf16[544,512]{1,0:T(8,128)(2,1)S(1)} collective-permute-done((bf16[544,512]{1,0:T(8,128)(2,1)S(1)}, bf16[544,512]{1,0:T(8,128)(2,1)S(1)}, u32[]{:S(2)}, u32[]{:S(2)}) %collective-permute-start.10) | collective-permute-done | bytes 557088 | tf_op jit(solution)/shard_map/ppermute | solution.py:449
  42.0 2.6 %part.5 = (bf16[2048,512]{1,0:T(8,128)(2,1)S(1)}, s32[2,8,2048]{2,1,0:T(8,128)S(1)}, bf16[1024,2048]{1,0:T(8,128)(2,1)S(1)}, bf16[1024,2048]{1,0:T(8,128)(2,1)S(1)}, f32[8,128]{1,0:T(8,128)S(1)}) custom-call(bf16[544,512]{1,0:T(8,128)(2,1)S(1)} %collective-permute-done.10.refs_0_, ...), custom_call_target="tpu_custom_call", output_to_operand_aliasing={{0}: (3, {}), {1}: (4, {}), {2}: (5, {}), {3}: (6, {}), {4}... | custom-call | flops 1073741824 | bytes 2097152 | tf_op jit(solution)/shard_map/part/pallas_call | solution.py:188
  44.6 2.7 %collective-permute-done.9.refs_0_ = bf16[544,512]{1,0:T(8,128)(2,1)S(1)} collective-permute-done((bf16[544,512]{1,0:T(8,128)(2,1)S(1)}, bf16[544,512]{1,0:T(8,128)(2,1)S(1)}, u32[]{:S(2)}, u32[]{:S(2)}) %collective-permute-start.9) | collective-permute-done | bytes 557088 | tf_op jit(solution)/shard_map/ppermute | solution.py:449
  47.3 2.8 %part.6 = (bf16[2048,512]{1,0:T(8,128)(2,1)S(1)}, s32[2,8,2048]{2,1,0:T(8,128)S(1)}, bf16[1024,2048]{1,0:T(8,128)(2,1)S(1)}, bf16[1024,2048]{1,0:T(8,128)(2,1)S(1)}, f32[8,128]{1,0:T(8,128)S(1)}) custom-call(bf16[544,512]{1,0:T(8,128)(2,1)S(1)} %collective-permute-done.9.refs_0_, ...), custom_call_target="tpu_custom_call", output_to_operand_aliasing={{0}: (3, {}), {1}: (4, {}), {2}: (5, {}), {3}: (6, {}), {4}... | custom-call | flops 1073741824 | bytes 2097152 | tf_op jit(solution)/shard_map/part/pallas_call | solution.py:188
  50.1 4.6 %part.7 = (bf16[2048,512]{1,0:T(8,128)(2,1)S(1)}, s32[2,8,2048]{2,1,0:T(8,128)S(1)}, bf16[1024,2048]{1,0:T(8,128)(2,1)S(1)}, bf16[1024,2048]{1,0:T(8,128)(2,1)S(...) custom-call(bf16[544,512]{1,0:T(8,128)(2,1)S(1)} %collective-permute, ...), custom_call_target="tpu_custom_call", output_to_operand_aliasing={{0}: (3, {}), {1}: (4, {}), {2}: (5, {}), {3}: (6, {}), {4}... | custom-call | flops 2147483648 | bytes 2097152 | tf_op jit(solution)/shard_map/part/pallas_call | solution.py:188
  54.7 9.2 %collective-permute-start.11 = (f32[1024,512]{1,0:T(8,128)S(1)}, f32[1024,512]{1,0:T(8,128)S(1)}, u32[]{:S(2)}, u32[]{:S(2)}) collective-permute-start(f32[1024,512]{1,0:T(8,128)S(1)} %get-tuple-element.106), channel_id=1, source_target_pairs={{0,2},{2,0},{4,6},{6,4},{8,10},{10,8},{12,14},{14,12},{16,18},{18,... | collective-permute-start | bytes 6291464 | tf_op jit(solution)/shard_map/ppermute | solution.py:449
  65.5 2.3 %grad.1.refs_0_ = f32[1024,512]{1,0:T(8,128)S(1)} custom-call(bf16[1024,2048]{1,0:T(8,128)(2,1)S(1)} %get-tuple-element.118.resid_ref.refs_0_, bf16[2048,512]{1,0:T(8,128)(2,1)S(1)} %get-tuple-element.108.q_ref.refs_1_.q), custom_call_target="tpu_custom_call" | custom-call | flops 2147483648 | bytes 8388608 | tf_op jit(solution)/shard_map/grad/pallas_call | solution.py:371
  68.4 1.8 %adamw.2 = (f32[1024,512]{1,0:T(8,128)S(1)}, f32[1024,512]{1,0:T(8,128)S(1)}, f32[1024,512]{1,0:T(8,128)S(1)}, bf16[1024,512]{1,0:T(8,128)(2,1)S(1)}) custom-call(f32[1024,512]{1,0:T(8,128)S(1)} %grad.1.refs_0_, f32[1024,512]{1,0:T(8,128)S(1)} %collective-permute-done.11.refs_1_, f32[1024,512]{1,0:T(8,128)S(1)} %copy-done, f32[1024,512]{1,0:T(8,128)S(1)} %copy-done.1, ...), custom_call_target="tpu_custom_call" | custom-call | flops 10485760 | bytes 6291456 | tf_op jit(solution)/shard_map/adamw/pallas_call | solution.py:422
  70.3 2.0 %collective-permute-start.12 = (bf16[512,512]{1,0:T(8,128)(2,1)S(1)}, bf16[512,512]{1,0:T(8,128)(2,1)S(1)}, u32[]{:S(2)}, u32[]{:S(2)}) collective-permute-start(bf16[512,512]{1,0:T(8,128)(2,1)S(1)} %terms.2), channel_id=1, source_target_pairs={{0,32},{2,35},{4,36},{6,39},{8,40},{10,43},{12,44},{14,47},{16,48}... | collective-permute-start | bytes 1572872 | tf_op jit(solution)/shard_map/ppermute | solution.py:449
  73.8 3.5 %plane.2 = (bf16[1024,2048]{1,0:T(8,128)(2,1)S(1)}, bf16[1024,2048]{1,0:T(8,128)(2,1)S(1)}, bf16[512,512]{1,0:T(8,128)(2,1)S(1)}) custom-call(f32[8,128]{1,0:T(8,128)S(1)} %get-tuple-element.115.refs_0_.most, bf16[2048,512]{1,0:T(8,128)(2,1)S(1)} %get-tuple-element.108.q_ref.refs_1_.q, s32[2,8,2048]{2,1,0:T(8,128)S(1)} %get-tuple-element.116.refs_2_.pos, ...), custom_call_target="tpu_custom_call" | custom-call | flops 2147483648 | bytes 4194304 | tf_op jit(solution)/shard_map/plane/pallas_call | solution.py:312
  77.4 2.6 %collective-permute-start.15 = (bf16[256,512]{1,0:T(8,128)(2,1)S(1)}, bf16[256,512]{1,0:T(8,128)(2,1)S(1)}, u32[]{:S(2)}, u32[]{:S(2)}) collective-permute-start(bf16[256,512]{1,0:T(8,128)(2,1)S(1)} %get-tuple-element.169), channel_id=1, source_target_pairs={{0,96},{2,227},{4,100},{6,231},{8,104},{10,235},{12,108},{14,239},... | collective-permute-start | bytes 786440 | tf_op jit(solution)/shard_map/ppermute | solution.py:449
  80.0 2.5 %collective-permute-start.14 = (bf16[256,512]{1,0:T(8,128)(2,1)S(1)}, bf16[256,512]{1,0:T(8,128)(2,1)S(1)}, u32[]{:S(2)}, u32[]{:S(2)}) collective-permute-start(bf16[256,512]{1,0:T(8,128)(2,1)S(1)} %get-tuple-element.170), channel_id=1, source_target_pairs={{0,32},{2,35},{4,36},{6,39},{8,40},{10,43},{12,44},{14,47},{16,48}... | collective-permute-start | bytes 786440 | tf_op jit(solution)/shard_map/ppermute | solution.py:449
  82.5 3.5 %plane.3 = (bf16[1024,2048]{1,0:T(8,128)(2,1)S(1)}, bf16[1024,2048]{1,0:T(8,128)(2,1)S(1)}, f32[512,512]{1,0:T(8,128)S(1)}) custom-call(f32[8,128]{1,0:T(8,128)S(1)} %get-tuple-element.115.refs_0_.most, bf16[2048,512]{1,0:T(8,128)(2,1)S(1)} %get-tuple-element.108.q_ref.refs_1_.q, ...), custom_call_target="tpu_custom_call", output_to_operand_aliasing={{0}: (5, {}), {1}: (6, {})} | custom-call | flops 2147483648 | bytes 4194304 | tf_op jit(solution)/shard_map/plane/pallas_call | solution.py:312
  87.3 1.8 %collective-permute-start.17 = (bf16[256,512]{1,0:T(8,128)(2,1)S(1)}, bf16[256,512]{1,0:T(8,128)(2,1)S(1)}, u32[]{:S(2)}, u32[]{:S(2)}) collective-permute-start(bf16[256,512]{1,0:T(8,128)(2,1)S(1)} %slice.104), channel_id=1, source_target_pairs={{0,64},{2,194},{4,68},{6,198},{8,72},{10,202},{12,76},{14,206},{16... | collective-permute-start | bytes 786440 | tf_op jit(solution)/shard_map/ppermute | solution.py:449
  89.0 4.3 %rest.2 = (bf16[1024,2048]{1,0:T(8,128)(2,1)S(1)}, f32[1024,512]{1,0:T(8,128)S(1)}) custom-call(f32[8,128]{1,0:T(8,128)S(1)} %get-tuple-element.115.refs_0_.most, bf16[2048,512]{1,0:T(8,128)(2,1)S(1)} %get-tuple-element.108.q_ref.refs_1_.q, s32[2,8,2048]{2,1,0:T(8,128)S(1)} %get-tuple-element.116.refs_2_.pos, ...), custom_call_target="tpu_custom_call", output_to_operand_aliasing={{0}: (4, {})} | custom-call | flops 3221225472 | bytes 8388608 | tf_op jit(solution)/shard_map/rest/pallas_call | solution.py:354
  93.4 2.2 %collective-permute-done.17 = bf16[256,512]{1,0:T(8,128)(2,1)S(1)} collective-permute-done((bf16[256,512]{1,0:T(8,128)(2,1)S(1)}, bf16[256,512]{1,0:T(8,128)(2,1)S(1)}, u32[]{:S(2)}, u32[]{:S(2)}) %collective-permute-start.17) | collective-permute-done | bytes 262176 | tf_op jit(solution)/shard_map/ppermute | solution.py:449
  96.1 2.7 %collective-permute-start.19 = (bf16[4,2,16,512]{3,2,1,0:T(8,128)(2,1)S(1)}, bf16[4,2,16,512]{3,2,1,0:T(8,128)(2,1)S(1)}, u32[]{:S(2)}, u32[]{:S(2)}) collective-permute-start(bf16[4,2,16,512]{3,2,1,0:T(8,128)(2,1)S(1)} %get-tuple-element.167), channel_id=1, source_target_pairs={{0,24},{2,10},{4,28},{6,14},{8,0},{10,18},{12,4},{14,22},{16,8},{1... | collective-permute-start | bytes 393224 | tf_op jit(solution)/shard_map/ppermute | solution.py:449
  98.8 2.2 %collective-permute-start.18 = (bf16[4,2,16,512]{3,2,1,0:T(8,128)(2,1)S(1)}, bf16[4,2,16,512]{3,2,1,0:T(8,128)(2,1)S(1)}, u32[]{:S(2)}, u32[]{:S(2)}) collective-permute-start(bf16[4,2,16,512]{3,2,1,0:T(8,128)(2,1)S(1)} %get-tuple-element.168), channel_id=1, source_target_pairs={{0,192},{2,66},{4,196},{6,70},{8,200},{10,74},{12,204},{14,78},{16... | collective-permute-start | bytes 393224 | tf_op jit(solution)/shard_map/ppermute | solution.py:449
  101.0 4.3 %rest.3 = (bf16[1024,2048]{1,0:T(8,128)(2,1)S(1)}, f32[1024,512]{1,0:T(8,128)S(1)}) custom-call(f32[8,128]{1,0:T(8,128)S(1)} %get-tuple-element.115.refs_0_.most, bf16[2048,512]{1,0:T(8,128)(2,1)S(1)} %get-tuple-element.108.q_ref.refs_1_.q, s32[2,8,2048]{2,1,0:T(8,128)S(1)} %get-tuple-element.116.refs_2_.pos, ...), custom_call_target="tpu_custom_call", output_to_operand_aliasing={{0}: (4, {})} | custom-call | flops 3221225472 | bytes 8388608 | tf_op jit(solution)/shard_map/rest/pallas_call | solution.py:354
  107.0 2.8 %collective-permute-start.21 = (f32[2,16,512]{2,1,0:T(8,128)S(1)}, f32[2,16,512]{2,1,0:T(8,128)S(1)}, u32[]{:S(2)}, u32[]{:S(2)}) collective-permute-start(f32[2,16,512]{2,1,0:T(8,128)S(1)} %get-tuple-element.173), channel_id=1, source_target_pairs={{0,30},{2,4},{4,2},{6,8},{8,6},{10,12},{12,10},{14,16},{16,14},{18... | collective-permute-start | bytes 196616 | tf_op jit(solution)/shard_map/ppermute | solution.py:449
  109.9 3.2 %adamw.3 = (f32[1024,512]{1,0:T(8,128)}, f32[1024,512]{1,0:T(8,128)}, f32[1024,512]{1,0:T(8,128)}) custom-call(f32[1024,512]{1,0:T(8,128)S(1)} %get-tuple-element.151.refs_0_, f32[1024,512]{1,0:T(8,128)S(1)} %collective-permute-done.24.refs_1_, f32[1024,512]{1,0:T(8,128)S(1)} %get-tuple-element.153.refs_2_, f32[1024,512]{1,0:T(8,128)S(1)} %get-tuple-element.154.refs_3_, ...), custom_call_target="tpu_custom_call" | custom-call | flops 10485760 | bytes 6291456 | tf_op jit(solution)/shard_map/adamw/pallas_call | solution.py:422
  (64 shorter events, 16.0 us)
Async XLA Ops:
  0.6 0.7 copy-start.3
  1.3 0.7 copy-start.4
  2.4 10.2 %collective-permute-start.2 = (bf16[16,640]{0,1:T(8,128)(2,1)S(1)}, bf16[16,640]{0,1:T(8,128)(2,1)S(1)}, u32[]{:S(2)}, u32[]{:S(2)}) collective-permute-start(bf16[16,640]{0,1:T(8,128)(2,1)S(1)} %copy.32), channel_id=1, source_target_pairs={{0,26},{2,8},{4,30},{6,12},{8,2},{10,16},{12,6},{14,20},{16,10},{1... | collective-permute-start | bytes 61448 | tf_op jit(solution)/shard_map/ppermute | solution.py:449
  6.9 6.8 %collective-permute-start.1 = (bf16[16,640]{0,1:T(8,128)(2,1)S(1)}, bf16[16,640]{0,1:T(8,128)(2,1)S(1)}, u32[]{:S(2)}, u32[]{:S(2)}) collective-permute-start(bf16[16,640]{0,1:T(8,128)(2,1)S(1)} %copy.32), channel_id=1, source_target_pairs={{0,4},{2,30},{4,8},{6,2},{8,12},{10,6},{12,16},{14,10},{16,20},{18... | collective-permute-start | bytes 61448 | tf_op jit(solution)/shard_map/ppermute | solution.py:449
  9.0 6.5 %collective-permute-start = (bf16[16,640]{0,1:T(8,128)(2,1)S(1)}, bf16[16,640]{0,1:T(8,128)(2,1)S(1)}, u32[]{:S(2)}, u32[]{:S(2)}) collective-permute-start(bf16[16,640]{0,1:T(8,128)(2,1)S(1)} %copy.32), channel_id=1, source_target_pairs={{0,30},{2,4},{4,2},{6,8},{8,6},{10,12},{12,10},{14,16},{16,14},{18... | collective-permute-start | bytes 61448 | tf_op jit(solution)/shard_map/ppermute | solution.py:449
  12.1 22.8 %collective-permute-start.7 = (bf16[1024,512]{1,0:T(8,128)(2,1)S(1)}, bf16[1024,512]{1,0:T(8,128)(2,1)S(1)}, u32[]{:S(2)}, u32[]{:S(2)}) collective-permute-start(bf16[1024,512]{1,0:T(8,128)(2,1)S(1)} %convert_element_type.34.refs_1_.refs_2_), channel_id=1, source_target_pairs={{0,2},{2,0},{4,6},{6,4},{8,10},{10,8},{12,14},{14,12},{16,18},{18,... | collective-permute-start | bytes 3145736 | tf_op jit(solution)/shard_map/ppermute | solution.py:449
  15.7 7.4 %collective-permute-start.3 = (bf16[64,640]{0,1:T(8,128)(2,1)S(1)}, bf16[64,640]{0,1:T(8,128)(2,1)S(1)}, u32[]{:S(2)}, u32[]{:S(2)}) collective-permute-start(bf16[64,640]{0,1:T(8,128)(2,1)S(1)} %pad_maximum_fusion.1), channel_id=1, source_target_pairs={{0,8},{2,26},{4,12},{6,30},{8,16},{10,2},{12,20},{14,6},{16,24},{1... | collective-permute-start | bytes 245768 | tf_op jit(solution)/shard_map/ppermute | solution.py:449
  23.6 5.5 %collective-permute-start.6 = (bf16[136,512]{1,0:T(8,128)(2,1)S(1)}, bf16[136,512]{1,0:T(8,128)(2,1)S(1)}, u32[]{:S(2)}, u32[]{:S(2)}) collective-permute-start(bf16[136,512]{1,0:T(8,128)(2,1)S(1)} %pad_maximum_fusion.2.refs_0_), channel_id=1, source_target_pairs={{0,128},{2,3},{4,132},{6,7},{8,136},{10,11},{12,140},{14,15},{16,1... | collective-permute-start | bytes 417800 | tf_op jit(solution)/shard_map/ppermute | solution.py:449
  26.6 5.1 %collective-permute-start.5 = (bf16[136,512]{1,0:T(8,128)(2,1)S(1)}, bf16[136,512]{1,0:T(8,128)(2,1)S(1)}, u32[]{:S(2)}, u32[]{:S(2)}) collective-permute-start(bf16[136,512]{1,0:T(8,128)(2,1)S(1)} %pad_maximum_fusion.2.refs_0_), channel_id=1, source_target_pairs={{0,192},{2,35},{4,196},{6,39},{8,200},{10,43},{12,204},{14,47},{16... | collective-permute-start | bytes 417800 | tf_op jit(solution)/shard_map/ppermute | solution.py:449
  27.4 4.3 %collective-permute-start.4 = (bf16[136,512]{1,0:T(8,128)(2,1)S(1)}, bf16[136,512]{1,0:T(8,128)(2,1)S(1)}, u32[]{:S(2)}, u32[]{:S(2)}) collective-permute-start(bf16[136,512]{1,0:T(8,128)(2,1)S(1)} %pad_maximum_fusion.2.refs_0_), channel_id=1, source_target_pairs={{0,64},{2,34},{4,68},{6,38},{8,72},{10,42},{12,76},{14,46},{16,80}... | collective-permute-start | bytes 417800 | tf_op jit(solution)/shard_map/ppermute | solution.py:449
  31.8 10.3 %collective-permute-start.10 = (bf16[544,512]{1,0:T(8,128)(2,1)S(1)}, bf16[544,512]{1,0:T(8,128)(2,1)S(1)}, u32[]{:S(2)}, u32[]{:S(2)}) collective-permute-start(bf16[544,512]{1,0:T(8,128)(2,1)S(1)} %pack.1.refs_0_), channel_id=1, source_target_pairs={{0,32},{2,66},{4,36},{6,70},{8,40},{10,74},{12,44},{14,78},{16,48}... | collective-permute-start | bytes 1671176 | tf_op jit(solution)/shard_map/ppermute | solution.py:449
  33.0 14.3 %collective-permute-start.9 = (bf16[544,512]{1,0:T(8,128)(2,1)S(1)}, bf16[544,512]{1,0:T(8,128)(2,1)S(1)}, u32[]{:S(2)}, u32[]{:S(2)}) collective-permute-start(bf16[544,512]{1,0:T(8,128)(2,1)S(1)} %pack.1.refs_0_), channel_id=1, source_target_pairs={{0,33},{2,194},{4,37},{6,198},{8,41},{10,202},{12,45},{14,206},{16... | collective-permute-start | bytes 1671176 | tf_op jit(solution)/shard_map/ppermute | solution.py:449
  37.4 12.7 %collective-permute-start.8 = (bf16[544,512]{1,0:T(8,128)(2,1)S(1)}, bf16[544,512]{1,0:T(8,128)(2,1)S(1)}, u32[]{:S(2)}, u32[]{:S(2)}) collective-permute-start(bf16[544,512]{1,0:T(8,128)(2,1)S(1)} %pack.1.refs_0_), channel_id=1, source_target_pairs={{0,1},{2,130},{4,5},{6,134},{8,9},{10,138},{12,13},{14,142},{16,17... | collective-permute-start | bytes 1671176 | tf_op jit(solution)/shard_map/ppermute | solution.py:449
  54.7 13.1 %collective-permute-start.11 = (f32[1024,512]{1,0:T(8,128)S(1)}, f32[1024,512]{1,0:T(8,128)S(1)}, u32[]{:S(2)}, u32[]{:S(2)}) collective-permute-start(f32[1024,512]{1,0:T(8,128)S(1)} %get-tuple-element.106), channel_id=1, source_target_pairs={{0,2},{2,0},{4,6},{6,4},{8,10},{10,8},{12,14},{14,12},{16,18},{18,... | collective-permute-start | bytes 6291464 | tf_op jit(solution)/shard_map/ppermute | solution.py:449
  65.5 2.4 %copy-start = (f32[1024,512]{1,0:T(8,128)S(1)}, f32[1024,512]{1,0:T(8,128)}, u32[]{:S(2)}) copy-start(f32[1024,512]{1,0:T(8,128)} %refs_2_.1) | copy-start | bytes 6291460
  65.5 2.4 %copy-start.1 = (f32[1024,512]{1,0:T(8,128)S(1)}, f32[1024,512]{1,0:T(8,128)}, u32[]{:S(2)}) copy-start(f32[1024,512]{1,0:T(8,128)} %refs_3_.1) | copy-start | bytes 6291460
  65.5 2.8 %copy-start.2 = (f32[1024,512]{1,0:T(8,128)S(1)}, f32[1024,512]{1,0:T(8,128)}, u32[]{:S(2)}) copy-start(f32[1024,512]{1,0:T(8,128)} %refs_4_.1) | copy-start | bytes 6291460
  70.1 3.7 %collective-permute-start.13 = (bf16[1024,512]{1,0:T(8,128)(2,1)S(1)}, bf16[1024,512]{1,0:T(8,128)(2,1)S(1)}, u32[]{:S(2)}, u32[]{:S(2)}) collective-permute-start(bf16[1024,512]{1,0:T(8,128)(2,1)S(1)} %get-tuple-element.117.refs_3_.wb), channel_id=1, source_target_pairs={{0,2},{2,0},{4,6},{6,4},{8,10},{10,8},{12,14},{14,12},{16,18},{18,... | collective-permute-start | bytes 3145736 | tf_op jit(solution)/shard_map/ppermute | solution.py:449
  70.3 15.7 %collective-permute-start.12 = (bf16[512,512]{1,0:T(8,128)(2,1)S(1)}, bf16[512,512]{1,0:T(8,128)(2,1)S(1)}, u32[]{:S(2)}, u32[]{:S(2)}) collective-permute-start(bf16[512,512]{1,0:T(8,128)(2,1)S(1)} %terms.2), channel_id=1, source_target_pairs={{0,32},{2,35},{4,36},{6,39},{8,40},{10,43},{12,44},{14,47},{16,48}... | collective-permute-start | bytes 1572872 | tf_op jit(solution)/shard_map/ppermute | solution.py:449
  77.4 16.0 %collective-permute-start.15 = (bf16[256,512]{1,0:T(8,128)(2,1)S(1)}, bf16[256,512]{1,0:T(8,128)(2,1)S(1)}, u32[]{:S(2)}, u32[]{:S(2)}) collective-permute-start(bf16[256,512]{1,0:T(8,128)(2,1)S(1)} %get-tuple-element.169), channel_id=1, source_target_pairs={{0,96},{2,227},{4,100},{6,231},{8,104},{10,235},{12,108},{14,239},... | collective-permute-start | bytes 786440 | tf_op jit(solution)/shard_map/ppermute | solution.py:449
  80.0 13.4 %collective-permute-start.14 = (bf16[256,512]{1,0:T(8,128)(2,1)S(1)}, bf16[256,512]{1,0:T(8,128)(2,1)S(1)}, u32[]{:S(2)}, u32[]{:S(2)}) collective-permute-start(bf16[256,512]{1,0:T(8,128)(2,1)S(1)} %get-tuple-element.170), channel_id=1, source_target_pairs={{0,32},{2,35},{4,36},{6,39},{8,40},{10,43},{12,44},{14,47},{16,48}... | collective-permute-start | bytes 786440 | tf_op jit(solution)/shard_map/ppermute | solution.py:449
  86.3 7.1 %collective-permute-start.16 = (bf16[256,512]{1,0:T(8,128)(2,1)S(1)}, bf16[256,512]{1,0:T(8,128)(2,1)S(1)}, u32[]{:S(2)}, u32[]{:S(2)}) collective-permute-start(bf16[256,512]{1,0:T(8,128)(2,1)S(1)} %slice.105), channel_id=1, source_target_pairs={{0,64},{2,194},{4,68},{6,198},{8,72},{10,202},{12,76},{14,206},{16... | collective-permute-start | bytes 786440 | tf_op jit(solution)/shard_map/ppermute | solution.py:449
  87.3 8.3 %collective-permute-start.17 = (bf16[256,512]{1,0:T(8,128)(2,1)S(1)}, bf16[256,512]{1,0:T(8,128)(2,1)S(1)}, u32[]{:S(2)}, u32[]{:S(2)}) collective-permute-start(bf16[256,512]{1,0:T(8,128)(2,1)S(1)} %slice.104), channel_id=1, source_target_pairs={{0,64},{2,194},{4,68},{6,198},{8,72},{10,202},{12,76},{14,206},{16... | collective-permute-start | bytes 786440 | tf_op jit(solution)/shard_map/ppermute | solution.py:449
  95.6 14.3 %collective-permute-start.24 = (f32[1024,512]{1,0:T(8,128)S(1)}, f32[1024,512]{1,0:T(8,128)S(1)}, u32[]{:S(2)}, u32[]{:S(2)}) collective-permute-start(f32[1024,512]{1,0:T(8,128)S(1)} %get-tuple-element.152), channel_id=1, source_target_pairs={{0,2},{2,0},{4,6},{6,4},{8,10},{10,8},{12,14},{14,12},{16,18},{18,... | collective-permute-start | bytes 6291464 | tf_op jit(solution)/shard_map/ppermute | solution.py:449
  96.0 9.3 %collective-permute-start.20 = (bf16[4,2,16,512]{3,2,1,0:T(8,128)(2,1)S(1)}, bf16[4,2,16,512]{3,2,1,0:T(8,128)(2,1)S(1)}, u32[]{:S(2)}, u32[]{:S(2)}) collective-permute-start(bf16[4,2,16,512]{3,2,1,0:T(8,128)(2,1)S(1)} %get-tuple-element.166), channel_id=1, source_target_pairs={{0,216},{2,74},{4,220},{6,78},{8,192},{10,82},{12,196},{14,86},{16... | collective-permute-start | bytes 393224 | tf_op jit(solution)/shard_map/ppermute | solution.py:449
  96.1 9.2 %collective-permute-start.19 = (bf16[4,2,16,512]{3,2,1,0:T(8,128)(2,1)S(1)}, bf16[4,2,16,512]{3,2,1,0:T(8,128)(2,1)S(1)}, u32[]{:S(2)}, u32[]{:S(2)}) collective-permute-start(bf16[4,2,16,512]{3,2,1,0:T(8,128)(2,1)S(1)} %get-tuple-element.167), channel_id=1, source_target_pairs={{0,24},{2,10},{4,28},{6,14},{8,0},{10,18},{12,4},{14,22},{16,8},{1... | collective-permute-start | bytes 393224 | tf_op jit(solution)/shard_map/ppermute | solution.py:449
  98.8 6.5 %collective-permute-start.18 = (bf16[4,2,16,512]{3,2,1,0:T(8,128)(2,1)S(1)}, bf16[4,2,16,512]{3,2,1,0:T(8,128)(2,1)S(1)}, u32[]{:S(2)}, u32[]{:S(2)}) collective-permute-start(bf16[4,2,16,512]{3,2,1,0:T(8,128)(2,1)S(1)} %get-tuple-element.168), channel_id=1, source_target_pairs={{0,192},{2,66},{4,196},{6,70},{8,200},{10,74},{12,204},{14,78},{16... | collective-permute-start | bytes 393224 | tf_op jit(solution)/shard_map/ppermute | solution.py:449
  105.5 7.6 %collective-permute-start.23 = (f32[2,16,512]{2,1,0:T(8,128)S(1)}, f32[2,16,512]{2,1,0:T(8,128)S(1)}, u32[]{:S(2)}, u32[]{:S(2)}) collective-permute-start(f32[2,16,512]{2,1,0:T(8,128)S(1)} %get-tuple-element.171), channel_id=1, source_target_pairs={{0,26},{2,8},{4,30},{6,12},{8,2},{10,16},{12,6},{14,20},{16,10},{1... | collective-permute-start | bytes 196616 | tf_op jit(solution)/shard_map/ppermute | solution.py:449
  107.0 6.0 %collective-permute-start.22 = (f32[2,16,512]{2,1,0:T(8,128)S(1)}, f32[2,16,512]{2,1,0:T(8,128)S(1)}, u32[]{:S(2)}, u32[]{:S(2)}) collective-permute-start(f32[2,16,512]{2,1,0:T(8,128)S(1)} %get-tuple-element.172), channel_id=1, source_target_pairs={{0,28},{2,6},{4,0},{6,10},{8,4},{10,14},{12,8},{14,18},{16,12},{18... | collective-permute-start | bytes 196616 | tf_op jit(solution)/shard_map/ppermute | solution.py:449
  107.0 6.0 %collective-permute-start.21 = (f32[2,16,512]{2,1,0:T(8,128)S(1)}, f32[2,16,512]{2,1,0:T(8,128)S(1)}, u32[]{:S(2)}, u32[]{:S(2)}) collective-permute-start(f32[2,16,512]{2,1,0:T(8,128)S(1)} %get-tuple-element.173), channel_id=1, source_target_pairs={{0,30},{2,4},{4,2},{6,8},{8,6},{10,12},{12,10},{14,16},{16,14},{18... | collective-permute-start | bytes 196616 | tf_op jit(solution)/shard_map/ppermute | solution.py:449
